TPU v7x, 32 devices: a whole 2x2x4 slice. The times are simulated.
32 devices in a mesh: blk: 8 (over y, x, core), head: 4 (over z).
Axes of the slice: x: 2, y: 2, z: 4, core: 2. Of those that a mesh axis runs over, the one named last changes fastest.
Arguments:
- tokens: bfloat16 [2, 2048, 768], P(None, ('blk', 'head')), may hold values from -6 to 6
- starts: int32 [2, 16], replicated, may hold values from 0 to 2047, as said below
- w_qkv: bfloat16 [768, 2304], P(('blk', 'head')), may hold values from -0.21875 to 0.21875
- bias_q: bfloat16 [768], P(('blk', 'head')), may hold values from -3 to 3
- bias_v: bfloat16 [768], P(('blk', 'head')), may hold values from -3 to 3
- w_out: bfloat16 [768, 768], P(('blk', 'head'))
- bias_out: bfloat16 [768], P(('blk', 'head')), may hold values from -3 to 3
- gain_one: bfloat16 [768], P(('blk', 'head')), may hold values from 0.25 to 1.75
- shift_one: bfloat16 [768], P(('blk', 'head')), may hold values from -3 to 3
- w_up: bfloat16 [768, 3072], P(('blk', 'head')), may hold values from -0.21875 to 0.21875
- bias_up: bfloat16 [3072], P(('blk', 'head')), may hold values from -3 to 3
- w_down: bfloat16 [3072, 768], P(('blk', 'head')), may hold values from -0.109375 to 0.109375
- bias_down: bfloat16 [768], P(('blk', 'head')), may hold values from -3 to 3
- gain_two: bfloat16 [768], P(('blk', 'head')), may hold values from 0.25 to 1.75
- shift_two: bfloat16 [768], P(('blk', 'head')), may hold values from -3 to 3
- cotangent: bfloat16 [2, 2048, 768], P(None, ('blk', 'head')), may hold values from -6 to 6
Outputs:
- output: float32 [2, 2048, 768], P(None, ('blk', 'head'))
- grad_tokens: float32 [2, 2048, 768], P(None, ('blk', 'head'))
- grad_w_qkv: float32 [768, 2304], P(('blk', 'head'))
- grad_bias_q: float32 [768], P(('blk', 'head'))
- grad_bias_v: float32 [768], P(('blk', 'head'))
- grad_w_out: float32 [768, 768], P(('blk', 'head'))
- grad_bias_out: float32 [768], P(('blk', 'head'))
- grad_gain_one: float32 [768], P(('blk', 'head'))
- grad_shift_one: float32 [768], P(('blk', 'head'))
- grad_w_up: float32 [768, 3072], P(('blk', 'head'))
- grad_bias_up: float32 [3072], P(('blk', 'head'))
- grad_w_down: float32 [3072, 768], P(('blk', 'head'))
- grad_bias_down: float32 [768], P(('blk', 'head'))
- grad_gain_two: float32 [768], P(('blk', 'head'))
- grad_shift_two: float32 [768], P(('blk', 'head'))
Inputs may be any that keep to these rules, and one draw needn't show every extreme that they name: Each row of 16 document starts is strictly increasing and begins with 0. In one row, drawn from the seed, entry 7 lies below 256, entry 8 above 1792, and the last entry is 2047. In every other row consecutive starts, and the last start and 2048, lie at most 1024 apart, and exactly 1024 apart for one document of the row.
All inputs are finite; a program needn't handle non-finite values.
Results may differ from a plain program's by a relative error of at most 0.04.
Values may be sent and summed in bfloat16 or wider, within the bound.
A program may use at most 448 MiB of HBM per device.

v0:
```python
from functools import partial

import jax
import jax.numpy as jnp
from jax import lax
from jax.sharding import PartitionSpec as P

H = 12
HD = 64
MB = 2


EPS = 1e-05
NEG = -1e30


def norm_forward(values, gain_vec, shift_vec):
    center = values - jnp.mean(values, axis=-1, keepdims=True)
    inverse = lax.rsqrt(jnp.mean(center * center, axis=-1, keepdims=True) + EPS)
    normed = center * inverse
    return (normed * gain_vec + shift_vec, normed, inverse)


def norm_backward(upstream, normed, inverse, gain_vec):
    scaled = upstream * gain_vec
    inner = (
        scaled
        - jnp.mean(scaled, axis=-1, keepdims=True)
        - normed * jnp.mean(scaled * normed, axis=-1, keepdims=True)
    )
    return inner * inverse


def segment_of(starts_row, positions):
    return jnp.sum((starts_row[None, :] <= positions[:, None]).astype(jnp.int32), axis=1) - 1


def masked_scores(query_heads, key_heads, in_doc):
    scores = jnp.einsum(
        "qhd,khd->hqk", query_heads, key_heads, preferred_element_type=jnp.float32
    ) * HD ** (-0.5)
    return jnp.where(in_doc, scores, NEG)


def score_grads(query_heads, key_heads, value_heads, grad_numer, row_top, correction, in_doc):
    exp_score = jnp.where(
        in_doc, jnp.exp(masked_scores(query_heads, key_heads, in_doc) - row_top), 0.0
    )
    grad_weights = jnp.einsum(
        "qhd,khd->hqk", grad_numer, value_heads, preferred_element_type=jnp.float32
    )
    grad_scores = (exp_score * (grad_weights - correction)).astype(jnp.bfloat16)
    return (exp_score.astype(jnp.bfloat16), grad_scores)


def scatter_end(parts):
    (
        grad_proj_in,
        grad_query_bias,
        grad_value_bias,
        grad_proj_out,
        grad_out_bias,
        grad_norm_gain,
        grad_norm_shift,
        grad_up,
        grad_up_bias,
        grad_down,
        grad_down_bias,
        grad_final_gain,
        grad_final_shift,
    ) = parts
    return (
        lax.psum_scatter(grad_proj_in, ("blk", "head"), scatter_dimension=0, tiled=True),
        lax.psum_scatter(grad_query_bias, ("blk", "head"), scatter_dimension=0, tiled=True),
        lax.psum_scatter(grad_value_bias, ("blk", "head"), scatter_dimension=0, tiled=True),
        lax.psum_scatter(grad_proj_out, ("blk", "head"), scatter_dimension=0, tiled=True),
        lax.psum_scatter(grad_out_bias, ("blk", "head"), scatter_dimension=0, tiled=True),
        lax.psum_scatter(grad_norm_gain, ("blk", "head"), scatter_dimension=0, tiled=True),
        lax.psum_scatter(grad_norm_shift, ("blk", "head"), scatter_dimension=0, tiled=True),
        lax.psum_scatter(grad_up, ("blk", "head"), scatter_dimension=0, tiled=True),
        lax.psum_scatter(grad_up_bias, ("blk", "head"), scatter_dimension=0, tiled=True),
        lax.psum_scatter(grad_down, ("blk", "head"), scatter_dimension=0, tiled=True),
        lax.psum_scatter(grad_down_bias, ("blk", "head"), scatter_dimension=0, tiled=True),
        lax.psum_scatter(grad_final_gain, ("blk", "head"), scatter_dimension=0, tiled=True),
        lax.psum_scatter(grad_final_shift, ("blk", "head"), scatter_dimension=0, tiled=True),
    )


def per_device(
    tokens,
    starts,
    w_qkv,
    bias_q,
    bias_v,
    w_out,
    bias_out,
    gain_one,
    shift_one,
    w_up,
    bias_up,
    w_down,
    bias_down,
    gain_two,
    shift_two,
    cotangent,
):
    (
        proj_in,
        query_bias,
        value_bias,
        proj_out,
        out_bias,
        norm_gain,
        norm_shift,
        up_full,
        up_bias,
        down_full,
        down_bias,
        final_gain,
        final_shift,
    ) = (
        lax.all_gather(w_qkv, ("blk", "head"), axis=0, tiled=True),
        lax.all_gather(bias_q, ("blk", "head"), axis=0, tiled=True),
        lax.all_gather(bias_v, ("blk", "head"), axis=0, tiled=True),
        lax.all_gather(w_out, ("blk", "head"), axis=0, tiled=True),
        lax.all_gather(bias_out, ("blk", "head"), axis=0, tiled=True),
        lax.all_gather(gain_one, ("blk", "head"), axis=0, tiled=True),
        lax.all_gather(shift_one, ("blk", "head"), axis=0, tiled=True),
        lax.all_gather(w_up, ("blk", "head"), axis=0, tiled=True),
        lax.all_gather(bias_up, ("blk", "head"), axis=0, tiled=True),
        lax.all_gather(w_down, ("blk", "head"), axis=0, tiled=True),
        lax.all_gather(bias_down, ("blk", "head"), axis=0, tiled=True),
        lax.all_gather(gain_two, ("blk", "head"), axis=0, tiled=True),
        lax.all_gather(shift_two, ("blk", "head"), axis=0, tiled=True),
    )
    query_bias = query_bias.astype(jnp.float32)
    value_bias = value_bias.astype(jnp.float32)
    out_bias = out_bias.astype(jnp.float32)
    norm_gain = norm_gain.astype(jnp.float32)
    norm_shift = norm_shift.astype(jnp.float32)
    up_bias = up_bias.astype(jnp.float32)
    down_bias = down_bias.astype(jnp.float32)
    final_gain = final_gain.astype(jnp.float32)
    final_shift = final_shift.astype(jnp.float32)
    model_width = proj_out.shape[0]
    row_count = tokens.shape[1]
    head_count = lax.axis_size("head")
    block_rows = row_count * head_count
    heads_dev = H // head_count
    local_width = heads_dev * HD
    scale = HD ** (-0.5)
    local_pos = lax.axis_index("blk") * block_rows + jnp.arange(block_rows, dtype=jnp.int32)
    kept_list = []
    outputs = []
    for part_index in range(MB):
        inputs = tokens[part_index]
        starts_row = starts[part_index]
        projected = jnp.dot(inputs, proj_in, preferred_element_type=jnp.float32)
        query_rows = (projected[:, :model_width] + query_bias).astype(jnp.bfloat16)
        key_rows = projected[:, model_width : 2 * model_width].astype(jnp.bfloat16)
        value_rows = (projected[:, 2 * model_width :] + value_bias).astype(jnp.bfloat16)
        query_loc, key_loc, value_loc = (
            lax.all_to_all(query_rows, "head", split_axis=1, concat_axis=0, tiled=True),
            lax.all_to_all(key_rows, "head", split_axis=1, concat_axis=0, tiled=True),
            lax.all_to_all(value_rows, "head", split_axis=1, concat_axis=0, tiled=True),
        )
        doc_local = segment_of(starts_row, local_pos)
        query_heads = query_loc.reshape(block_rows, heads_dev, HD)

        def fold_keys(running, portion):
            row_top, row_total, weighted = running
            key_part, value_part = portion
            piece_len = key_part.shape[0]
            key_doc = segment_of(starts_row, jnp.arange(piece_len, dtype=jnp.int32))
            in_doc = (doc_local[:, None] == key_doc[None, :])[None]
            scores = masked_scores(query_heads, key_part.reshape(piece_len, heads_dev, HD), in_doc)
            new_top = jnp.maximum(row_top, jnp.max(scores, axis=-1, keepdims=True))
            exp_score = jnp.where(in_doc, jnp.exp(scores - new_top), 0.0)
            row_total = jnp.sum(exp_score, axis=-1, keepdims=True)
            weighted = jnp.einsum(
                "hqk,khd->hqd",
                exp_score.astype(jnp.bfloat16),
                value_part.reshape(piece_len, heads_dev, HD),
                preferred_element_type=jnp.float32,
            )
            return (new_top, row_total, weighted)

        start_state = (
            jnp.full((heads_dev, block_rows, 1), NEG, jnp.float32),
            jnp.zeros((heads_dev, block_rows, 1), jnp.float32),
            jnp.zeros((heads_dev, block_rows, HD), jnp.float32),
        )
        row_top, row_total, weighted = fold_keys(
            start_state,
            (
                lax.all_gather(key_loc, "blk", axis=0, tiled=True),
                lax.all_gather(value_loc, "blk", axis=0, tiled=True),
            ),
        )
        attended = jnp.transpose(weighted / row_total, (1, 0, 2))
        mixed_rows = lax.all_to_all(
            attended.reshape(block_rows, local_width).astype(jnp.bfloat16),
            "head",
            split_axis=0,
            concat_axis=1,
            tiled=True,
        )
        attn_out = jnp.dot(mixed_rows, proj_out, preferred_element_type=jnp.float32) + out_bias
        first_norm, normed_one, inverse_one = norm_forward(
            inputs.astype(jnp.float32) + attn_out, norm_gain, norm_shift
        )
        first_low = first_norm.astype(jnp.bfloat16)
        hidden = jnp.dot(first_low, up_full, preferred_element_type=jnp.float32) + up_bias
        active = jax.nn.gelu(hidden, approximate=False).astype(jnp.bfloat16)
        ffn_out = jnp.dot(active, down_full, preferred_element_type=jnp.float32) + down_bias
        result, normed_two, inverse_two = norm_forward(
            first_norm + ffn_out, final_gain, final_shift
        )
        outputs.append(result)
        kept_list.append(
            (
                inputs,
                starts_row,
                query_loc,
                key_loc,
                value_loc,
                doc_local,
                row_top,
                row_total,
                attended,
                mixed_rows,
                normed_one,
                inverse_one,
                first_low,
                hidden,
                active,
                normed_two,
                inverse_two,
            )
        )
    input_grads = []
    grad_sum = None
    for part_index in range(MB):
        (
            inputs,
            starts_row,
            query_loc,
            key_loc,
            value_loc,
            doc_local,
            row_top,
            row_total,
            attended,
            mixed_rows,
            normed_one,
            inverse_one,
            first_low,
            hidden,
            active,
            normed_two,
            inverse_two,
        ) = kept_list[part_index]
        grad_result = cotangent[part_index].astype(jnp.float32)
        grad_final_gain = jnp.sum(grad_result * normed_two, axis=0)
        grad_final_shift = jnp.sum(grad_result, axis=0)
        grad_two = norm_backward(grad_result, normed_two, inverse_two, final_gain)
        grad_ffn = grad_two.astype(jnp.bfloat16)
        grad_down_bias = jnp.sum(grad_ffn.astype(jnp.float32), axis=0)
        grad_down = jnp.einsum("rf,rd->fd", active, grad_ffn, preferred_element_type=jnp.float32)
        grad_active = jnp.einsum(
            "rd,fd->rf", grad_ffn, down_full, preferred_element_type=jnp.float32
        )
        gelu_pull = jax.vjp(partial(jax.nn.gelu, approximate=False), hidden)[1]
        grad_hidden = gelu_pull(grad_active)[0].astype(jnp.bfloat16)
        grad_up_bias = jnp.sum(grad_hidden.astype(jnp.float32), axis=0)
        grad_up = jnp.einsum(
            "rd,rf->df", first_low, grad_hidden, preferred_element_type=jnp.float32
        )
        grad_first = grad_two + jnp.einsum(
            "rf,df->rd", grad_hidden, up_full, preferred_element_type=jnp.float32
        )
        grad_norm_gain = jnp.sum(grad_first * normed_one, axis=0)
        grad_norm_shift = jnp.sum(grad_first, axis=0)
        grad_one = norm_backward(grad_first, normed_one, inverse_one, norm_gain)
        grad_attn = grad_one.astype(jnp.bfloat16)
        grad_out_bias = jnp.sum(grad_attn.astype(jnp.float32), axis=0)
        grad_proj_out = jnp.einsum(
            "rc,rd->cd", mixed_rows, grad_attn, preferred_element_type=jnp.float32
        )
        grad_mixed = jnp.einsum(
            "rd,cd->rc", grad_attn, proj_out, preferred_element_type=jnp.float32
        ).astype(jnp.bfloat16)
        grad_loc = lax.all_to_all(grad_mixed, "head", split_axis=1, concat_axis=0, tiled=True)
        grad_heads = grad_loc.astype(jnp.float32).reshape(block_rows, heads_dev, HD)
        total_rows = jnp.transpose(row_total, (1, 0, 2))
        correction = jnp.transpose(
            jnp.sum(grad_heads * attended, axis=-1, keepdims=True) / total_rows, (1, 0, 2)
        )
        grad_numer = (grad_heads / total_rows).astype(jnp.bfloat16)
        query_heads = query_loc.reshape(block_rows, heads_dev, HD)
        key_heads_loc = key_loc.reshape(block_rows, heads_dev, HD)
        value_heads_loc = value_loc.reshape(block_rows, heads_dev, HD)
        fold_key_part = lax.all_gather(key_loc, "blk", axis=0, tiled=True)
        fold_value_part = lax.all_gather(value_loc, "blk", axis=0, tiled=True)
        fold_piece_len = fold_key_part.shape[0]
        fold_key_doc = segment_of(starts_row, jnp.arange(fold_piece_len, dtype=jnp.int32))
        fold_in_doc = (doc_local[:, None] == fold_key_doc[None, :])[None]
        key_heads = fold_key_part.reshape(fold_piece_len, heads_dev, HD)
        exp_low, grad_scores = score_grads(
            query_heads,
            key_heads,
            fold_value_part.reshape(fold_piece_len, heads_dev, HD),
            grad_numer,
            row_top,
            correction,
            fold_in_doc,
        )
        grad_query = (
            jnp.einsum("hqk,khd->qhd", grad_scores, key_heads, preferred_element_type=jnp.float32)
            * scale
        )
        top_rows = jnp.transpose(row_top[:, :, 0])
        corr_rows = jnp.transpose(correction[:, :, 0])

        def fold_keygrad(portion):
            query_part, numer_part, top_part, corr_part = portion
            piece_len = query_part.shape[0]
            query_doc = segment_of(starts_row, jnp.arange(piece_len, dtype=jnp.int32))
            in_doc = (query_doc[:, None] == doc_local[None, :])[None]
            query_piece = query_part.reshape(piece_len, heads_dev, HD)
            numer_piece = numer_part.reshape(piece_len, heads_dev, HD)
            exp_low, grad_scores = score_grads(
                query_piece,
                key_heads_loc,
                value_heads_loc,
                numer_piece,
                jnp.transpose(top_part)[:, :, None],
                jnp.transpose(corr_part)[:, :, None],
                in_doc,
            )
            grad_key_run = (
                jnp.einsum(
                    "hqk,qhd->khd", grad_scores, query_piece, preferred_element_type=jnp.float32
                )
                * scale
            )
            grad_value_run = jnp.einsum(
                "hqk,qhd->khd", exp_low, numer_piece, preferred_element_type=jnp.float32
            )
            return (grad_key_run, grad_value_run)

        grad_key, grad_value = fold_keygrad(
            (
                lax.all_gather(query_loc, "blk", axis=0, tiled=True),
                lax.all_gather(
                    grad_numer.reshape(block_rows, local_width), "blk", axis=0, tiled=True
                ),
                lax.all_gather(top_rows.astype(jnp.bfloat16), "blk", axis=0, tiled=True).astype(
                    jnp.float32
                ),
                lax.all_gather(corr_rows.astype(jnp.bfloat16), "blk", axis=0, tiled=True).astype(
                    jnp.float32
                ),
            )
        )
        grad_q_rows, grad_k_rows, grad_v_rows = (
            lax.all_to_all(
                grad_query.reshape(block_rows, local_width).astype(jnp.bfloat16),
                "head",
                split_axis=0,
                concat_axis=1,
                tiled=True,
            ),
            lax.all_to_all(
                grad_key.reshape(block_rows, local_width).astype(jnp.bfloat16),
                "head",
                split_axis=0,
                concat_axis=1,
                tiled=True,
            ),
            lax.all_to_all(
                grad_value.reshape(block_rows, local_width).astype(jnp.bfloat16),
                "head",
                split_axis=0,
                concat_axis=1,
                tiled=True,
            ),
        )
        grad_proj = jnp.concatenate([grad_q_rows, grad_k_rows, grad_v_rows], axis=1)
        grad_query_bias = jnp.sum(grad_q_rows.astype(jnp.float32), axis=0)
        grad_value_bias = jnp.sum(grad_v_rows.astype(jnp.float32), axis=0)
        grad_proj_in = jnp.einsum(
            "rd,re->de", inputs, grad_proj, preferred_element_type=jnp.float32
        )
        input_grads.append(
            grad_one
            + jnp.einsum("re,de->rd", grad_proj, proj_in, preferred_element_type=jnp.float32)
        )
        part_grads = (
            grad_proj_in,
            grad_query_bias,
            grad_value_bias,
            grad_proj_out,
            grad_out_bias,
            grad_norm_gain,
            grad_norm_shift,
            grad_up,
            grad_up_bias,
            grad_down,
            grad_down_bias,
            grad_final_gain,
            grad_final_shift,
        )
        grad_sum = (
            part_grads
            if grad_sum is None
            else tuple((left + right for left, right in zip(grad_sum, part_grads)))
        )
    grad_sum = scatter_end(grad_sum)
    (
        grad_proj_in,
        grad_query_bias,
        grad_value_bias,
        grad_proj_out,
        grad_out_bias,
        grad_norm_gain,
        grad_norm_shift,
        grad_up,
        grad_up_bias,
        grad_down,
        grad_down_bias,
        grad_final_gain,
        grad_final_shift,
    ) = grad_sum
    return (
        jnp.stack(outputs),
        jnp.stack(input_grads),
        grad_proj_in,
        grad_query_bias,
        grad_value_bias,
        grad_proj_out,
        grad_out_bias,
        grad_norm_gain,
        grad_norm_shift,
        grad_up,
        grad_up_bias,
        grad_down,
        grad_down_bias,
        grad_final_gain,
        grad_final_shift,
    )


def solution(mesh):
    return jax.shard_map(
        per_device,
        mesh=mesh,
        in_specs=(
            P(None, ("blk", "head"), None),
            P(),
            P(("blk", "head"), None),
            P(("blk", "head")),
            P(("blk", "head")),
            P(("blk", "head"), None),
            P(("blk", "head")),
            P(("blk", "head")),
            P(("blk", "head")),
            P(("blk", "head"), None),
            P(("blk", "head")),
            P(("blk", "head"), None),
            P(("blk", "head")),
            P(("blk", "head")),
            P(("blk", "head")),
            P(None, ("blk", "head"), None),
        ),
        out_specs=(
            P(None, ("blk", "head"), None),
            P(None, ("blk", "head"), None),
            P(("blk", "head"), None),
            P(("blk", "head")),
            P(("blk", "head")),
            P(("blk", "head"), None),
            P(("blk", "head")),
            P(("blk", "head")),
            P(("blk", "head")),
            P(("blk", "head"), None),
            P(("blk", "head")),
            P(("blk", "head"), None),
            P(("blk", "head")),
            P(("blk", "head")),
            P(("blk", "head")),
        ),
        check_vma=False,
    )
```

profile of v0, /device:TPU:1, one launch (start us, length us, event | category | flops | bytes accessed | tf_op | source)
XLA Modules:
  0.0 867.1 jit_solution(11552827569191889788)
XLA Ops:
  20.0 42.1 %all-reduce.19 = (bf16[768]{0:T(1024)(128)(2,1)S(1)}, bf16[768]{0:T(1024)(128)(2,1)S(1)}, bf16[768]{0:T(1024)(128)(2,1)S(1)}, bf16[768]{0:T(1024)(128)(2,1)S(1)}...) all-reduce(bf16[768]{0:T(1024)(128)(2,1)S(1)} %dynamic-update-slice, ...), channel_id=1, replica_groups=mesh['blk'=8,'head'=4] {'blk','head'}, use_global_device_ids=true, to_apply=%add.1 | all-reduce | flops 9216 | bytes 36864
  62.1 11.7 %all-gather.5.cloned.1.call-done = bf16[768,2304]{1,0:T(8,128)(2,1)} async-done(((bf16[24,2304]{1,0:T(8,128)(2,1)}), bf16[768,2304]{1,0:T(8,128)(2,1)}) %all-gather.5.cloned.1.call-update) | async-done | bytes 3538960 | tf_op jit(solution)/shard_map/all_gather | solution.py:122
  105.3 12.9 %all_gather.81 = bf16[2048,192]{1,0:T(8,128)(2,1)S(1)} all-gather(bf16[256,192]{1,0:T(8,128)(2,1)S(1)} %bitcast.291), channel_id=1, replica_groups=mesh['blk'=8,'head'=4] {'blk'}, dimensions={0}, use_global_device_ids=true | all-gather | bytes 884736 | tf_op jit(solution)/shard_map/all_gather | solution.py:196
  130.7 10.4 %all_gather.83 = bf16[2048,192]{1,0:T(8,128)(2,1)S(1)} all-gather(bf16[256,192]{1,0:T(8,128)(2,1)S(1)} %bitcast.293), channel_id=1, replica_groups=mesh['blk'=8,'head'=4] {'blk'}, dimensions={0}, use_global_device_ids=true | all-gather | bytes 884736 | tf_op jit(solution)/shard_map/all_gather | solution.py:197
  159.4 12.7 %all_gather.94 = bf16[2048,192]{1,0:T(8,128)(2,1)S(1)} all-gather(bf16[256,192]{1,0:T(8,128)(2,1)S(1)} %bitcast.299), channel_id=1, replica_groups=mesh['blk'=8,'head'=4] {'blk'}, dimensions={0}, use_global_device_ids=true | all-gather | bytes 884736 | tf_op jit(solution)/shard_map/all_gather | solution.py:196
  177.2 15.9 %all_gather.95 = bf16[2048,192]{1,0:T(8,128)(2,1)S(1)} all-gather(bf16[256,192]{1,0:T(8,128)(2,1)S(1)} %bitcast.295), channel_id=1, replica_groups=mesh['blk'=8,'head'=4] {'blk'}, dimensions={0}, use_global_device_ids=true | all-gather | bytes 884736 | tf_op jit(solution)/shard_map/all_gather | solution.py:197
  202.4 11.0 %all_gather.100 = bf16[2048,192]{1,0:T(8,128)(2,1)S(1)} all-gather(bf16[256,192]{1,0:T(8,128)(2,1)S(1)} %bitcast.298), channel_id=1, replica_groups=mesh['blk'=8,'head'=4] {'blk'}, dimensions={0}, use_global_device_ids=true | all-gather | bytes 884736 | tf_op jit(solution)/shard_map/all_gather | solution.py:354
  214.3 8.2 all_gather.101
  222.5 8.6 all_gather.97
  235.9 10.6 %all_gather.96 = bf16[2048,192]{1,0:T(8,128)(2,1)S(1)} all-gather(bf16[256,192]{1,0:T(8,128)(2,1)S(1)} %bitcast.290), channel_id=1, replica_groups=mesh['blk'=8,'head'=4] {'blk'}, dimensions={0}, use_global_device_ids=true | all-gather | bytes 884736 | tf_op jit(solution)/shard_map/all_gather | solution.py:354
  247.4 13.1 %all-to-all-start.7 = ((bf16[4,64,192]{2,1,0:T(8,128)(2,1)}), bf16[4,64,192]{2,1,0:T(8,128)(2,1)S(1)}, u32[]{:S(2)}, u32[]{:S(2)}) async-start(bf16[4,64,192]{2,1,0:T(8,128)(2,1)} %copy.183), calls=%async_computation.7 | async-start | bytes 262144 | tf_op jit(solution)/shard_map/all_to_all | solution.py:201
  317.2 6.3 fusion.53
  324.5 10.5 %all_gather.103 = bf16[2048,3]{0,1:T(4,128)(2,1)S(1)} all-gather(bf16[256,3]{0,1:T(4,128)(2,1)S(1)} %get-tuple-element.138), channel_id=1, replica_groups=mesh['blk'=8,'head'=4] {'blk'}, dimensions={0}, use_global_device_ids=true | all-gather | bytes 13824 | tf_op jit(solution)/shard_map/all_gather | solution.py:361
  336.6 10.6 %all_gather.102 = bf16[2048,192]{1,0:T(8,128)(2,1)S(1)} all-gather(bf16[256,192]{1,0:T(8,128)(2,1)S(1)} %fusion.74), channel_id=1, replica_groups=mesh['blk'=8,'head'=4] {'blk'}, dimensions={0}, use_global_device_ids=true | all-gather | bytes 884736 | tf_op jit(solution)/shard_map/all_gather | solution.py:355
  355.1 6.7 fusion.55
  361.9 8.9 %all_gather.99 = bf16[2048,3]{0,1:T(4,128)(2,1)S(1)} all-gather(bf16[256,3]{0,1:T(4,128)(2,1)S(1)} %get-tuple-element.136), channel_id=1, replica_groups=mesh['blk'=8,'head'=4] {'blk'}, dimensions={0}, use_global_device_ids=true | all-gather | bytes 13824 | tf_op jit(solution)/shard_map/all_gather | solution.py:361
  375.8 6.5 fusion.52
  400.9 11.8 %all_gather.98 = bf16[2048,192]{1,0:T(8,128)(2,1)S(1)} all-gather(bf16[256,192]{1,0:T(8,128)(2,1)S(1)} %fusion.75), channel_id=1, replica_groups=mesh['blk'=8,'head'=4] {'blk'}, dimensions={0}, use_global_device_ids=true | all-gather | bytes 884736 | tf_op jit(solution)/shard_map/all_gather | solution.py:355
  418.2 5.9 fusion.54
  450.6 8.0 copy.218
  500.1 43.6 %all-reduce.18 = (f32[768]{0:T(1024)}, f32[768]{0:T(1024)}, f32[768]{0:T(1024)}, f32[768]{0:T(1024)}, f32[768]{0:T(1024)}, /*index=5*/f32[3072]{0:T(1024)}, f32[768]{0:T(1024)}, f32[768]{0:T(1024)}, f32[768]{0:T(1024)S(1)}) all-reduce(f32[768]{0:T(1024)} %add.312, ...), channel_id=3, replica_groups=mesh['blk'=8,'head'=4] {'blk','head'}, use_global_device_ids=true, to_apply=%region_29.30.clone | all-reduce | flops 9216 | bytes 73728
  559.5 17.4 %reduce-scatter.13.cloned.1.call-done = f32[24,2304]{1,0:T(8,128)} async-done(((f32[768,2304]{1,0:T(8,128)}), f32[24,2304]{1,0:T(8,128)}) %reduce-scatter.13.cloned.1.call-update) | async-done | bytes 221200
  577.0 141.0 %reduce-scatter.9.cloned.1.call-done = f32[24,3072]{1,0:T(8,128)} async-done(((f32[768,3072]{1,0:T(8,128)}), f32[24,3072]{1,0:T(8,128)}) %reduce-scatter.9.cloned.1.call-update) | async-done | bytes 294928 | tf_op jit(solution)/shard_map/reduce_scatter | solution.py:80
  718.0 142.1 %reduce-scatter.11.cloned.1.call-done = f32[96,768]{1,0:T(8,128)} async-done(((f32[3072,768]{1,0:T(8,128)}), f32[96,768]{1,0:T(8,128)}) %reduce-scatter.11.cloned.1.call-update) | async-done | bytes 294928 | tf_op jit(solution)/shard_map/reduce_scatter | solution.py:82
  (435 shorter events, 274.9 us)
Async XLA Ops:
  7.2 66.7 %all-gather.5.cloned.1.call-start = ((), (), s32[]{:S(2)}) async-start(), calls=%async_computation.20 | async-start | bytes 3649536 | tf_op jit(solution)/shard_map/all_gather | solution.py:122
  7.9 263.0 %all-gather.7.cloned.1.call-start = ((), (), s32[]{:S(2)}) async-start(), calls=%async_computation.21 | async-start | bytes 1216512 | tf_op jit(solution)/shard_map/all_gather | solution.py:125
  8.7 266.2 %all-gather.9.cloned.1.call-start = ((), (), s32[]{:S(2)}) async-start(), calls=%async_computation.22 | async-start | bytes 4866048 | tf_op jit(solution)/shard_map/all_gather | solution.py:129
  9.4 268.8 %all-gather.11.cloned.1.call-start = ((), (), s32[]{:S(2)}) async-start(), calls=%async_computation.23 | async-start | bytes 4866048 | tf_op jit(solution)/shard_map/all_gather | solution.py:131
  80.3 8.2 all-to-all-start
  88.6 12.2 %all-to-all-start.1 = ((bf16[64,4,192]{2,0,1:T(8,128)(2,1)}), bf16[64,4,192]{2,0,1:T(8,128)(2,1)S(1)}, u32[]{:S(2)}, u32[]{:S(2)}) async-start(bf16[64,4,192]{2,0,1:T(8,128)(2,1)} %copy.171), calls=%async_computation.1 | async-start | bytes 262144 | tf_op jit(solution)/shard_map/all_to_all | solution.py:164
  100.8 25.0 %all-to-all-start.2 = ((bf16[64,4,192]{2,0,1:T(8,128)(2,1)}), bf16[64,4,192]{2,0,1:T(8,128)(2,1)S(1)}, u32[]{:S(2)}, u32[]{:S(2)}) async-start(bf16[64,4,192]{2,0,1:T(8,128)(2,1)} %copy.173), calls=%async_computation.2 | async-start | bytes 262144 | tf_op jit(solution)/shard_map/all_to_all | solution.py:165
  125.8 16.5 %all-to-all-start.4 = ((bf16[64,4,192]{2,0,1:T(8,128)(2,1)}), bf16[64,4,192]{2,0,1:T(8,128)(2,1)S(1)}, u32[]{:S(2)}, u32[]{:S(2)}) async-start(bf16[64,4,192]{2,0,1:T(8,128)(2,1)} %copy.177), calls=%async_computation.4 | async-start | bytes 262144 | tf_op jit(solution)/shard_map/all_to_all | solution.py:163
  142.3 12.5 %all-to-all-start.5 = ((bf16[64,4,192]{2,0,1:T(8,128)(2,1)}), bf16[64,4,192]{2,0,1:T(8,128)(2,1)S(1)}, u32[]{:S(2)}, u32[]{:S(2)}) async-start(bf16[64,4,192]{2,0,1:T(8,128)(2,1)} %copy.179), calls=%async_computation.5 | async-start | bytes 262144 | tf_op jit(solution)/shard_map/all_to_all | solution.py:164
  154.8 17.7 %all-to-all-start.6 = ((bf16[64,4,192]{2,0,1:T(8,128)(2,1)}), bf16[64,4,192]{2,0,1:T(8,128)(2,1)S(1)}, u32[]{:S(2)}, u32[]{:S(2)}) async-start(bf16[64,4,192]{2,0,1:T(8,128)(2,1)} %copy.181), calls=%async_computation.6 | async-start | bytes 262144 | tf_op jit(solution)/shard_map/all_to_all | solution.py:165
  172.6 74.8 %all-to-all-start.3 = ((bf16[4,64,192]{2,1,0:T(8,128)(2,1)}), bf16[4,64,192]{2,1,0:T(8,128)(2,1)}, u32[]{:S(2)}, u32[]{:S(2)}) async-start(bf16[4,64,192]{2,1,0:T(8,128)(2,1)} %copy.175), calls=%async_computation.3 | async-start | bytes 262144 | tf_op jit(solution)/shard_map/all_to_all | solution.py:201
  247.4 23.2 %all-to-all-start.7 = ((bf16[4,64,192]{2,1,0:T(8,128)(2,1)}), bf16[4,64,192]{2,1,0:T(8,128)(2,1)S(1)}, u32[]{:S(2)}, u32[]{:S(2)}) async-start(bf16[4,64,192]{2,1,0:T(8,128)(2,1)} %copy.183), calls=%async_computation.7 | async-start | bytes 262144 | tf_op jit(solution)/shard_map/all_to_all | solution.py:201
  302.8 9.3 %all-to-all-start.12 = ((bf16[64,4,192]{2,0,1:T(8,128)(2,1)}), bf16[64,4,192]{2,0,1:T(8,128)(2,1)S(1)}, u32[]{:S(2)}, u32[]{:S(2)}) async-start(bf16[64,4,192]{2,0,1:T(8,128)(2,1)} %copy.198), calls=%async_computation.12 | async-start | bytes 262144 | tf_op jit(solution)/shard_map/all_to_all | solution.py:293
  307.4 252.2 %reduce-scatter.7.cloned.1.call-start = ((), (), s32[]{:S(2)}) async-start(), calls=%async_computation.24 | async-start | bytes 2433024 | tf_op jit(solution)/shard_map/reduce_scatter | solution.py:76
  312.2 36.2 %all-to-all-start.8 = ((bf16[64,4,192]{2,0,1:T(8,128)(2,1)}), bf16[64,4,192]{2,0,1:T(8,128)(2,1)S(1)}, u32[]{:S(2)}, u32[]{:S(2)}) async-start(bf16[64,4,192]{2,0,1:T(8,128)(2,1)} %copy.185), calls=%async_computation.8 | async-start | bytes 262144 | tf_op jit(solution)/shard_map/all_to_all | solution.py:293
  348.4 39.1 %all-to-all-start.13 = ((bf16[4,64,192]{2,1,0:T(8,128)(2,1)}), bf16[4,64,192]{2,1,0:T(8,128)(2,1)S(1)}, u32[]{:S(2)}, u32[]{:S(2)}) async-start(bf16[4,64,192]{2,1,0:T(8,128)(2,1)} %copy.200), calls=%async_computation.13 | async-start | bytes 262144 | tf_op jit(solution)/shard_map/all_to_all | solution.py:367
  387.6 9.6 %all-to-all-start.14 = ((bf16[4,64,192]{2,1,0:T(8,128)(2,1)}), bf16[4,64,192]{2,1,0:T(8,128)(2,1)S(1)}, u32[]{:S(2)}, u32[]{:S(2)}) async-start(bf16[4,64,192]{2,1,0:T(8,128)(2,1)} %copy.207), calls=%async_computation.14 | async-start | bytes 262144 | tf_op jit(solution)/shard_map/all_to_all | solution.py:374
  397.1 16.0 %all-to-all-start.15 = ((bf16[4,64,192]{2,1,0:T(8,128)(2,1)}), bf16[4,64,192]{2,1,0:T(8,128)(2,1)S(1)}, u32[]{:S(2)}, u32[]{:S(2)}) async-start(bf16[4,64,192]{2,1,0:T(8,128)(2,1)} %copy.209), calls=%async_computation.15 | async-start | bytes 262144 | tf_op jit(solution)/shard_map/all_to_all | solution.py:381
  413.2 11.8 %all-to-all-start.9 = ((bf16[4,64,192]{2,1,0:T(8,128)(2,1)}), bf16[4,64,192]{2,1,0:T(8,128)(2,1)S(1)}, u32[]{:S(2)}, u32[]{:S(2)}) async-start(bf16[4,64,192]{2,1,0:T(8,128)(2,1)} %copy.187), calls=%async_computation.9 | async-start | bytes 262144 | tf_op jit(solution)/shard_map/all_to_all | solution.py:367
  425.0 9.5 %all-to-all-start.10 = ((bf16[4,64,192]{2,1,0:T(8,128)(2,1)}), bf16[4,64,192]{2,1,0:T(8,128)(2,1)S(1)}, u32[]{:S(2)}, u32[]{:S(2)}) async-start(bf16[4,64,192]{2,1,0:T(8,128)(2,1)} %copy.194), calls=%async_computation.10 | async-start | bytes 262144 | tf_op jit(solution)/shard_map/all_to_all | solution.py:374
  434.5 9.3 %all-to-all-start.11 = ((bf16[4,64,192]{2,1,0:T(8,128)(2,1)}), bf16[4,64,192]{2,1,0:T(8,128)(2,1)S(1)}, u32[]{:S(2)}, u32[]{:S(2)}) async-start(bf16[4,64,192]{2,1,0:T(8,128)(2,1)} %copy.196), calls=%async_computation.11 | async-start | bytes 262144 | tf_op jit(solution)/shard_map/all_to_all | solution.py:381
  439.0 138.0 %reduce-scatter.13.cloned.1.call-start = ((), (), s32[]{:S(2)}) async-start(), calls=%async_computation.27 | async-start | bytes 7299072
  458.7 259.3 %reduce-scatter.9.cloned.1.call-start = ((), (), s32[]{:S(2)}) async-start(), calls=%async_computation.25 | async-start | bytes 9732096 | tf_op jit(solution)/shard_map/reduce_scatter | solution.py:80
  466.3 393.8 %reduce-scatter.11.cloned.1.call-start = ((), (), s32[]{:S(2)}) async-start(), calls=%async_computation.26 | async-start | bytes 9732096 | tf_op jit(solution)/shard_map/reduce_scatter | solution.py:82
  (77 other events, 971.4 us)
Sparse Core Ops, SparseCore 0:
  10.8 62.9 all-gather.4
  76.6 54.2 all-gather.6
  133.7 67.3 all-gather.8
  203.8 63.2 all-gather.10
  313.7 99.4 reduce-scatter.6
  458.8 118.1 reduce-scatter.12
  583.5 134.4 reduce-scatter.8
  725.5 134.5 reduce-scatter.10
where the time goes:
time: 877 us; the launch traced here: 867 us
  waiting for transfers between devices  328 us (37%)
  blocking collectives  218 us (25%)
  matrix products  114 us (13%)
  starting transfers between devices  79.9 us (9%)
  local copies, waits for them, and re-layouts  73.5 us (8%)
  other arithmetic  38.1 us (4%)
  between operations  15.9 us (2%)
    reduce_scatter x1, waiting for transfers between devices, scatter_end(): lax.psum_scatter(grad_down, ('blk', 'head'), scatter_dimension=0, tiled=T...  142 us
    reduce_scatter x1, waiting for transfers between devices, scatter_end(): lax.psum_scatter(grad_up, ('blk', 'head'), scatter_dimension=0, tiled=True)  141 us
    unnamed x2, blocking collectives  85.6 us
    unnamed x190, local copies, waits for them, and re-layouts  35.4 us
    all_gather x2, blocking collectives, per_device(): lax.all_gather(value_loc, 'blk', axis=0, tiled=True)  26.4 us
    all_gather x2, blocking collectives, per_device(): lax.all_gather(key_loc, 'blk', axis=0, tiled=True)  25.6 us
    all_gather x2, blocking collectives, per_device(): lax.all_gather(grad_numer.reshape(block_rows, local_width), 'blk', axis=0...  22.4 us
    all_gather x2, blocking collectives, per_device(): lax.all_gather(query_loc, 'blk', axis=0, tiled=True)  21.6 us
  transfers between devices with their start and end apart: 24, of which 8 were waited for; matrix products, arithmetic and copies ran while one was open for 22% of the time, Pallas kernels for 0%

commit v1 on v0

--- a/solution.py
+++ b/solution.py
@@ -1,10 +1,16 @@
 from functools import partial
+from types import SimpleNamespace
 
 import jax
 import jax.numpy as jnp
 from jax import lax
+from jax.experimental import pallas as pl
+from jax.experimental.pallas import tpu as pltpu
 from jax.sharding import PartitionSpec as P
 
+BLK = "blk"
+HEAD = "head"
+BOTH = (BLK, HEAD)
 H = 12
 HD = 64
 MB = 2
@@ -70,19 +76,19 @@
         grad_final_shift,
     ) = parts
     return (
-        lax.psum_scatter(grad_proj_in, ("blk", "head"), scatter_dimension=0, tiled=True),
-        lax.psum_scatter(grad_query_bias, ("blk", "head"), scatter_dimension=0, tiled=True),
-        lax.psum_scatter(grad_value_bias, ("blk", "head"), scatter_dimension=0, tiled=True),
-        lax.psum_scatter(grad_proj_out, ("blk", "head"), scatter_dimension=0, tiled=True),
-        lax.psum_scatter(grad_out_bias, ("blk", "head"), scatter_dimension=0, tiled=True),
-        lax.psum_scatter(grad_norm_gain, ("blk", "head"), scatter_dimension=0, tiled=True),
-        lax.psum_scatter(grad_norm_shift, ("blk", "head"), scatter_dimension=0, tiled=True),
-        lax.psum_scatter(grad_up, ("blk", "head"), scatter_dimension=0, tiled=True),
-        lax.psum_scatter(grad_up_bias, ("blk", "head"), scatter_dimension=0, tiled=True),
-        lax.psum_scatter(grad_down, ("blk", "head"), scatter_dimension=0, tiled=True),
-        lax.psum_scatter(grad_down_bias, ("blk", "head"), scatter_dimension=0, tiled=True),
-        lax.psum_scatter(grad_final_gain, ("blk", "head"), scatter_dimension=0, tiled=True),
-        lax.psum_scatter(grad_final_shift, ("blk", "head"), scatter_dimension=0, tiled=True),
+        lax.psum_scatter(grad_proj_in, BOTH, scatter_dimension=0, tiled=True),
+        lax.psum_scatter(grad_query_bias, BOTH, scatter_dimension=0, tiled=True),
+        lax.psum_scatter(grad_value_bias, BOTH, scatter_dimension=0, tiled=True),
+        lax.psum_scatter(grad_proj_out, BOTH, scatter_dimension=0, tiled=True),
+        lax.psum_scatter(grad_out_bias, BOTH, scatter_dimension=0, tiled=True),
+        lax.psum_scatter(grad_norm_gain, BOTH, scatter_dimension=0, tiled=True),
+        lax.psum_scatter(grad_norm_shift, BOTH, scatter_dimension=0, tiled=True),
+        lax.psum_scatter(grad_up, BOTH, scatter_dimension=0, tiled=True),
+        lax.psum_scatter(grad_up_bias, BOTH, scatter_dimension=0, tiled=True),
+        lax.psum_scatter(grad_down, BOTH, scatter_dimension=0, tiled=True),
+        lax.psum_scatter(grad_down_bias, BOTH, scatter_dimension=0, tiled=True),
+        lax.psum_scatter(grad_final_gain, BOTH, scatter_dimension=0, tiled=True),
+        lax.psum_scatter(grad_final_shift, BOTH, scatter_dimension=0, tiled=True),
     )
 
 
@@ -119,19 +125,19 @@
         final_gain,
         final_shift,
     ) = (
-        lax.all_gather(w_qkv, ("blk", "head"), axis=0, tiled=True),
-        lax.all_gather(bias_q, ("blk", "head"), axis=0, tiled=True),
-        lax.all_gather(bias_v, ("blk", "head"), axis=0, tiled=True),
-        lax.all_gather(w_out, ("blk", "head"), axis=0, tiled=True),
-        lax.all_gather(bias_out, ("blk", "head"), axis=0, tiled=True),
-        lax.all_gather(gain_one, ("blk", "head"), axis=0, tiled=True),
-        lax.all_gather(shift_one, ("blk", "head"), axis=0, tiled=True),
-        lax.all_gather(w_up, ("blk", "head"), axis=0, tiled=True),
-        lax.all_gather(bias_up, ("blk", "head"), axis=0, tiled=True),
-        lax.all_gather(w_down, ("blk", "head"), axis=0, tiled=True),
-        lax.all_gather(bias_down, ("blk", "head"), axis=0, tiled=True),
-        lax.all_gather(gain_two, ("blk", "head"), axis=0, tiled=True),
-        lax.all_gather(shift_two, ("blk", "head"), axis=0, tiled=True),
+        lax.all_gather(w_qkv, BOTH, axis=0, tiled=True),
+        lax.all_gather(bias_q, BOTH, axis=0, tiled=True),
+        lax.all_gather(bias_v, BOTH, axis=0, tiled=True),
+        lax.all_gather(w_out, BOTH, axis=0, tiled=True),
+        lax.all_gather(bias_out, BOTH, axis=0, tiled=True),
+        lax.all_gather(gain_one, BOTH, axis=0, tiled=True),
+        lax.all_gather(shift_one, BOTH, axis=0, tiled=True),
+        lax.all_gather(w_up, BOTH, axis=0, tiled=True),
+        lax.all_gather(bias_up, BOTH, axis=0, tiled=True),
+        lax.all_gather(w_down, BOTH, axis=0, tiled=True),
+        lax.all_gather(bias_down, BOTH, axis=0, tiled=True),
+        lax.all_gather(gain_two, BOTH, axis=0, tiled=True),
+        lax.all_gather(shift_two, BOTH, axis=0, tiled=True),
     )
     query_bias = query_bias.astype(jnp.float32)
     value_bias = value_bias.astype(jnp.float32)
@@ -144,12 +150,12 @@
     final_shift = final_shift.astype(jnp.float32)
     model_width = proj_out.shape[0]
     row_count = tokens.shape[1]
-    head_count = lax.axis_size("head")
+    head_count = lax.axis_size(HEAD)
     block_rows = row_count * head_count
     heads_dev = H // head_count
     local_width = heads_dev * HD
     scale = HD ** (-0.5)
-    local_pos = lax.axis_index("blk") * block_rows + jnp.arange(block_rows, dtype=jnp.int32)
+    local_pos = lax.axis_index(BLK) * block_rows + jnp.arange(block_rows, dtype=jnp.int32)
     kept_list = []
     outputs = []
     for part_index in range(MB):
@@ -160,9 +166,9 @@
         key_rows = projected[:, model_width : 2 * model_width].astype(jnp.bfloat16)
         value_rows = (projected[:, 2 * model_width :] + value_bias).astype(jnp.bfloat16)
         query_loc, key_loc, value_loc = (
-            lax.all_to_all(query_rows, "head", split_axis=1, concat_axis=0, tiled=True),
-            lax.all_to_all(key_rows, "head", split_axis=1, concat_axis=0, tiled=True),
-            lax.all_to_all(value_rows, "head", split_axis=1, concat_axis=0, tiled=True),
+            lax.all_to_all(query_rows, HEAD, split_axis=1, concat_axis=0, tiled=True),
+            lax.all_to_all(key_rows, HEAD, split_axis=1, concat_axis=0, tiled=True),
+            lax.all_to_all(value_rows, HEAD, split_axis=1, concat_axis=0, tiled=True),
         )
         doc_local = segment_of(starts_row, local_pos)
         query_heads = query_loc.reshape(block_rows, heads_dev, HD)
@@ -193,14 +199,14 @@
         row_top, row_total, weighted = fold_keys(
             start_state,
             (
-                lax.all_gather(key_loc, "blk", axis=0, tiled=True),
-                lax.all_gather(value_loc, "blk", axis=0, tiled=True),
+                lax.all_gather(key_loc, BLK, axis=0, tiled=True),
+                lax.all_gather(value_loc, BLK, axis=0, tiled=True),
             ),
         )
         attended = jnp.transpose(weighted / row_total, (1, 0, 2))
         mixed_rows = lax.all_to_all(
             attended.reshape(block_rows, local_width).astype(jnp.bfloat16),
-            "head",
+            HEAD,
             split_axis=0,
             concat_axis=1,
             tiled=True,
@@ -290,7 +296,7 @@
         grad_mixed = jnp.einsum(
             "rd,cd->rc", grad_attn, proj_out, preferred_element_type=jnp.float32
         ).astype(jnp.bfloat16)
-        grad_loc = lax.all_to_all(grad_mixed, "head", split_axis=1, concat_axis=0, tiled=True)
+        grad_loc = lax.all_to_all(grad_mixed, HEAD, split_axis=1, concat_axis=0, tiled=True)
         grad_heads = grad_loc.astype(jnp.float32).reshape(block_rows, heads_dev, HD)
         total_rows = jnp.transpose(row_total, (1, 0, 2))
         correction = jnp.transpose(
@@ -300,8 +306,8 @@
         query_heads = query_loc.reshape(block_rows, heads_dev, HD)
         key_heads_loc = key_loc.reshape(block_rows, heads_dev, HD)
         value_heads_loc = value_loc.reshape(block_rows, heads_dev, HD)
-        fold_key_part = lax.all_gather(key_loc, "blk", axis=0, tiled=True)
-        fold_value_part = lax.all_gather(value_loc, "blk", axis=0, tiled=True)
+        fold_key_part = lax.all_gather(key_loc, BLK, axis=0, tiled=True)
+        fold_value_part = lax.all_gather(value_loc, BLK, axis=0, tiled=True)
         fold_piece_len = fold_key_part.shape[0]
         fold_key_doc = segment_of(starts_row, jnp.arange(fold_piece_len, dtype=jnp.int32))
         fold_in_doc = (doc_local[:, None] == fold_key_doc[None, :])[None]
@@ -351,14 +357,14 @@
 
         grad_key, grad_value = fold_keygrad(
             (
-                lax.all_gather(query_loc, "blk", axis=0, tiled=True),
+                lax.all_gather(query_loc, BLK, axis=0, tiled=True),
                 lax.all_gather(
-                    grad_numer.reshape(block_rows, local_width), "blk", axis=0, tiled=True
+                    grad_numer.reshape(block_rows, local_width), BLK, axis=0, tiled=True
                 ),
-                lax.all_gather(top_rows.astype(jnp.bfloat16), "blk", axis=0, tiled=True).astype(
+                lax.all_gather(top_rows.astype(jnp.bfloat16), BLK, axis=0, tiled=True).astype(
                     jnp.float32
                 ),
-                lax.all_gather(corr_rows.astype(jnp.bfloat16), "blk", axis=0, tiled=True).astype(
+                lax.all_gather(corr_rows.astype(jnp.bfloat16), BLK, axis=0, tiled=True).astype(
                     jnp.float32
                 ),
             )
@@ -366,21 +372,21 @@
         grad_q_rows, grad_k_rows, grad_v_rows = (
             lax.all_to_all(
                 grad_query.reshape(block_rows, local_width).astype(jnp.bfloat16),
-                "head",
+                HEAD,
                 split_axis=0,
                 concat_axis=1,
                 tiled=True,
             ),
             lax.all_to_all(
                 grad_key.reshape(block_rows, local_width).astype(jnp.bfloat16),
-                "head",
+                HEAD,
                 split_axis=0,
                 concat_axis=1,
                 tiled=True,
             ),
             lax.all_to_all(
                 grad_value.reshape(block_rows, local_width).astype(jnp.bfloat16),
-                "head",
+                HEAD,
                 split_axis=0,
                 concat_axis=1,
                 tiled=True,
@@ -451,44 +457,1016 @@
     )
 
 
+MESH = pl.DeviceIdType.MESH
+F32 = jnp.float32
+BF16 = jnp.bfloat16
+DM = 768
+FF = 3072
+TOK = 64
+SEQ = 2048
+HALF = DM // 2
+QKV_N = 3 * HALF
+UP_N = FF // 2
+CHUNK = 256
+
+QKV, OUT, UP, DOWN = range(4)
+SHAPES = (
+    (4, 2, 4, 24, QKV_N),
+    (4, 4, 24, DM),
+    (4, 2, 4, 24, UP_N),
+    (4, 4, 96, DM),
+)
+
+
+def by_column(kind):
+    return kind in (QKV, UP)
+
+
+def half_shape(kind):
+    shape = SHAPES[kind]
+    return shape[2:] if by_column(kind) else (2,) + shape[2:]
+
+
+def piece_shape(kind):
+    shape = SHAPES[kind]
+    return (2,) + shape[3:] if by_column(kind) else shape[2:]
+
+
+def when(cond, run):
+    if cond is None:
+        run()
+    else:
+        pl.when(cond)(run)
+
+
+def both(left, right):
+    if left is None:
+        return right
+    if right is None:
+        return left
+    return jnp.logical_and(left, right)
+
+
+class Place:
+    def __init__(self):
+        b = lax.axis_index(BLK)
+        z = lax.axis_index(HEAD)
+        c = lax.rem(b, 2)
+        x = lax.rem(lax.div(b, 2), 2)
+        y = lax.div(b, 4)
+        self.b, self.z, self.c, self.x, self.y = b, z, c, x, y
+        self.line = 4 * b + z
+        self.chip = 4 * lax.div(b, 2) + z
+        self.sib = (b + 1 - 2 * c, z)
+        self.dx = (4 * y + 2 * (1 - x) + c, z)
+        self.dy = (4 * (1 - y) + 2 * x + c, z)
+        self.up = (b, jnp.minimum(z + 1, 3))
+        self.down = (b, jnp.maximum(z - 1, 0))
+        self.swap = (4 * c + 2 * x + y, z)
+        self.stays = y == c
+        self.moves = y != c
+        self.not_top = z < 3
+        self.not_bottom = z > 0
+        q = 2 * y + x
+        self.q = q
+        turn = lax.rem(q - z + 4, 4)
+        self.active = turn < 3
+        self.pair = jnp.where(self.active, 4 * turn + z, 0)
+        self.part = lax.div(self.pair, 6)
+
+    def cols(self, kind):
+        x, y = self.x, self.y
+        if by_column(kind):
+            return (2 * y + x, 2 * y + 1 - x, 2 * (1 - y) + x, 2 * (1 - y) + 1 - x)
+        return (2 * x + y, 2 * (1 - x) + y, 2 * x + 1 - y, 2 * (1 - x) + 1 - y)
+
+
+def pair_place(pair):
+    z = pair % 4
+    return ((pair // 4 + z) % 4, z)
+
+
+def chunk(kind, ref, col, z):
+    return ref.at[col, :, z] if by_column(kind) else ref.at[col, z]
+
+
+def half(kind, ref, col, h):
+    return ref.at[col, h] if by_column(kind) else ref.at[col, pl.ds(2 * h, 2)]
+
+
+class Links:
+    def __init__(self, sems, here):
+        self.sems, self.here, self.count, self.pending = sems, here, 0, []
+
+    def alloc(self, n=1):
+        at = self.count
+        self.count += n
+        return at
+
+    def make(self, src, dst, s, r, dev):
+        return pltpu.make_async_remote_copy(
+            src_ref=src, dst_ref=dst, send_sem=self.sems.at[s], recv_sem=self.sems.at[r],
+            device_id=dev, device_id_type=MESH,
+        )
+
+    def send(self, src, dst, s, r, dev, cond=None, keep=True):
+        when(cond, lambda: self.make(src, dst, s, r, dev).start())
+        if keep:
+            self.pending.append((cond, src, dst, s, r, dev))
+
+    def recv(self, dst, r, cond=None):
+        when(cond, lambda: self.make(dst, dst, r, r, self.here.sib).wait_recv())
+
+    def sent(self, src, dst, s, r, dev, cond=None):
+        when(cond, lambda: self.make(src, dst, s, r, dev).wait_send())
+
+    def finish(self):
+        for cond, src, dst, s, r, dev in self.pending:
+            self.sent(src, dst, s, r, dev, cond)
+        self.pending = []
+
+
+class Gather:
+    def __init__(self, links, here, kind, ref):
+        self.links, self.here, self.kind, self.ref = links, here, kind, ref
+        self.s0, self.r0 = links.alloc(), links.alloc()
+        self.su, self.sd, self.rz = links.alloc(4), links.alloc(4), links.alloc(4)
+        self.s_col = links.alloc(4)
+        self.r_col = links.alloc(4)
+        self.col, self.col_x, self.col_y, self.col_d = here.cols(kind)
+
+    def first_wait(self):
+        here, kind = self.here, self.kind
+        if by_column(kind):
+            self.links.recv(self.ref.at[self.col, 1 - here.c, here.z], self.r0)
+        else:
+            self.links.recv(self.ref.at[self.col, here.z], self.r0, here.moves)
+
+    def z_hop(self, z, up, cond):
+        piece = chunk(self.kind, self.ref, self.col, z)
+        base = self.su if up else self.sd
+        self.links.send(piece, piece, base + z, self.rz + z, self.here.up if up else self.here.down, cond)
+
+    def z_own(self):
+        self.first_wait()
+        here = self.here
+        self.z_hop(here.z, True, here.not_top)
+        self.z_hop(here.z, False, here.not_bottom)
+
+    def z_relay(self, r):
+        here = self.here
+        from_below = here.z >= r
+        from_above = here.z <= 3 - r
+        low = jnp.maximum(here.z - r, 0)
+        high = jnp.minimum(here.z + r, 3)
+        self.links.recv(chunk(self.kind, self.ref, self.col, low), self.rz + low, from_below)
+        if r < 3:
+            self.z_hop(low, True, both(from_below, here.not_top))
+        self.links.recv(chunk(self.kind, self.ref, self.col, high), self.rz + high, from_above)
+        if r < 3:
+            self.z_hop(high, False, both(from_above, here.not_bottom))
+
+    def plane_send(self):
+        piece = self.ref.at[self.col]
+        self.links.send(piece, piece, self.s_col, self.r_col, self.here.dx)
+        self.links.send(piece, piece, self.s_col + 1, self.r_col + 1, self.here.dy)
+
+    def plane_relay(self):
+        self.links.recv(self.ref.at[self.col_x], self.r_col)
+        piece = half(self.kind, self.ref, self.col_x, 0)
+        self.links.send(piece, piece, self.s_col + 2, self.r_col + 2, self.here.dy)
+        self.links.recv(self.ref.at[self.col_y], self.r_col + 1)
+        piece = half(self.kind, self.ref, self.col_y, 1)
+        self.links.send(piece, piece, self.s_col + 3, self.r_col + 3, self.here.dx)
+
+    def plane_done(self):
+        self.links.recv(half(self.kind, self.ref, self.col_d, 0), self.r_col + 2)
+        self.links.recv(half(self.kind, self.ref, self.col_d, 1), self.r_col + 3)
+
+
+def add_into(dst, terms, steps):
+    def one(i, carry):
+        total = terms[0][i].astype(F32)
+        for term in terms[1:]:
+            total = total + term[i].astype(F32)
+        dst[i] = total.astype(dst.dtype)
+        return carry
+
+    lax.fori_loop(0, steps, one, 0)
+
+
+class Scatter:
+    def __init__(self, links, here, kind, refs):
+        self.links, self.here, self.kind = links, here, kind
+        self.grad, self.rx, self.ry, self.cx, self.cy, self.zb, self.zu, self.zd, self.fin, self.last = refs
+        self.s = links.alloc(6)
+        self.r = links.alloc(6)
+        self.su, self.ru = links.alloc(4), links.alloc(4)
+        self.sd, self.rd = links.alloc(4), links.alloc(4)
+        self.s_end, self.r_end = links.alloc(), links.alloc()
+        self.col, self.col_x, self.col_y, self.col_d = here.cols(kind)
+
+    def half_of(self, ref, h):
+        return ref.at[h] if by_column(self.kind) else ref.at[pl.ds(2 * h, 2)]
+
+    def plane_send(self):
+        links, here, kind = self.links, self.here, self.kind
+        s, r = self.s, self.r
+        links.send(half(kind, self.grad, self.col_d, 0), self.rx, s, r, here.dx)
+        links.send(half(kind, self.grad, self.col_d, 1), self.ry, s + 1, r + 1, here.dy)
+        links.send(half(kind, self.grad, self.col_x, 0), self.half_of(self.cx, 0), s + 2, r + 2, here.dx)
+        links.send(half(kind, self.grad, self.col_y, 1), self.half_of(self.cy, 1), s + 3, r + 3, here.dy)
+
+    def plane_relay(self):
+        links, here, kind = self.links, self.here, self.kind
+        steps = half_shape(kind)[0]
+        s, r = self.s, self.r
+        links.recv(self.rx, r)
+        piece = half(kind, self.grad, self.col_y, 0)
+        add_into(piece, (piece, self.rx), steps)
+        links.send(piece, self.half_of(self.cy, 0), s + 4, r + 4, here.dy)
+        links.recv(self.ry, r + 1)
+        piece = half(kind, self.grad, self.col_x, 1)
+        add_into(piece, (piece, self.ry), steps)
+        links.send(piece, self.half_of(self.cx, 1), s + 5, r + 5, here.dx)
+
+    def plane_done(self):
+        links, kind = self.links, self.kind
+        r = self.r
+        links.recv(self.half_of(self.cx, 0), r + 2)
+        links.recv(self.half_of(self.cy, 1), r + 3)
+        links.recv(self.half_of(self.cy, 0), r + 4)
+        links.recv(self.half_of(self.cx, 1), r + 5)
+        own = self.grad.at[self.col]
+        if by_column(kind):
+            for h in range(2):
+                add_into(self.zb.at[h], (own.at[h], self.cx.at[h], self.cy.at[h]), 4)
+        else:
+            add_into(self.zb, (own, self.cx, self.cy), 4)
+
+    def z_piece(self, z):
+        return self.zb.at[:, z] if by_column(self.kind) else self.zb.at[z]
+
+    def z_add(self, z, other):
+        if by_column(self.kind):
+            for h in range(2):
+                self.zb[h, z] = (self.zb[h, z].astype(F32) + other[z, h].astype(F32)).astype(BF16)
+        else:
+            self.zb[z] = (self.zb[z].astype(F32) + other[z].astype(F32)).astype(BF16)
+
+    def z_step(self, target, up):
+        links, here = self.links, self.here
+        if up:
+            cond, more, buf, s, r, dev = here.z < target, here.not_bottom, self.zu, self.su, self.ru, here.up
+        else:
+            cond, more, buf, s, r, dev = here.z > target, here.not_top, self.zd, self.sd, self.rd, here.down
+
+        def add():
+            self.z_add(target, buf)
+
+        links.recv(buf.at[target], r + target, both(cond, more))
+        when(both(cond, more), add)
+        links.send(self.z_piece(target), buf.at[target], s + target, r + target, dev, cond)
+
+    def z_first(self):
+        for target, up in ((3, True), (0, False), (2, True), (1, False), (1, True), (2, False)):
+            self.z_step(target, up)
+
+    def z_last(self):
+        links, here = self.links, self.here
+        z = here.z
+        links.recv(self.zu.at[z], self.ru + z, here.not_bottom)
+        links.recv(self.zd.at[z], self.rd + z, here.not_top)
+        if by_column(self.kind):
+            for h in range(2):
+                self.fin[h] = self.zb[h, z].astype(F32)
+        else:
+            self.fin[...] = self.zb[z].astype(F32)
+
+        def add_low():
+            self.fin[...] += self.zu[z].astype(F32)
+
+        def add_high():
+            self.fin[...] += self.zd[z].astype(F32)
+
+        when(here.not_bottom, add_low)
+        when(here.not_top, add_high)
+        if by_column(self.kind):
+            links.send(self.fin.at[1 - here.c], self.last, self.s_end, self.r_end, here.sib)
+        else:
+            links.send(self.fin, self.last, self.s_end, self.r_end, here.swap, here.moves)
+
+    def finish(self, out):
+        links, here, kind = self.links, self.here, self.kind
+        c = here.c
+        if kind == QKV:
+            for j in range(3):
+                at = pl.multiple_of(DM * j + HALF * c, 128)
+                out[:, pl.ds(at, HALF)] = self.fin[c, :, HALF * j : HALF * (j + 1)]
+            links.recv(self.last, self.r_end)
+            for j in range(3):
+                at = pl.multiple_of(DM * j + HALF * (1 - c), 128)
+                out[:, pl.ds(at, HALF)] = self.last[:, HALF * j : HALF * (j + 1)]
+        elif kind == UP:
+            out[:, pl.ds(pl.multiple_of(UP_N * c, 128), UP_N)] = self.fin[c]
+            links.recv(self.last, self.r_end)
+            out[:, pl.ds(pl.multiple_of(UP_N * (1 - c), 128), UP_N)] = self.last[...]
+        else:
+            links.recv(self.last, self.r_end, here.moves)
+
+            def keep():
+                out[...] = self.fin[...]
+
+            def take():
+                out[...] = self.last[...]
+
+            when(here.stays, keep)
+            when(here.moves, take)
+
+
+def dot(a, b):
+    return jnp.dot(a, b, preferred_element_type=F32)
+
+
+def dot_nt(a, b):
+    return lax.dot_general(a, b, (((1,), (1,)), ((), ())), preferred_element_type=F32)
+
+
+def dot_tn(a, b):
+    return lax.dot_general(a, b, (((0,), (0,)), ((), ())), preferred_element_type=F32)
+
+
+def row_sum(values):
+    return jnp.sum(values, axis=0, keepdims=True)
+
+
+def div24(n):
+    return lax.shift_right_logical(n * 2731, 16)
+
+
+def iota(shape, dim):
+    return lax.broadcasted_iota(jnp.int32, shape, dim)
+
+
+def select_24():
+    n = iota((128, DM), 1)
+    return (iota((128, DM), 0) == n - 24 * div24(n)).astype(BF16)
+
+
+def select_96():
+    n = iota((128, UP_N), 1)
+    run = lax.shift_right_logical(div24(n), 2)
+    return (iota((128, UP_N), 0) == 32 + n - 96 * run).astype(BF16)
+
+
+def owner_24(lead):
+    shape = (lead, 8, DM)
+    return div24(iota(shape, 2)) == iota(shape, 0)
+
+
+def owner_96():
+    shape = (16, UP_N)
+    return lax.shift_right_logical(div24(iota(shape, 1)), 2) == iota(shape, 0)
+
+
+def exact_nt(values, select):
+    high = values.astype(BF16)
+    rest = values - high.astype(F32)
+    mid = rest.astype(BF16)
+    low = (rest - mid.astype(F32)).astype(BF16)
+    return dot_nt(high, select) + dot_nt(mid, select) + dot_nt(low, select)
+
+
+SCRATCH = dict(
+    wq=((24, QKV_N), BF16),
+    vec_all=((32, 8, 128), F32),
+    vec_rows=((8, DM), F32),
+    up_row=((1, UP_N), F32),
+    x_chip=((2, 2, TOK, DM), BF16),
+    fl_chip=((2, 2, TOK, DM), BF16),
+    gf_chip=((2, 2, TOK, DM), BF16),
+    ga_chip=((2, 2, TOK, DM), BF16),
+    partial=((2, 2, TOK, DM), F32),
+    back0=((2, TOK, DM), F32),
+    back1=((2, TOK, DM), F32),
+    back2=((2, TOK, DM), F32),
+    back3=((2, TOK, DM), F32),
+    send_q=((12, 192, 128), BF16),
+    qkv_t=((192, SEQ), BF16),
+    k_rows=((SEQ, HD), BF16),
+    v_rows=((SEQ, HD), BF16),
+    q_rows=((SEQ, HD), BF16),
+    g_rows=((SEQ, HD), BF16),
+    key_doc=((SEQ, 128), jnp.int32),
+    query_doc=((1, SEQ), jnp.int32),
+    scores=((SEQ, CHUNK), F32),
+    weights=((SEQ, SEQ), BF16),
+    total=((1, SEQ), F32),
+    att_t=((HD, SEQ), F32),
+    att_send=((HD, SEQ), BF16),
+    mix_in=((12, HD, 128), BF16),
+    g_send=((12, HD, 128), BF16),
+    g_t=((HD, SEQ), BF16),
+    gn_t=((HD, SEQ), BF16),
+    corr=((1, SEQ), F32),
+    ds=((CHUNK, SEQ), BF16),
+    dq_t=((HD, SEQ), F32),
+    d_send=((192, SEQ), BF16),
+    d_in=((12, 192, 128), BF16),
+    mixed_t=((HALF, 2 * 128), BF16),
+    first=((2 * TOK, DM), F32),
+    normed1=((2 * TOK, DM), F32),
+    inv1=((2 * TOK, 1), F32),
+    active=((4 * TOK, UP_N), BF16),
+    slope=((4 * TOK, UP_N), F32),
+    gh=((4 * TOK, UP_N), BF16),
+    gh2=((2 * TOK, DM), F32),
+    gh1=((2 * TOK, DM), F32),
+    gp=((4 * TOK, QKV_N), BF16),
+    vec_grad=((8, DM), F32),
+    up_grad=((1, UP_N), F32),
+    vec_send=((32, 8, 128), F32),
+    vec_recv=((32, 8, 128), F32),
+)
+
+
+def kind_scratch(kind):
+    shape = SHAPES[kind]
+    piece = piece_shape(kind)
+    last = piece[1:] if by_column(kind) else piece
+    low = [shape, shape, half_shape(kind), half_shape(kind), shape[1:], shape[1:], shape[1:]]
+    low += [(4,) + piece, (4,) + piece]
+    return [(s, BF16) for s in low] + [(piece, F32), (last, F32)]
+
+
+def all_scratch():
+    shapes = list(SCRATCH.values())
+    for kind in range(4):
+        shapes += kind_scratch(kind)
+    return [pltpu.VMEM(shape, dtype) for shape, dtype in shapes] + [pltpu.SemaphoreType.DMA((N_SEM,))]
+
+
+N_SEM = 512
+
+
+def layer_kernel(
+    tokens, starts, w_qkv, w_out, w_up, w_down, vecs, cotangent,
+    o_out, o_tok, o_qkv, o_bq, o_bv, o_wout, o_bo, o_g1, o_s1, o_up, o_bup, o_down, o_bd, o_g2, o_s2,
+    *scratch,
+):
+    named = len(SCRATCH)
+    m = SimpleNamespace(**dict(zip(SCRATCH, scratch)))
+    kinds = [scratch[named + 11 * kind : named + 11 * (kind + 1)] for kind in range(4)]
+    sems = scratch[-1]
+    here = Place()
+    links = Links(sems, here)
+    b, z, c = here.b, here.z, here.c
+    line, chip = here.line, here.chip
+    gathers = [Gather(links, here, kind, kinds[kind][0]) for kind in range(4)]
+    scatters = [Scatter(links, here, kind, kinds[kind][1:]) for kind in range(4)]
+
+    def peer(d):
+        other = lax.rem(line + d, 32)
+        return (lax.div(other, 4), lax.rem(other, 4))
+
+    barrier = pltpu.get_barrier_semaphore()
+
+    def greet(d, carry):
+        pl.semaphore_signal(barrier, inc=1, device_id=peer(d), device_id_type=MESH)
+        return carry
+
+    lax.fori_loop(1, 32, greet, 0)
+    pl.semaphore_wait(barrier, 31)
+
+    def pack(which):
+        return [w_qkv[:, pl.ds(pl.multiple_of(DM * j + HALF * which, 128), HALF)] for j in range(3)]
+
+    for j, block in enumerate(pack(1 - c)):
+        m.wq[:, HALF * j : HALF * (j + 1)] = block
+    g_qkv, g_out, g_up, g_down = gathers
+    slot = g_qkv.ref.at[g_qkv.col, c, z]
+    links.send(m.wq, slot, g_qkv.s0, g_qkv.r0, here.sib)
+    x_sem = links.alloc(2)
+    x_chip = m.x_chip
+    links.send(tokens, x_chip.at[:, c], x_sem, x_sem + 1, here.sib)
+    links.send(
+        w_up.at[:, pl.ds(pl.multiple_of(UP_N * (1 - c), 128), UP_N)],
+        g_up.ref.at[g_up.col, c, z], g_up.s0, g_up.r0, here.sib,
+    )
+    for gather, shard in ((g_out, w_out), (g_down, w_down)):
+        slot = gather.ref.at[2 * here.x + c, z]
+        links.send(shard, slot, gather.s0, gather.r0, here.swap, here.moves)
+    vec_sem = links.alloc(4)
+    vec_all = m.vec_all
+
+    def vec_copy(d):
+        return links.make(vecs, vec_all.at[line], vec_sem, vec_sem + 1, peer(d))
+
+    def vec_start(d, carry):
+        vec_copy(d).start()
+        return carry
+
+    lax.fori_loop(1, 32, vec_start, 0)
+
+    for j, block in enumerate(pack(c)):
+        g_qkv.ref[g_qkv.col, c, z, :, HALF * j : HALF * (j + 1)] = block
+    g_up.ref[g_up.col, c, z] = w_up[:, pl.ds(pl.multiple_of(UP_N * c, 128), UP_N)]
+
+    def keep_rows():
+        g_out.ref[g_out.col, z] = w_out[...]
+        g_down.ref[g_down.col, z] = w_down[...]
+
+    when(here.stays, keep_rows)
+    for part in range(MB):
+        x_chip[part, c] = tokens[part]
+    vec_all[line] = vecs[...]
+    m.vec_grad[...] = jnp.zeros((8, DM), F32)
+
+    g_qkv.z_own()
+    for r in (1, 2, 3):
+        g_qkv.z_relay(r)
+    g_qkv.plane_send()
+    for gather in (g_up, g_out, g_down):
+        gather.z_own()
+
+    many = vec_all.at[pl.ds(0, 31)]
+    links.make(many, many, vec_sem, vec_sem + 1, here.sib).wait_send()
+    links.recv(many, vec_sem + 1)
+    spread = dot(vec_all[...].reshape(256, 128).astype(BF16), select_24()).reshape(32, 8, DM)
+    m.vec_rows[...] = jnp.sum(jnp.where(owner_24(32), spread, 0.0), axis=0)
+    spread = dot(vec_all[pl.ds(16 * c, 16), 0, :].astype(BF16), select_96())
+    m.up_row[...] = row_sum(jnp.where(owner_96(), spread, 0.0))
+
+    def vector(j):
+        return m.vec_rows[j : j + 1, :]
+
+    def vector_half(j):
+        return m.vec_rows[j : j + 1, pl.ds(pl.multiple_of(HALF * c, 128), HALF)]
+
+    def documents():
+        def position(n):
+            q_part = lax.shift_left(lax.shift_right_logical(n, 9), 9)
+            core_part = lax.shift_left(jnp.bitwise_and(lax.shift_right_logical(n, 6), 1), 8)
+            z_part = lax.shift_left(jnp.bitwise_and(lax.shift_right_logical(n, 7), 3), 6)
+            return q_part + core_part + z_part + jnp.bitwise_and(n, 63)
+
+        def doc_of(n):
+            place = position(n)
+            doc = jnp.zeros(place.shape, jnp.int32)
+            for j in range(starts.shape[1]):
+                doc = doc + (starts[here.part, j] <= place).astype(jnp.int32)
+            return doc
+
+        m.query_doc[...] = doc_of(iota((1, SEQ), 1))
+
+        def rows(i, carry):
+            at = pl.multiple_of(i * 256, 256)
+            m.key_doc[pl.ds(at, 256), :] = doc_of(iota((256, 128), 0) + i * 256)
+            return carry
+
+        lax.fori_loop(0, SEQ // 256, rows, 0)
+
+    when(here.active, documents)
+
+    links.recv(x_chip.at[:, 1 - c], x_sem + 1)
+    g_qkv.plane_relay()
+    for gather in (g_up, g_out, g_down):
+        gather.z_relay(1)
+    g_qkv.plane_done()
+
+    def weight_qkv(j):
+        return g_qkv.ref[:, :, :, :, HALF * j : HALF * (j + 1)].reshape(DM, HALF)
+
+    def x_rows():
+        return x_chip[...].reshape(4 * TOK, DM)
+
+    send_q = m.send_q
+    for j in range(3):
+        rows = dot(x_rows(), weight_qkv(j))
+        if j == 0:
+            rows = (rows + vector_half(0)).astype(BF16) * jnp.asarray(HD ** (-0.5), BF16)
+        elif j == 1:
+            rows = rows.astype(BF16)
+        else:
+            rows = (rows + vector_half(1)).astype(BF16)
+        turned = rows.T
+        for part in range(MB):
+            piece = turned[:, 128 * part : 128 * (part + 1)].reshape(6, HD, 128)
+            send_q[6 * part : 6 * part + 6, HD * j : HD * (j + 1), :] = piece
+
+    chip_lanes = pl.ds(pl.multiple_of(chip * 128, 128), 128)
+
+    def to_pairs(src, dst_of, rows):
+        s, r, local = links.alloc(12), links.alloc(), links.alloc()
+        for pair in range(12):
+            q_to, z_to = pair_place(pair)
+            mine = jnp.logical_and(here.q == q_to, z == z_to)
+            links.send(src.at[pair], dst_of(chip_lanes), s + pair, r, (2 * q_to + c, z_to), jnp.logical_not(mine))
+
+        def own():
+            copy = pltpu.make_async_copy(src.at[here.pair], dst_of(chip_lanes), sems.at[local])
+            copy.start()
+            copy.wait()
+
+        when(here.active, own)
+        return lambda: links.recv(dst_of(pl.ds(0, 15 * 128)), r, here.active)
+
+    def to_chips(src_of, dst):
+        s, r, local = links.alloc(16), links.alloc(), links.alloc()
+        for other in range(16):
+            cond = both(here.active, chip != other)
+            lanes = pl.ds(128 * other, 128)
+            links.send(
+                src_of(lanes), dst.at[here.pair], s + other, r, (2 * (other // 4) + c, other % 4), cond
+            )
+
+        def own():
+            copy = pltpu.make_async_copy(src_of(chip_lanes), dst.at[here.pair], sems.at[local])
+            copy.start()
+            copy.wait()
+
+        when(here.active, own)
+
+        def wait():
+            links.recv(dst.at[pl.ds(0, 11)], r, here.active)
+            links.recv(dst.at[pl.ds(0, 12)], r, jnp.logical_not(here.active))
+
+        return wait
+
+    qkv_t = m.qkv_t
+    wait_q = to_pairs(send_q, lambda lanes: qkv_t.at[:, lanes], 192)
+    for r in (2, 3):
+        for gather in (g_up, g_out, g_down):
+            gather.z_relay(r)
+    for gather in (g_out, g_up, g_down):
+        gather.plane_send()
+    wait_q()
+
+    weights = m.weights
+
+    def turn_keys():
+        m.k_rows[...] = qkv_t[HD : 2 * HD, :].T
+        m.v_rows[...] = qkv_t[2 * HD : 3 * HD, :].T
+        m.q_rows[...] = qkv_t[0:HD, :].T
+
+    when(here.active, turn_keys)
+
+    def attend(i):
+        lanes = pl.ds(pl.multiple_of(i * CHUNK, CHUNK), CHUNK)
+        query = qkv_t[0:HD, lanes]
+        doc = m.query_doc[:, lanes]
+        top = None
+        for k in range(8):
+            rows = slice(256 * k, 256 * (k + 1))
+            key_doc = m.key_doc[rows, :]
+            same = jnp.concatenate([key_doc, key_doc], axis=1) == doc
+            scores = jnp.where(same, dot(m.k_rows[rows, :], query), NEG)
+            m.scores[rows, :] = scores
+            here_top = jnp.max(scores, axis=0, keepdims=True)
+            top = here_top if top is None else jnp.maximum(top, here_top)
+        total = None
+        for k in range(8):
+            rows = slice(256 * k, 256 * (k + 1))
+            grown = jnp.exp(m.scores[rows, :] - top)
+            weights[rows, lanes] = grown.astype(BF16)
+            part_sum = row_sum(grown)
+            total = part_sum if total is None else total + part_sum
+        numer = dot(qkv_t[2 * HD : 3 * HD, :], weights[:, lanes])
+        attended = numer / total
+        m.total[:, lanes] = total
+        m.att_t[:, lanes] = attended
+        m.att_send[:, lanes] = attended.astype(BF16)
+
+    def attend_some(first, last):
+        def run():
+            def one(i, carry):
+                attend(i)
+                return carry
+
+            lax.fori_loop(first, last, one, 0)
+
+        when(here.active, run)
+
+    attend_some(0, 4)
+    for gather in (g_out, g_up, g_down):
+        gather.plane_relay()
+    attend_some(4, 8)
+
+    wait_mix = to_chips(lambda lanes: m.att_send.at[:, lanes], m.mix_in)
+    wait_mix()
+    for gather in (g_out, g_up, g_down):
+        gather.plane_done()
+
+    def share(buf, values):
+        at = links.alloc(2)
+        buf[:, c] = values.reshape(MB, TOK, DM)
+        links.send(buf.at[:, c], buf.at[:, c], at, at + 1, here.sib)
+        links.recv(buf.at[:, 1 - c], at + 1)
+
+    def combine(values, back):
+        at = links.alloc(2)
+        partial = m.partial
+        partial[...] = values.reshape(MB, 2, TOK, DM)
+        links.send(partial.at[:, 1 - c], back, at, at + 1, here.sib, keep=False)
+        links.recv(back, at + 1)
+        total = partial[:, c].reshape(2 * TOK, DM) + back[...].reshape(2 * TOK, DM)
+        links.sent(partial.at[:, 1 - c], back, at, at + 1, here.sib)
+        return total
+
+    def norm_rows(values, gain, shift):
+        center = values - jnp.mean(values, axis=-1, keepdims=True)
+        inverse = lax.rsqrt(jnp.mean(center * center, axis=-1, keepdims=True) + EPS)
+        normed = center * inverse
+        return normed * gain + shift, normed, inverse
+
+    def norm_back(upstream, normed, inverse, gain):
+        scaled = upstream * gain
+        return inverse * (
+            scaled
+            - jnp.mean(scaled, axis=-1, keepdims=True)
+            - normed * jnp.mean(scaled * normed, axis=-1, keepdims=True)
+        )
+
+    mixed_t = m.mixed_t
+    mixed = []
+    for part in range(MB):
+        piece = m.mix_in[6 * part : 6 * part + 6].reshape(HALF, 128)
+        mixed_t[:, 128 * part : 128 * (part + 1)] = piece
+        mixed.append(piece.T)
+    mixed = jnp.concatenate(mixed, axis=0)
+
+    def weight_out():
+        return g_out.ref[...].reshape(HALF, DM)
+
+    attn = combine(dot(mixed, weight_out()), m.back0) + vector(2)
+    first, normed_one, inverse_one = norm_rows(
+        tokens[...].reshape(2 * TOK, DM).astype(F32) + attn, vector(3), vector(4)
+    )
+    m.first[...] = first
+    m.normed1[...] = normed_one
+    m.inv1[...] = inverse_one
+    share(m.fl_chip, first.astype(BF16))
+
+    def fl_rows():
+        return m.fl_chip[...].reshape(4 * TOK, DM)
+
+    def weight_up(j):
+        return g_up.ref[:, :, :, :, HALF * j : HALF * (j + 1)].reshape(DM, HALF)
+
+    def weight_down(j):
+        return g_down.ref[j].reshape(HALF, DM)
+
+    ffn = None
+    for j in range(4):
+        lanes = slice(HALF * j, HALF * (j + 1))
+        hidden = dot(fl_rows(), weight_up(j)) + m.up_row[:, lanes]
+        cdf = 0.5 * (1.0 + lax.erf(hidden * (0.5**0.5)))
+        m.slope[:, lanes] = cdf + hidden * (jnp.exp(-0.5 * hidden * hidden) * 0.3989422804014327)
+        m.active[:, lanes] = (hidden * cdf).astype(BF16)
+        term = dot(m.active[:, lanes], weight_down(j))
+        ffn = term if ffn is None else ffn + term
+    ffn = combine(ffn, m.back1) + vector(5)
+    result, normed_two, inverse_two = norm_rows(m.first[...] + ffn, vector(6), vector(7))
+    o_out[...] = result.reshape(MB, TOK, DM)
+
+    vec_grad = m.vec_grad
+    grad_result = cotangent[...].reshape(2 * TOK, DM).astype(F32)
+    vec_grad[6:7, :] = row_sum(grad_result * normed_two)
+    vec_grad[7:8, :] = row_sum(grad_result)
+    grad_two = norm_back(grad_result, normed_two, inverse_two, vector(6))
+    m.gh2[...] = grad_two
+    grad_ffn = grad_two.astype(BF16)
+    vec_grad[5:6, :] = row_sum(grad_ffn.astype(F32))
+    share(m.gf_chip, grad_ffn)
+
+    def gf_rows():
+        return m.gf_chip[...].reshape(4 * TOK, DM)
+
+    s_qkv, s_out, s_up, s_down = scatters
+    for j in range(4):
+        lanes = slice(HALF * j, HALF * (j + 1))
+        s_down.grad[j] = dot_tn(m.active[:, lanes], gf_rows()).astype(BF16).reshape(4, 96, DM)
+    s_down.plane_send()
+    for j in range(4):
+        lanes = slice(HALF * j, HALF * (j + 1))
+        grad_active = dot_nt(gf_rows(), weight_down(j))
+        grad_hidden = (grad_active * m.slope[:, lanes]).astype(BF16)
+        m.gh[:, lanes] = grad_hidden
+        m.up_grad[:, lanes] = row_sum(grad_hidden.astype(F32))
+    grad_first = None
+    for j in range(4):
+        lanes = slice(HALF * j, HALF * (j + 1))
+        term = dot_nt(m.gh[:, lanes], weight_up(j))
+        grad_first = term if grad_first is None else grad_first + term
+    grad_first = m.gh2[...] + combine(grad_first, m.back2)
+    normed_one = m.normed1[...]
+    vec_grad[3:4, :] = row_sum(grad_first * normed_one)
+    vec_grad[4:5, :] = row_sum(grad_first)
+    grad_one = norm_back(grad_first, normed_one, m.inv1[...], vector(3))
+    m.gh1[...] = grad_one
+    grad_attn = grad_one.astype(BF16)
+    vec_grad[2:3, :] = row_sum(grad_attn.astype(F32))
+    share(m.ga_chip, grad_attn)
+
+    def ga_rows():
+        return m.ga_chip[...].reshape(4 * TOK, DM)
+
+    turned = dot_nt(ga_rows(), weight_out()).astype(BF16).T
+    for part in range(MB):
+        m.g_send[6 * part : 6 * part + 6] = turned[:, 128 * part : 128 * (part + 1)].reshape(6, HD, 128)
+    g_t = m.g_t
+    wait_g = to_pairs(m.g_send, lambda lanes: g_t.at[:, lanes], HD)
+    for j in range(4):
+        lanes = slice(HALF * j, HALF * (j + 1))
+        s_up.grad[:, :, :, :, lanes] = (
+            dot_tn(fl_rows(), m.gh[:, lanes]).astype(BF16).reshape(4, 2, 4, 24, HALF)
+        )
+    s_up.plane_send()
+    s_out.grad[...] = dot(mixed_t[...], ga_rows()).astype(BF16).reshape(SHAPES[OUT])
+    s_out.plane_send()
+    s_down.plane_relay()
+    wait_g()
+
+    d_send = m.d_send
+
+    def turn_grads():
+        grad = g_t[...].astype(F32)
+        inverse = 1.0 / m.total[...]
+        numer = grad * inverse
+        m.gn_t[...] = numer.astype(BF16)
+        m.g_rows[...] = numer.astype(BF16).T
+        m.corr[...] = row_sum(grad * m.att_t[...]) * inverse
+        m.dq_t[...] = jnp.zeros((HD, SEQ), F32)
+
+    when(here.active, turn_grads)
+
+    def back(k):
+        at = pl.ds(pl.multiple_of(k * CHUNK, CHUNK), CHUNK)
+        value = m.v_rows[at, :]
+        for i in range(4):
+            lanes = slice(512 * i, 512 * (i + 1))
+            grad_weights = dot(value, m.gn_t[:, lanes])
+            grown = weights[at, lanes].astype(F32)
+            m.ds[:, lanes] = (grown * (grad_weights - m.corr[:, lanes])).astype(BF16)
+        ds = m.ds
+        d_send[HD : 2 * HD, at] = dot(ds[...], m.q_rows[...]).T.astype(BF16)
+        d_send[2 * HD : 3 * HD, at] = dot(weights[at, :], m.g_rows[...]).T.astype(BF16)
+        m.dq_t[...] += dot(qkv_t[HD : 2 * HD, at], ds[...])
+
+    def back_some(first, last):
+        def run():
+            def one(i, carry):
+                back(i)
+                return carry
+
+            lax.fori_loop(first, last, one, 0)
+
+        when(here.active, run)
+
+    back_some(0, 4)
+    s_up.plane_relay()
+    s_out.plane_relay()
+    s_down.plane_done()
+    s_down.z_first()
+    back_some(4, 8)
+
+    def last_query():
+        d_send[0:HD, :] = (m.dq_t[...] * (HD ** (-0.5))).astype(BF16)
+
+    when(here.active, last_query)
+    d_in = m.d_in
+    wait_d = to_chips(lambda lanes: d_send.at[:, lanes], d_in)
+    s_up.plane_done()
+    s_up.z_first()
+    s_out.plane_done()
+    s_out.z_first()
+    wait_d()
+
+    gp = m.gp
+    for part in range(MB):
+        for j in range(3):
+            piece = d_in[6 * part : 6 * part + 6, HD * j : HD * (j + 1), :].reshape(HALF, 128)
+            gp[128 * part : 128 * (part + 1), HALF * j : HALF * (j + 1)] = piece.T
+    own_half = pl.ds(pl.multiple_of(HALF * c, 128), HALF)
+    for j in range(3):
+        lanes = slice(HALF * j, HALF * (j + 1))
+        s_qkv.grad[:, :, :, :, lanes] = (
+            dot_tn(x_rows(), gp[:, lanes]).astype(BF16).reshape(4, 2, 4, 24, HALF)
+        )
+    s_qkv.plane_send()
+    vec_grad[0:1, own_half] = row_sum(gp[:, 0:HALF].astype(F32))
+    vec_grad[1:2, own_half] = row_sum(gp[:, 2 * HALF : 3 * HALF].astype(F32))
+
+    vec_send, vec_recv = m.vec_send, m.vec_recv
+    spread = jnp.where(owner_24(32), vec_grad[...][None], 0.0).reshape(256, DM)
+    vec_send[...] = exact_nt(spread, select_24()).reshape(32, 8, 128)
+    spread = jnp.where(owner_96(), m.up_grad[...], 0.0)
+    own_lines = pl.ds(16 * c, 16)
+    vec_send[own_lines, 0, :] = vec_send[own_lines, 0, :] + exact_nt(spread, select_96())
+
+    def grad_copy(d):
+        other = lax.rem(line + d, 32)
+        return links.make(vec_send.at[other], vec_recv.at[line], vec_sem + 2, vec_sem + 3, peer(d))
+
+    def grad_start(d, carry):
+        grad_copy(d).start()
+        return carry
+
+    lax.fori_loop(1, 32, grad_start, 0)
+    vec_recv[line] = vec_send[line]
+
+    grad_tokens = None
+    for j in range(3):
+        term = dot_nt(gp[:, HALF * j : HALF * (j + 1)], weight_qkv(j))
+        grad_tokens = term if grad_tokens is None else grad_tokens + term
+    o_tok[...] = (m.gh1[...] + combine(grad_tokens, m.back3)).reshape(MB, TOK, DM)
+
+    for scatter, out in ((s_down, o_down), (s_up, o_up), (s_out, o_wout)):
+        scatter.z_last()
+    s_qkv.plane_relay()
+    for scatter, out in ((s_down, o_down), (s_up, o_up), (s_out, o_wout)):
+        scatter.finish(out)
+
+    many_send, many_recv = vec_send.at[pl.ds(0, 31)], vec_recv.at[pl.ds(0, 31)]
+    links.make(many_send, many_send, vec_sem + 2, vec_sem + 3, here.sib).wait_send()
+    links.recv(many_recv, vec_sem + 3)
+    rows = jnp.sum(vec_recv[...], axis=0)
+    for j, out in enumerate((o_bq, o_bv, o_bo, o_g1, o_s1, o_bd, o_g2, o_s2)):
+        out[...] = rows[j, 0:24]
+    o_bup[...] = rows[0, 32:128]
+
+    s_qkv.plane_done()
+    s_qkv.z_first()
+    s_qkv.z_last()
+    s_qkv.finish(o_qkv)
+    links.finish()
+
+
+def fused(
+    tokens, starts, w_qkv, bias_q, bias_v, w_out, bias_out, gain_one, shift_one,
+    w_up, bias_up, w_down, bias_down, gain_two, shift_two, cotangent,
+):
+    rows = jnp.stack([bias_q, bias_v, bias_out, gain_one, shift_one, bias_down, gain_two, shift_two])
+    vecs = jnp.pad(rows.astype(F32), ((0, 0), (0, 104)))
+    vecs = vecs + jnp.pad(bias_up.astype(F32)[None], ((0, 7), (32, 0)))
+    shapes = [tokens.shape] * 2 + [w_qkv.shape, bias_q.shape, bias_v.shape, w_out.shape, bias_out.shape]
+    shapes += [gain_one.shape, shift_one.shape, w_up.shape, bias_up.shape, w_down.shape, bias_down.shape]
+    shapes += [gain_two.shape, shift_two.shape]
+    vmem = pl.BlockSpec(memory_space=pltpu.VMEM)
+    return tuple(
+        pl.pallas_call(
+            layer_kernel,
+            name="layer",
+            out_shape=[jax.ShapeDtypeStruct(shape, F32) for shape in shapes],
+            in_specs=[vmem, pl.BlockSpec(memory_space=pltpu.SMEM)] + [vmem] * 6,
+            out_specs=[vmem] * len(shapes),
+            scratch_shapes=all_scratch(),
+            compiler_params=pltpu.CompilerParams(
+                collective_id=0, has_side_effects=True, vmem_limit_bytes=63 * 2**20
+            ),
+        )(tokens, starts, w_qkv, w_out, w_up, w_down, vecs, cotangent)
+    )
+
+
 def solution(mesh):
+    small = dict(mesh.shape) == {BLK: 8, HEAD: 4}
     return jax.shard_map(
-        per_device,
+        fused if small else per_device,
         mesh=mesh,
         in_specs=(
-            P(None, ("blk", "head"), None),
+            P(None, BOTH, None),
             P(),
-            P(("blk", "head"), None),
-            P(("blk", "head")),
-            P(("blk", "head")),
-            P(("blk", "head"), None),
-            P(("blk", "head")),
-            P(("blk", "head")),
-            P(("blk", "head")),
-            P(("blk", "head"), None),
-            P(("blk", "head")),
-            P(("blk", "head"), None),
-            P(("blk", "head")),
-            P(("blk", "head")),
-            P(("blk", "head")),
-            P(None, ("blk", "head"), None),
+            P(BOTH, None),
+            P(BOTH),
+            P(BOTH),
+            P(BOTH, None),
+            P(BOTH),
+            P(BOTH),
+            P(BOTH),
+            P(BOTH, None),
+            P(BOTH),
+            P(BOTH, None),
+            P(BOTH),
+            P(BOTH),
+            P(BOTH),
+            P(None, BOTH, None),
         ),
         out_specs=(
-            P(None, ("blk", "head"), None),
-            P(None, ("blk", "head"), None),
-            P(("blk", "head"), None),
-            P(("blk", "head")),
-            P(("blk", "head")),
-            P(("blk", "head"), None),
-            P(("blk", "head")),
-            P(("blk", "head")),
-            P(("blk", "head")),
-            P(("blk", "head"), None),
-            P(("blk", "head")),
-            P(("blk", "head"), None),
-            P(("blk", "head")),
-            P(("blk", "head")),
-            P(("blk", "head")),
+            P(None, BOTH, None),
+            P(None, BOTH, None),
+            P(BOTH, None),
+            P(BOTH),
+            P(BOTH),
+            P(BOTH, None),
+            P(BOTH),
+            P(BOTH),
+            P(BOTH),
+            P(BOTH, None),
+            P(BOTH),
+            P(BOTH, None),
+            P(BOTH),
+            P(BOTH),
+            P(BOTH),
         ),
         check_vma=False,
     )

time: 877 us -> 247 us (0.28); the launches traced: 867 us -> 247 us
  waiting for transfers between devices: 328 us -> 0 us
  Pallas kernels: 0 us -> 233 us
  blocking collectives: 218 us -> 0 us
  matrix products: 114 us -> 0 us
  starting transfers between devices: 79.9 us -> 0 us
  local copies, waits for them, and re-layouts: 73.5 us -> 12.1 us
  other arithmetic: 38.1 us -> 0.67 us
  between operations: 15.9 us -> 0.76 us
    reduce_scatter x3 -> x0, waiting for transfers between devices: 283 us -> none  [the longest x1 142 us: scatter_end(): lax.psum_scatter(grad_down, ('blk', 'head'), scatter_dimension=0, tiled=T...]
    pallas_call x0 -> x1, Pallas kernels: none -> 233 us  [fused(): pl.pallas_call(layer_kernel, name='layer', out_shape=[jax.ShapeDtypeStruc...]
    all_gather x12 -> x0, blocking collectives: 132 us -> none  [the longest x2 26.4 us: per_device(): lax.all_gather(value_loc, 'blk', axis=0, tiled=True)]
    dot_general x36 -> x0, matrix products: 114 us -> none  [the longest x2 13 us: per_device(): jnp.einsum('hqk,khd->qhd', grad_scores, key_heads, preferred_element_type...]
    unnamed x2 -> x0, blocking collectives: 85.6 us -> none
    all_to_all x16 -> x0, starting transfers between devices: 79.5 us -> none  [the longest x2 17.7 us: per_device(): lax.all_to_all(attended.reshape(block_rows, local_width).astype(jnp.bfloa...]
    unnamed x190 -> x61, local copies, waits for them, and re-layouts: 35.4 us -> 12.1 us
    unnamed x9 -> x0, waiting for transfers between devices: 20.1 us -> none
  transfers between devices with their start and end apart: 24 -> 0, of which waited for: 8 -> 0; matrix products, arithmetic and copies ran while one was open for 22% -> 0% of each run, Pallas kernels for 0% -> 0%
where the time goes in v1:
time: 247 us
  Pallas kernels  233 us (94%)
  local copies, waits for them, and re-layouts  12.1 us (5%)
    pallas_call x1, Pallas kernels, fused(): pl.pallas_call(layer_kernel, name='layer', out_shape=[jax.ShapeDtypeStruc...  233 us
    unnamed x61, local copies, waits for them, and re-layouts  12.1 us

profile of v1, /device:TPU:1, one launch (start us, length us, event | category | flops | bytes accessed | tf_op | source)
XLA Modules:
  0.0 246.8 jit_solution(8981065088622456337)
XLA Ops:
  0.7 0.6 copy-done.12
  1.5 0.6 copy-done.13
  2.1 0.7 convert_add_fusion.vecs
  2.7 233.3 %layer.1 = (f32[2,64,768]{2,1,0:T(8,128)}, f32[2,64,768]{2,1,0:T(8,128)}, f32[24,2304]{1,0:T(8,128)}, f32[24]{0:T(128)}, f32[24]{0:T(128)}, /*index=5*/f32[24,76...) custom-call(bf16[2,64,768]{2,1,0:T(8,128)(2,1)} %tokens.1, ...), custom_call_target="tpu_custom_call" | custom-call | tf_op jit(solution)/shard_map/layer/pallas_call | solution.py:1417
  236.1 1.8 copy.46
  237.9 0.7 copy.47
  238.6 0.3 copy-done.3
  239.0 0.7 copy.48
  239.6 0.5 copy.49
  240.2 0.1 copy-done.21
  240.3 0.5 copy.50
  240.8 0.6 copy.51
  241.4 0.5 copy.52
  241.9 0.1 copy-done.19
  242.0 0.5 copy.53
  242.6 0.5 copy.54
  243.1 0.7 copy.55
  243.8 0.5 copy.56
  244.3 0.7 copy.57
  245.1 0.5 copy.58
  245.6 0.1 copy-done.15
  245.7 0.5 copy.59
  246.2 0.1 copy-done.14
  246.3 0.5 copy.60
  (40 shorter events, 0.3 us)
Async XLA Ops:
  0.6 0.7 copy-start.12
  0.7 0.7 copy-start.8
  0.7 0.7 copy-start.9
  0.7 0.7 copy-start.10
  0.7 0.7 copy-start.11
  0.7 0.7 copy-start.5
  0.7 0.7 copy-start.6
  0.7 0.7 copy-start.7
  1.4 0.7 copy-start.13
  236.0 1.8 copy-start
  237.9 1.1 copy-start.3
  239.0 0.7 copy-start.22
  239.0 1.8 copy-start.4
  239.0 4.1 %copy-start.2 = (f32[24,3072]{1,0:T(8,128)S(1)}, f32[24,3072]{1,0:T(8,128)}, u32[]{:S(2)}) copy-start(f32[24,3072]{1,0:T(8,128)} %get-tuple-element.39) | copy-start | bytes 884740
  239.6 0.6 copy-start.21
  240.8 0.6 copy-start.20
  241.4 0.6 copy-start.19
  242.0 0.6 copy-start.18
  243.1 0.7 copy-start.17
  243.1 1.2 copy-start.1
  244.3 0.7 copy-start.16
  245.1 0.6 copy-start.15
  245.7 0.7 copy-start.14

commit v2 on v1

--- a/solution.py
+++ b/solution.py
@@ -482,11 +482,6 @@
     return kind in (QKV, UP)
 
 
-def half_shape(kind):
-    shape = SHAPES[kind]
-    return shape[2:] if by_column(kind) else (2,) + shape[2:]
-
-
 def piece_shape(kind):
     shape = SHAPES[kind]
     return (2,) + shape[3:] if by_column(kind) else shape[2:]
@@ -520,13 +515,12 @@
         self.sib = (b + 1 - 2 * c, z)
         self.dx = (4 * y + 2 * (1 - x) + c, z)
         self.dy = (4 * (1 - y) + 2 * x + c, z)
-        self.up = (b, jnp.minimum(z + 1, 3))
-        self.down = (b, jnp.maximum(z - 1, 0))
+        self.near = z + 1 - 2 * lax.rem(z, 2)
+        self.far = lax.rem(z + 2, 4)
+        self.cross = 3 - z
         self.swap = (4 * c + 2 * x + y, z)
         self.stays = y == c
         self.moves = y != c
-        self.not_top = z < 3
-        self.not_bottom = z > 0
         q = 2 * y + x
         self.q = q
         turn = lax.rem(q - z + 4, 4)
@@ -550,13 +544,9 @@
     return ref.at[col, :, z] if by_column(kind) else ref.at[col, z]
 
 
-def half(kind, ref, col, h):
-    return ref.at[col, h] if by_column(kind) else ref.at[col, pl.ds(2 * h, 2)]
-
-
 class Links:
     def __init__(self, sems, here):
-        self.sems, self.here, self.count, self.pending = sems, here, 0, []
+        self.sems, self.here, self.count, self.pending, self.waits = sems, here, 0, [], []
 
     def alloc(self, n=1):
         at = self.count
@@ -580,10 +570,19 @@
     def sent(self, src, dst, s, r, dev, cond=None):
         when(cond, lambda: self.make(src, dst, s, r, dev).wait_send())
 
+    def local(self, src, dst, cond=None):
+        sem = self.sems.at[self.alloc()]
+        when(cond, lambda: pltpu.make_async_copy(src, dst, sem).start())
+        return lambda: when(cond, lambda: pltpu.make_async_copy(src, dst, sem).wait())
+
+    def put(self, src, dst):
+        self.waits.append(self.local(src, dst))
+
     def finish(self):
         for cond, src, dst, s, r, dev in self.pending:
             self.sent(src, dst, s, r, dev, cond)
-        self.pending = []
+        for wait in self.waits:
+            wait()
 
 
 class Gather:
@@ -591,8 +590,8 @@
         self.links, self.here, self.kind, self.ref = links, here, kind, ref
         self.s0, self.r0 = links.alloc(), links.alloc()
         self.su, self.sd, self.rz = links.alloc(4), links.alloc(4), links.alloc(4)
-        self.s_col = links.alloc(4)
-        self.r_col = links.alloc(4)
+        self.sx, self.sy, self.rx, self.ry = (links.alloc(4) for _ in range(4))
+        self.s_far, self.r_far = links.alloc(4), links.alloc(4)
         self.col, self.col_x, self.col_y, self.col_d = here.cols(kind)
 
     def first_wait(self):
@@ -602,155 +601,122 @@
         else:
             self.links.recv(self.ref.at[self.col, here.z], self.r0, here.moves)
 
-    def z_hop(self, z, up, cond):
-        piece = chunk(self.kind, self.ref, self.col, z)
-        base = self.su if up else self.sd
-        self.links.send(piece, piece, base + z, self.rz + z, self.here.up if up else self.here.down, cond)
-
-    def z_own(self):
+    def piece(self, col, z):
+        return chunk(self.kind, self.ref, col, z)
+
+    def z_hop(self, z, to, base):
+        piece = self.piece(self.col, z)
+        self.links.send(piece, piece, base + z, self.rz + z, (self.here.b, to))
+
+    def spread(self, z):
+        piece = self.piece(self.col, z)
+        self.links.send(piece, piece, self.sx + z, self.rx + z, self.here.dx)
+        self.links.send(piece, piece, self.sy + z, self.ry + z, self.here.dy)
+
+    def own_z(self):
         self.first_wait()
         here = self.here
-        self.z_hop(here.z, True, here.not_top)
-        self.z_hop(here.z, False, here.not_bottom)
-
-    def z_relay(self, r):
+        self.z_hop(here.z, here.far, self.su)
+        self.z_hop(here.z, here.near, self.sd)
+
+    def own_plane(self):
+        self.spread(self.here.z)
+
+    def land(self, z):
+        self.links.recv(self.piece(self.col, z), self.rz + z)
+
+    def hop(self):
+        self.z_hop(self.here.far, self.here.near, self.sd)
+
+    def relay(self, z):
         here = self.here
-        from_below = here.z >= r
-        from_above = here.z <= 3 - r
-        low = jnp.maximum(here.z - r, 0)
-        high = jnp.minimum(here.z + r, 3)
-        self.links.recv(chunk(self.kind, self.ref, self.col, low), self.rz + low, from_below)
-        if r < 3:
-            self.z_hop(low, True, both(from_below, here.not_top))
-        self.links.recv(chunk(self.kind, self.ref, self.col, high), self.rz + high, from_above)
-        if r < 3:
-            self.z_hop(high, False, both(from_above, here.not_bottom))
-
-    def plane_send(self):
-        piece = self.ref.at[self.col]
-        self.links.send(piece, piece, self.s_col, self.r_col, self.here.dx)
-        self.links.send(piece, piece, self.s_col + 1, self.r_col + 1, self.here.dy)
-
-    def plane_relay(self):
-        self.links.recv(self.ref.at[self.col_x], self.r_col)
-        piece = half(self.kind, self.ref, self.col_x, 0)
-        self.links.send(piece, piece, self.s_col + 2, self.r_col + 2, self.here.dy)
-        self.links.recv(self.ref.at[self.col_y], self.r_col + 1)
-        piece = half(self.kind, self.ref, self.col_y, 1)
-        self.links.send(piece, piece, self.s_col + 3, self.r_col + 3, self.here.dx)
-
-    def plane_done(self):
-        self.links.recv(half(self.kind, self.ref, self.col_d, 0), self.r_col + 2)
-        self.links.recv(half(self.kind, self.ref, self.col_d, 1), self.r_col + 3)
-
-
-def add_into(dst, terms, steps):
-    def one(i, carry):
-        total = terms[0][i].astype(F32)
-        for term in terms[1:]:
-            total = total + term[i].astype(F32)
-        dst[i] = total.astype(dst.dtype)
-        return carry
-
-    lax.fori_loop(0, steps, one, 0)
+        low = z < 2
+        piece = self.piece(jnp.where(low, self.col_x, self.col_y), z)
+        self.links.recv(piece, jnp.where(low, self.rx + z, self.ry + z))
+        dev = (jnp.where(low, here.dy[0], here.dx[0]), here.z)
+        self.links.send(piece, piece, self.s_far + z, self.r_far + z, dev)
+
+    def done(self):
+        for z in range(4):
+            if z < 2:
+                self.links.recv(self.piece(self.col_y, z), self.ry + z)
+            else:
+                self.links.recv(self.piece(self.col_x, z), self.rx + z)
+            self.links.recv(self.piece(self.col_d, z), self.r_far + z)
 
 
 class Scatter:
     def __init__(self, links, here, kind, refs):
         self.links, self.here, self.kind = links, here, kind
-        self.grad, self.rx, self.ry, self.cx, self.cy, self.zb, self.zu, self.zd, self.fin, self.last = refs
-        self.s = links.alloc(6)
-        self.r = links.alloc(6)
-        self.su, self.ru = links.alloc(4), links.alloc(4)
-        self.sd, self.rd = links.alloc(4), links.alloc(4)
+        self.grad, self.far, self.cxy, self.zb, self.zr, self.fin, self.last = refs
+        self.s_far, self.r_far = links.alloc(4), links.alloc(4)
+        self.sxy, self.rxy = links.alloc(8), links.alloc(8)
+        self.sz, self.rz = links.alloc(4), links.alloc(4)
         self.s_end, self.r_end = links.alloc(), links.alloc()
         self.col, self.col_x, self.col_y, self.col_d = here.cols(kind)
 
-    def half_of(self, ref, h):
-        return ref.at[h] if by_column(self.kind) else ref.at[pl.ds(2 * h, 2)]
-
-    def plane_send(self):
-        links, here, kind = self.links, self.here, self.kind
-        s, r = self.s, self.r
-        links.send(half(kind, self.grad, self.col_d, 0), self.rx, s, r, here.dx)
-        links.send(half(kind, self.grad, self.col_d, 1), self.ry, s + 1, r + 1, here.dy)
-        links.send(half(kind, self.grad, self.col_x, 0), self.half_of(self.cx, 0), s + 2, r + 2, here.dx)
-        links.send(half(kind, self.grad, self.col_y, 1), self.half_of(self.cy, 1), s + 3, r + 3, here.dy)
-
-    def plane_relay(self):
-        links, here, kind = self.links, self.here, self.kind
-        steps = half_shape(kind)[0]
-        s, r = self.s, self.r
-        links.recv(self.rx, r)
-        piece = half(kind, self.grad, self.col_y, 0)
-        add_into(piece, (piece, self.rx), steps)
-        links.send(piece, self.half_of(self.cy, 0), s + 4, r + 4, here.dy)
-        links.recv(self.ry, r + 1)
-        piece = half(kind, self.grad, self.col_x, 1)
-        add_into(piece, (piece, self.ry), steps)
-        links.send(piece, self.half_of(self.cx, 1), s + 5, r + 5, here.dx)
-
-    def plane_done(self):
-        links, kind = self.links, self.kind
-        r = self.r
-        links.recv(self.half_of(self.cx, 0), r + 2)
-        links.recv(self.half_of(self.cy, 1), r + 3)
-        links.recv(self.half_of(self.cy, 0), r + 4)
-        links.recv(self.half_of(self.cx, 1), r + 5)
-        own = self.grad.at[self.col]
-        if by_column(kind):
-            for h in range(2):
-                add_into(self.zb.at[h], (own.at[h], self.cx.at[h], self.cy.at[h]), 4)
+    def piece(self, col, z):
+        return chunk(self.kind, self.grad, col, z)
+
+    def add(self, dst, terms):
+        blocks = [(h,) for h in range(2)] if by_column(self.kind) else [(slice(0, None),)]
+        for at in blocks:
+            total = terms[0][at].astype(F32)
+            for term in terms[1:]:
+                total = total + term[at].astype(F32)
+            dst[at] = total.astype(dst.dtype)
+
+    def side(self, z, first):
+        here = self.here
+        to_x = z < 2 if first else z >= 2
+        col = jnp.where(to_x, self.col_x, self.col_y)
+        dev = (jnp.where(to_x, here.dx[0], here.dy[0]), here.z)
+        slot = jnp.where(to_x, z, 4 + z)
+        self.links.send(self.piece(col, z), self.cxy.at[slot], self.sxy + slot, self.rxy + slot, dev)
+
+    def send(self, z):
+        here = self.here
+        dev = (jnp.where(z < 2, here.dx[0], here.dy[0]), here.z)
+        self.links.send(self.piece(self.col_d, z), self.far.at[z], self.s_far + z, self.r_far + z, dev)
+        self.side(z, True)
+
+    def relay(self, z):
+        self.links.recv(self.far.at[z], self.r_far + z)
+        piece = self.piece(jnp.where(z < 2, self.col_y, self.col_x), z)
+        self.add(piece, (piece, self.far.at[z]))
+        self.side(z, False)
+
+    def plane(self, z):
+        self.links.recv(self.cxy.at[z], self.rxy + z)
+        self.links.recv(self.cxy.at[4 + z], self.rxy + 4 + z)
+        self.add(self.zb.at[z], (self.piece(self.col, z), self.cxy.at[z], self.cxy.at[4 + z]))
+
+    def z_first(self):
+        here = self.here
+        for i, z in enumerate((here.near, here.cross)):
+            self.links.send(self.zb.at[z], self.zr.at[i], self.sz + i, self.rz + i, (here.b, here.near))
+
+    def z_second(self):
+        here = self.here
+        self.links.recv(self.zr.at[1], self.rz + 1)
+        piece = self.zb.at[here.far]
+        self.add(piece, (piece, self.zr.at[1]))
+        self.links.send(piece, self.zr.at[2], self.sz + 2, self.rz + 2, (here.b, here.far))
+
+    def z_direct(self, z):
+        here = self.here
+        self.links.send(self.zb.at[z], self.zr.at[here.z], self.sz + z, self.rz + here.z, (here.b, z))
+
+    def z_last(self, direct=False):
+        links, here = self.links, self.here
+        own = self.zb.at[here.z]
+        if direct:
+            others = (here.near, here.cross, here.far)
         else:
-            add_into(self.zb, (own, self.cx, self.cy), 4)
-
-    def z_piece(self, z):
-        return self.zb.at[:, z] if by_column(self.kind) else self.zb.at[z]
-
-    def z_add(self, z, other):
-        if by_column(self.kind):
-            for h in range(2):
-                self.zb[h, z] = (self.zb[h, z].astype(F32) + other[z, h].astype(F32)).astype(BF16)
-        else:
-            self.zb[z] = (self.zb[z].astype(F32) + other[z].astype(F32)).astype(BF16)
-
-    def z_step(self, target, up):
-        links, here = self.links, self.here
-        if up:
-            cond, more, buf, s, r, dev = here.z < target, here.not_bottom, self.zu, self.su, self.ru, here.up
-        else:
-            cond, more, buf, s, r, dev = here.z > target, here.not_top, self.zd, self.sd, self.rd, here.down
-
-        def add():
-            self.z_add(target, buf)
-
-        links.recv(buf.at[target], r + target, both(cond, more))
-        when(both(cond, more), add)
-        links.send(self.z_piece(target), buf.at[target], s + target, r + target, dev, cond)
-
-    def z_first(self):
-        for target, up in ((3, True), (0, False), (2, True), (1, False), (1, True), (2, False)):
-            self.z_step(target, up)
-
-    def z_last(self):
-        links, here = self.links, self.here
-        z = here.z
-        links.recv(self.zu.at[z], self.ru + z, here.not_bottom)
-        links.recv(self.zd.at[z], self.rd + z, here.not_top)
-        if by_column(self.kind):
-            for h in range(2):
-                self.fin[h] = self.zb[h, z].astype(F32)
-        else:
-            self.fin[...] = self.zb[z].astype(F32)
-
-        def add_low():
-            self.fin[...] += self.zu[z].astype(F32)
-
-        def add_high():
-            self.fin[...] += self.zd[z].astype(F32)
-
-        when(here.not_bottom, add_low)
-        when(here.not_top, add_high)
+            others = (0, 2)
+        for z in others:
+            links.recv(self.zr.at[z], self.rz + z)
+        self.add(self.fin, [own] + [self.zr.at[z] for z in others])
         if by_column(self.kind):
             links.send(self.fin.at[1 - here.c], self.last, self.s_end, self.r_end, here.sib)
         else:
@@ -838,7 +804,15 @@
 
 
 SCRATCH = dict(
-    wq=((24, QKV_N), BF16),
+    vecs=((8, 128), F32),
+    cot=((2, TOK, DM), BF16),
+    b_out=((2, TOK, DM), F32),
+    b_tok=((2, TOK, DM), F32),
+    b_qkv=((24, 2 * QKV_N), F32),
+    b_wout=((24, DM), F32),
+    b_up=((24, FF), F32),
+    b_down=((96, DM), F32),
+    b_vec=((8, 128), F32),
     vec_all=((32, 8, 128), F32),
     vec_rows=((8, DM), F32),
     up_row=((1, UP_N), F32),
@@ -894,8 +868,7 @@
     shape = SHAPES[kind]
     piece = piece_shape(kind)
     last = piece[1:] if by_column(kind) else piece
-    low = [shape, shape, half_shape(kind), half_shape(kind), shape[1:], shape[1:], shape[1:]]
-    low += [(4,) + piece, (4,) + piece]
+    low = [shape, shape, (4,) + piece, (8,) + piece, (4,) + piece, (4,) + piece]
     return [(s, BF16) for s in low] + [(piece, F32), (last, F32)]
 
 
@@ -903,20 +876,24 @@
     shapes = list(SCRATCH.values())
     for kind in range(4):
         shapes += kind_scratch(kind)
+    shapes += [((24,), BF16)] * 8 + [((96,), BF16)]
     return [pltpu.VMEM(shape, dtype) for shape, dtype in shapes] + [pltpu.SemaphoreType.DMA((N_SEM,))]
 
 
-N_SEM = 512
+N_SEM = 414
 
 
 def layer_kernel(
-    tokens, starts, w_qkv, w_out, w_up, w_down, vecs, cotangent,
-    o_out, o_tok, o_qkv, o_bq, o_bv, o_wout, o_bo, o_g1, o_s1, o_up, o_bup, o_down, o_bd, o_g2, o_s2,
+    tokens, starts, w_qkv, w_out, w_up, w_down,
+    v0, v1, v2, v3, v4, v5, v6, v7, v8, cotangent,
+    o_out, o_tok, o_qkv, o_wout, o_up, o_down, o_vec,
     *scratch,
 ):
+    vec_in = (v0, v1, v2, v3, v4, v5, v6, v7, v8)
     named = len(SCRATCH)
     m = SimpleNamespace(**dict(zip(SCRATCH, scratch)))
-    kinds = [scratch[named + 11 * kind : named + 11 * (kind + 1)] for kind in range(4)]
+    kinds = [scratch[named + 8 * kind : named + 8 * (kind + 1)] for kind in range(4)]
+    vec_rows_in = scratch[-10:-1]
     sems = scratch[-1]
     here = Place()
     links = Links(sems, here)
@@ -929,6 +906,35 @@
         other = lax.rem(line + d, 32)
         return (lax.div(other, 4), lax.rem(other, 4))
 
+    g_qkv, g_out, g_up, g_down = gathers
+    x_chip = m.x_chip
+
+    def third(j, which):
+        return w_qkv.at[:, pl.ds(pl.multiple_of(DM * j + HALF * which, 128), HALF)]
+
+    def up_part(which):
+        return w_up.at[:, pl.ds(pl.multiple_of(UP_N * which, 128), UP_N)]
+
+    def slot_part(j):
+        return g_qkv.ref.at[g_qkv.col, c, z, :, pl.ds(HALF * j, HALF)]
+
+    vec_waits = [links.local(src, dst) for src, dst in zip(vec_in, vec_rows_in)]
+    qkv_waits = [links.local(third(j, c), slot_part(j)) for j in range(3)]
+    x_wait = links.local(tokens, x_chip.at[:, c])
+    up_wait = links.local(up_part(c), g_up.ref.at[g_up.col, c, z])
+    row_waits = [
+        links.local(shard, gather.ref.at[gather.col, z], here.stays)
+        for gather, shard in ((g_out, w_out), (g_down, w_down))
+    ]
+    cot_wait = links.local(cotangent, m.cot)
+    m.vec_grad[...] = jnp.zeros((8, DM), F32)
+    m.vecs[...] = jnp.zeros((8, 128), F32)
+    for wait in vec_waits:
+        wait()
+    for j in range(8):
+        m.vecs[j : j + 1, 0:24] = vec_rows_in[j][...].astype(F32).reshape(1, 24)
+    m.vecs[0:1, 32:128] = vec_rows_in[8][...].astype(F32).reshape(1, 96)
+
     barrier = pltpu.get_barrier_semaphore()
 
     def greet(d, carry):
@@ -938,21 +944,12 @@
     lax.fori_loop(1, 32, greet, 0)
     pl.semaphore_wait(barrier, 31)
 
-    def pack(which):
-        return [w_qkv[:, pl.ds(pl.multiple_of(DM * j + HALF * which, 128), HALF)] for j in range(3)]
-
-    for j, block in enumerate(pack(1 - c)):
-        m.wq[:, HALF * j : HALF * (j + 1)] = block
-    g_qkv, g_out, g_up, g_down = gathers
-    slot = g_qkv.ref.at[g_qkv.col, c, z]
-    links.send(m.wq, slot, g_qkv.s0, g_qkv.r0, here.sib)
+    q_sem = links.alloc(3)
+    for j in range(3):
+        links.send(third(j, 1 - c), slot_part(j), q_sem + j, g_qkv.r0, here.sib)
     x_sem = links.alloc(2)
-    x_chip = m.x_chip
     links.send(tokens, x_chip.at[:, c], x_sem, x_sem + 1, here.sib)
-    links.send(
-        w_up.at[:, pl.ds(pl.multiple_of(UP_N * (1 - c), 128), UP_N)],
-        g_up.ref.at[g_up.col, c, z], g_up.s0, g_up.r0, here.sib,
-    )
+    links.send(up_part(1 - c), g_up.ref.at[g_up.col, c, z], g_up.s0, g_up.r0, here.sib)
     for gather, shard in ((g_out, w_out), (g_down, w_down)):
         slot = gather.ref.at[2 * here.x + c, z]
         links.send(shard, slot, gather.s0, gather.r0, here.swap, here.moves)
@@ -960,35 +957,52 @@
     vec_all = m.vec_all
 
     def vec_copy(d):
-        return links.make(vecs, vec_all.at[line], vec_sem, vec_sem + 1, peer(d))
+        return links.make(m.vecs, vec_all.at[line], vec_sem, vec_sem + 1, peer(d))
 
     def vec_start(d, carry):
         vec_copy(d).start()
         return carry
 
     lax.fori_loop(1, 32, vec_start, 0)
-
-    for j, block in enumerate(pack(c)):
-        g_qkv.ref[g_qkv.col, c, z, :, HALF * j : HALF * (j + 1)] = block
-    g_up.ref[g_up.col, c, z] = w_up[:, pl.ds(pl.multiple_of(UP_N * c, 128), UP_N)]
-
-    def keep_rows():
-        g_out.ref[g_out.col, z] = w_out[...]
-        g_down.ref[g_down.col, z] = w_down[...]
-
-    when(here.stays, keep_rows)
-    for part in range(MB):
-        x_chip[part, c] = tokens[part]
-    vec_all[line] = vecs[...]
-    m.vec_grad[...] = jnp.zeros((8, DM), F32)
-
-    g_qkv.z_own()
-    for r in (1, 2, 3):
-        g_qkv.z_relay(r)
-    g_qkv.plane_send()
-    for gather in (g_up, g_out, g_down):
-        gather.z_own()
-
+    vec_all[line] = m.vecs[...]
+    for wait in (*qkv_waits, x_wait, up_wait, *row_waits, cot_wait):
+        wait()
+
+    g_qkv.own_z()
+    g_qkv.own_plane()
+    rest = (g_out, g_up, g_down)
+
+    def documents():
+        def position(n):
+            q_part = lax.shift_left(lax.shift_right_logical(n, 9), 9)
+            core_part = lax.shift_left(jnp.bitwise_and(lax.shift_right_logical(n, 6), 1), 8)
+            z_part = lax.shift_left(jnp.bitwise_and(lax.shift_right_logical(n, 7), 3), 6)
+            return q_part + core_part + z_part + jnp.bitwise_and(n, 63)
+
+        def doc_of(n):
+            place = position(n)
+            doc = jnp.zeros(place.shape, jnp.int32)
+            for j in range(starts.shape[1]):
+                doc = doc + (starts[here.part, j] <= place).astype(jnp.int32)
+            return doc
+
+        m.query_doc[...] = doc_of(iota((1, SEQ), 1))
+
+        def rows(i, carry):
+            at = pl.multiple_of(i * 256, 256)
+            m.key_doc[pl.ds(at, 256), :] = doc_of(iota((256, 128), 0) + i * 256)
+            return carry
+
+        lax.fori_loop(0, SEQ // 256, rows, 0)
+
+    when(here.active, documents)
+
+    g_qkv.relay(z)
+    g_qkv.land(here.far)
+    g_qkv.hop()
+    g_qkv.spread(here.far)
+    for gather in rest[:2]:
+        gather.own_z()
     many = vec_all.at[pl.ds(0, 31)]
     links.make(many, many, vec_sem, vec_sem + 1, here.sib).wait_send()
     links.recv(many, vec_sem + 1)
@@ -1003,36 +1017,20 @@
     def vector_half(j):
         return m.vec_rows[j : j + 1, pl.ds(pl.multiple_of(HALF * c, 128), HALF)]
 
-    def documents():
-        def position(n):
-            q_part = lax.shift_left(lax.shift_right_logical(n, 9), 9)
-            core_part = lax.shift_left(jnp.bitwise_and(lax.shift_right_logical(n, 6), 1), 8)
-            z_part = lax.shift_left(jnp.bitwise_and(lax.shift_right_logical(n, 7), 3), 6)
-            return q_part + core_part + z_part + jnp.bitwise_and(n, 63)
-
-        def doc_of(n):
-            place = position(n)
-            doc = jnp.zeros(place.shape, jnp.int32)
-            for j in range(starts.shape[1]):
-                doc = doc + (starts[here.part, j] <= place).astype(jnp.int32)
-            return doc
-
-        m.query_doc[...] = doc_of(iota((1, SEQ), 1))
-
-        def rows(i, carry):
-            at = pl.multiple_of(i * 256, 256)
-            m.key_doc[pl.ds(at, 256), :] = doc_of(iota((256, 128), 0) + i * 256)
-            return carry
-
-        lax.fori_loop(0, SEQ // 256, rows, 0)
-
-    when(here.active, documents)
-
+    g_qkv.land(here.near)
+    g_qkv.spread(here.near)
+    g_qkv.relay(here.far)
+    for gather in rest[:2]:
+        gather.own_plane()
+    g_qkv.land(here.cross)
+    g_qkv.spread(here.cross)
+    g_qkv.relay(here.near)
+    g_qkv.relay(here.cross)
+    for gather in rest[:2]:
+        gather.land(here.far)
+        gather.hop()
     links.recv(x_chip.at[:, 1 - c], x_sem + 1)
-    g_qkv.plane_relay()
-    for gather in (g_up, g_out, g_down):
-        gather.z_relay(1)
-    g_qkv.plane_done()
+    g_qkv.done()
 
     def weight_qkv(j):
         return g_qkv.ref[:, :, :, :, HALF * j : HALF * (j + 1)].reshape(DM, HALF)
@@ -1071,36 +1069,48 @@
         when(here.active, own)
         return lambda: links.recv(dst_of(pl.ds(0, 15 * 128)), r, here.active)
 
-    def to_chips(src_of, dst):
-        s, r, local = links.alloc(16), links.alloc(), links.alloc()
-        for other in range(16):
-            cond = both(here.active, chip != other)
-            lanes = pl.ds(128 * other, 128)
-            links.send(
-                src_of(lanes), dst.at[here.pair], s + other, r, (2 * (other // 4) + c, other % 4), cond
-            )
-
-        def own():
-            copy = pltpu.make_async_copy(src_of(chip_lanes), dst.at[here.pair], sems.at[local])
-            copy.start()
-            copy.wait()
-
-        when(here.active, own)
-
-        def wait():
-            links.recv(dst.at[pl.ds(0, 11)], r, here.active)
-            links.recv(dst.at[pl.ds(0, 12)], r, jnp.logical_not(here.active))
-
-        return wait
+    class ToChips:
+        def __init__(self, src_of, dst_of, own):
+            self.src_of, self.dst_of, self.own = src_of, dst_of, own
+            self.s, self.r = links.alloc(16), links.alloc()
+
+        def start(self, other):
+            src, dst = self.src_of(pl.ds(pl.multiple_of(128 * other, 128), 128)), self.dst_of(here.pair)
+            dev = (2 * lax.div(other, 4) + c, lax.rem(other, 4))
+            links.send(src, dst, self.s + other, self.r, dev, chip != other, keep=False)
+
+        def finish(self):
+            for other in range(16):
+                src, dst = self.src_of(pl.ds(128 * other, 128)), self.dst_of(here.pair)
+                links.pending.append((both(here.active, chip != other), src, dst, self.s + other, self.r, here.sib))
+            when(here.active, self.own)
+
+        def wait(self):
+            links.recv(self.dst_of(pl.ds(0, 11)), self.r, here.active)
+            links.recv(self.dst_of(pl.ds(0, 12)), self.r, jnp.logical_not(here.active))
 
     qkv_t = m.qkv_t
     wait_q = to_pairs(send_q, lambda lanes: qkv_t.at[:, lanes], 192)
-    for r in (2, 3):
-        for gather in (g_up, g_out, g_down):
-            gather.z_relay(r)
-    for gather in (g_out, g_up, g_down):
-        gather.plane_send()
+    for gather in rest[:2]:
+        gather.spread(here.far)
+    for gather in rest[:2]:
+        gather.relay(z)
+    for gather in rest[:2]:
+        gather.land(here.near)
+        gather.spread(here.near)
+    for gather in rest[:2]:
+        gather.relay(here.far)
     wait_q()
+    g_down.own_z()
+    for gather in rest[:2]:
+        gather.land(here.cross)
+        gather.spread(here.cross)
+    g_down.own_plane()
+
+    def own_mix():
+        m.mix_in[here.pair] = m.att_send[:, chip_lanes]
+
+    mix = ToChips(lambda lanes: m.att_send.at[:, lanes], lambda pair: m.mix_in.at[pair], own_mix)
 
     weights = m.weights
 
@@ -1136,6 +1146,8 @@
         m.total[:, lanes] = total
         m.att_t[:, lanes] = attended
         m.att_send[:, lanes] = attended.astype(BF16)
+        mix.start(2 * i)
+        mix.start(2 * i + 1)
 
     def attend_some(first, last):
         def run():
@@ -1147,16 +1159,26 @@
 
         when(here.active, run)
 
-    attend_some(0, 4)
-    for gather in (g_out, g_up, g_down):
-        gather.plane_relay()
-    attend_some(4, 8)
-
-    wait_mix = to_chips(lambda lanes: m.att_send.at[:, lanes], m.mix_in)
-    wait_mix()
-    for gather in (g_out, g_up, g_down):
-        gather.plane_done()
-
+    attend_some(0, 2)
+    for gather in rest[:2]:
+        gather.relay(here.near)
+    g_down.land(here.far)
+    g_down.hop()
+    g_down.spread(here.far)
+    attend_some(2, 5)
+    for gather in rest[:2]:
+        gather.relay(here.cross)
+    g_down.land(here.near)
+    g_down.spread(here.near)
+    g_down.relay(z)
+    attend_some(5, 8)
+
+    g_down.land(here.cross)
+    g_down.spread(here.cross)
+    g_down.relay(here.far)
+    mix.finish()
+    mix.wait()
+    g_out.done()
     def share(buf, values):
         at = links.alloc(2)
         buf[:, c] = values.reshape(MB, TOK, DM)
@@ -1200,13 +1222,15 @@
 
     attn = combine(dot(mixed, weight_out()), m.back0) + vector(2)
     first, normed_one, inverse_one = norm_rows(
-        tokens[...].reshape(2 * TOK, DM).astype(F32) + attn, vector(3), vector(4)
+        x_chip[:, c].reshape(2 * TOK, DM).astype(F32) + attn, vector(3), vector(4)
     )
     m.first[...] = first
     m.normed1[...] = normed_one
     m.inv1[...] = inverse_one
     share(m.fl_chip, first.astype(BF16))
 
+    g_down.relay(here.near)
+    g_up.done()
     def fl_rows():
         return m.fl_chip[...].reshape(4 * TOK, DM)
 
@@ -1216,21 +1240,26 @@
     def weight_down(j):
         return g_down.ref[j].reshape(HALF, DM)
 
-    ffn = None
     for j in range(4):
         lanes = slice(HALF * j, HALF * (j + 1))
         hidden = dot(fl_rows(), weight_up(j)) + m.up_row[:, lanes]
         cdf = 0.5 * (1.0 + lax.erf(hidden * (0.5**0.5)))
         m.slope[:, lanes] = cdf + hidden * (jnp.exp(-0.5 * hidden * hidden) * 0.3989422804014327)
         m.active[:, lanes] = (hidden * cdf).astype(BF16)
+    g_down.relay(here.cross)
+    g_down.done()
+    ffn = None
+    for j in range(4):
+        lanes = slice(HALF * j, HALF * (j + 1))
         term = dot(m.active[:, lanes], weight_down(j))
         ffn = term if ffn is None else ffn + term
     ffn = combine(ffn, m.back1) + vector(5)
     result, normed_two, inverse_two = norm_rows(m.first[...] + ffn, vector(6), vector(7))
-    o_out[...] = result.reshape(MB, TOK, DM)
+    m.b_out[...] = result.reshape(MB, TOK, DM)
+    links.put(m.b_out, o_out)
 
     vec_grad = m.vec_grad
-    grad_result = cotangent[...].reshape(2 * TOK, DM).astype(F32)
+    grad_result = m.cot[...].reshape(2 * TOK, DM).astype(F32)
     vec_grad[6:7, :] = row_sum(grad_result * normed_two)
     vec_grad[7:8, :] = row_sum(grad_result)
     grad_two = norm_back(grad_result, normed_two, inverse_two, vector(6))
@@ -1243,10 +1272,12 @@
         return m.gf_chip[...].reshape(4 * TOK, DM)
 
     s_qkv, s_out, s_up, s_down = scatters
+    targets = (here.near, here.cross, here.far, z)
     for j in range(4):
         lanes = slice(HALF * j, HALF * (j + 1))
         s_down.grad[j] = dot_tn(m.active[:, lanes], gf_rows()).astype(BF16).reshape(4, 96, DM)
-    s_down.plane_send()
+    for t in targets:
+        s_down.send(t)
     for j in range(4):
         lanes = slice(HALF * j, HALF * (j + 1))
         grad_active = dot_nt(gf_rows(), weight_down(j))
@@ -1281,12 +1312,27 @@
         s_up.grad[:, :, :, :, lanes] = (
             dot_tn(fl_rows(), m.gh[:, lanes]).astype(BF16).reshape(4, 2, 4, 24, HALF)
         )
-    s_up.plane_send()
+    for t in targets:
+        s_up.send(t)
     s_out.grad[...] = dot(mixed_t[...], ga_rows()).astype(BF16).reshape(SHAPES[OUT])
-    s_out.plane_send()
-    s_down.plane_relay()
+    for t in targets:
+        s_out.send(t)
+    for t in targets:
+        s_down.relay(t)
     wait_g()
 
+    d_in = m.d_in
+
+    def own_kv():
+        d_in[here.pair, HD : 3 * HD, :] = d_send[HD : 3 * HD, chip_lanes]
+
+    def own_q():
+        d_in[here.pair, 0:HD, :] = d_send[0:HD, chip_lanes]
+
+    grad_kv = ToChips(
+        lambda lanes: d_send.at[pl.ds(HD, 2 * HD), lanes], lambda pair: d_in.at[pair, pl.ds(HD, 2 * HD)], own_kv
+    )
+    grad_q = ToChips(lambda lanes: d_send.at[pl.ds(0, HD), lanes], lambda pair: d_in.at[pair, pl.ds(0, HD)], own_q)
     d_send = m.d_send
 
     def turn_grads():
@@ -1311,6 +1357,8 @@
         ds = m.ds
         d_send[HD : 2 * HD, at] = dot(ds[...], m.q_rows[...]).T.astype(BF16)
         d_send[2 * HD : 3 * HD, at] = dot(weights[at, :], m.g_rows[...]).T.astype(BF16)
+        grad_kv.start(2 * k)
+        grad_kv.start(2 * k + 1)
         m.dq_t[...] += dot(qkv_t[HD : 2 * HD, at], ds[...])
 
     def back_some(first, last):
@@ -1324,24 +1372,27 @@
         when(here.active, run)
 
     back_some(0, 4)
-    s_up.plane_relay()
-    s_out.plane_relay()
-    s_down.plane_done()
-    s_down.z_first()
     back_some(4, 8)
 
     def last_query():
         d_send[0:HD, :] = (m.dq_t[...] * (HD ** (-0.5))).astype(BF16)
+        for other in range(16):
+            grad_q.start(other)
 
     when(here.active, last_query)
-    d_in = m.d_in
-    wait_d = to_chips(lambda lanes: d_send.at[:, lanes], d_in)
-    s_up.plane_done()
-    s_up.z_first()
-    s_out.plane_done()
-    s_out.z_first()
-    wait_d()
-
+    grad_kv.finish()
+    grad_q.finish()
+    for t in targets:
+        s_up.relay(t)
+    for t in targets:
+        s_out.relay(t)
+    for t in targets:
+        s_down.plane(t)
+        if t is here.cross:
+            s_down.z_first()
+    grad_kv.wait()
+    grad_q.wait()
+    s_down.z_second()
     gp = m.gp
     for part in range(MB):
         for j in range(3):
@@ -1353,7 +1404,8 @@
         s_qkv.grad[:, :, :, :, lanes] = (
             dot_tn(x_rows(), gp[:, lanes]).astype(BF16).reshape(4, 2, 4, 24, HALF)
         )
-    s_qkv.plane_send()
+    for t in targets:
+        s_qkv.send(t)
     vec_grad[0:1, own_half] = row_sum(gp[:, 0:HALF].astype(F32))
     vec_grad[1:2, own_half] = row_sum(gp[:, 2 * HALF : 3 * HALF].astype(F32))
 
@@ -1379,53 +1431,93 @@
     for j in range(3):
         term = dot_nt(gp[:, HALF * j : HALF * (j + 1)], weight_qkv(j))
         grad_tokens = term if grad_tokens is None else grad_tokens + term
-    o_tok[...] = (m.gh1[...] + combine(grad_tokens, m.back3)).reshape(MB, TOK, DM)
-
-    for scatter, out in ((s_down, o_down), (s_up, o_up), (s_out, o_wout)):
+    m.b_tok[...] = (m.gh1[...] + combine(grad_tokens, m.back3)).reshape(MB, TOK, DM)
+    links.put(m.b_tok, o_tok)
+
+    for scatter in (s_up, s_out):
+        for t in targets:
+            scatter.plane(t)
+            if t is here.cross:
+                scatter.z_first()
+    for t in targets:
+        s_qkv.relay(t)
+    s_up.z_second()
+    s_out.z_second()
+    for t in targets:
+        s_qkv.plane(t)
+        if t is not z:
+            s_qkv.z_direct(t)
+    for scatter in (s_down, s_up, s_out):
         scatter.z_last()
-    s_qkv.plane_relay()
-    for scatter, out in ((s_down, o_down), (s_up, o_up), (s_out, o_wout)):
+    for scatter, out, to in ((s_down, m.b_down, o_down), (s_up, m.b_up, o_up), (s_out, m.b_wout, o_wout)):
         scatter.finish(out)
+        links.put(out, to)
 
     many_send, many_recv = vec_send.at[pl.ds(0, 31)], vec_recv.at[pl.ds(0, 31)]
     links.make(many_send, many_send, vec_sem + 2, vec_sem + 3, here.sib).wait_send()
     links.recv(many_recv, vec_sem + 3)
-    rows = jnp.sum(vec_recv[...], axis=0)
-    for j, out in enumerate((o_bq, o_bv, o_bo, o_g1, o_s1, o_bd, o_g2, o_s2)):
-        out[...] = rows[j, 0:24]
-    o_bup[...] = rows[0, 32:128]
-
-    s_qkv.plane_done()
-    s_qkv.z_first()
-    s_qkv.z_last()
-    s_qkv.finish(o_qkv)
+    m.b_vec[...] = jnp.sum(vec_recv[...], axis=0)
+    links.put(m.b_vec, o_vec)
+
+    s_qkv.z_last(direct=True)
+    s_qkv.finish(m.b_qkv)
+    links.put(m.b_qkv, o_qkv)
     links.finish()
+    assert links.count == N_SEM, links.count
+
+
+def place_kernel(*refs):
+    ins, big_out, vec_out = refs[0:7], refs[7:13], refs[13:22]
+    held, rows, sems = refs[22:29], refs[29:38], refs[38]
+    loads = [pltpu.make_async_copy(src, dst, sems.at[i]) for i, (src, dst) in enumerate(zip(ins, held))]
+    for load in reversed(loads):
+        load.start()
+    stores = [pltpu.make_async_copy(src, dst, sems.at[7 + i]) for i, (src, dst) in enumerate(zip(held, big_out))]
+    stores += [pltpu.make_async_copy(src, dst, sems.at[13 + i]) for i, (src, dst) in enumerate(zip(rows, vec_out))]
+    loads[6].wait()
+    for j in range(8):
+        rows[j][...] = held[6][j, 0:24]
+    rows[8][...] = held[6][0, 32:128]
+    for store in stores[6:]:
+        store.start()
+    for load, store in zip(loads, stores[:6]):
+        load.wait()
+        store.start()
+    for store in stores:
+        store.wait()
 
 
 def fused(
     tokens, starts, w_qkv, bias_q, bias_v, w_out, bias_out, gain_one, shift_one,
     w_up, bias_up, w_down, bias_down, gain_two, shift_two, cotangent,
 ):
-    rows = jnp.stack([bias_q, bias_v, bias_out, gain_one, shift_one, bias_down, gain_two, shift_two])
-    vecs = jnp.pad(rows.astype(F32), ((0, 0), (0, 104)))
-    vecs = vecs + jnp.pad(bias_up.astype(F32)[None], ((0, 7), (32, 0)))
-    shapes = [tokens.shape] * 2 + [w_qkv.shape, bias_q.shape, bias_v.shape, w_out.shape, bias_out.shape]
-    shapes += [gain_one.shape, shift_one.shape, w_up.shape, bias_up.shape, w_down.shape, bias_down.shape]
-    shapes += [gain_two.shape, shift_two.shape]
-    vmem = pl.BlockSpec(memory_space=pltpu.VMEM)
-    return tuple(
-        pl.pallas_call(
-            layer_kernel,
-            name="layer",
-            out_shape=[jax.ShapeDtypeStruct(shape, F32) for shape in shapes],
-            in_specs=[vmem, pl.BlockSpec(memory_space=pltpu.SMEM)] + [vmem] * 6,
-            out_specs=[vmem] * len(shapes),
-            scratch_shapes=all_scratch(),
-            compiler_params=pltpu.CompilerParams(
-                collective_id=0, has_side_effects=True, vmem_limit_bytes=63 * 2**20
-            ),
-        )(tokens, starts, w_qkv, w_out, w_up, w_down, vecs, cotangent)
-    )
+    anywhere = pl.BlockSpec(memory_space=pl.ANY)
+    vectors = (bias_q, bias_v, bias_out, gain_one, shift_one, bias_down, gain_two, shift_two, bias_up)
+    big = [tokens.shape, tokens.shape, w_qkv.shape, w_out.shape, w_up.shape, w_down.shape]
+    big = [jax.ShapeDtypeStruct(shape, F32) for shape in big]
+    small = [jax.ShapeDtypeStruct(vector.shape, F32) for vector in vectors]
+    made = pl.pallas_call(
+        layer_kernel,
+        name="layer",
+        out_shape=big + [jax.ShapeDtypeStruct((8, 128), F32)],
+        in_specs=[anywhere, pl.BlockSpec(memory_space=pltpu.SMEM)] + [anywhere] * 14,
+        out_specs=[anywhere] * 7,
+        scratch_shapes=all_scratch(),
+        compiler_params=pltpu.CompilerParams(
+            collective_id=0, has_side_effects=True, vmem_limit_bytes=63 * 2**20
+        ),
+    )(tokens, starts, w_qkv, w_out, w_up, w_down, *vectors, cotangent)
+    placed = pl.pallas_call(
+        place_kernel,
+        name="place",
+        out_shape=big + small,
+        in_specs=[anywhere] * 7,
+        out_specs=[anywhere] * 15,
+        scratch_shapes=[pltpu.VMEM(array.shape, F32) for array in (*made, *vectors)]
+        + [pltpu.SemaphoreType.DMA((22,))],
+    )(*made)
+    out, tok, g_qkv, g_wout, g_up, g_down, bq, bv, bo, g1, s1, bd, g2, s2, bup = placed
+    return (out, tok, g_qkv, bq, bv, g_wout, bo, g1, s1, g_up, bup, g_down, bd, g2, s2)
 
 
 def solution(mesh):

time: 247 us -> 188 us (0.76)
  Pallas kernels: 233 us -> 187 us
  local copies, waits for them, and re-layouts: 12.1 us -> 0 us
    pallas_call x1 -> x2, Pallas kernels: 233 us -> 187 us  [the longest x1 184 us: fused(): pl.pallas_call(layer_kernel, name='layer', out_shape=big + [jax.ShapeDtyp...]
    unnamed x61 -> x0, local copies, waits for them, and re-layouts: 12.1 us -> none
where the time goes in v2:
time: 188 us; the launch traced here: 187 us
  Pallas kernels  187 us (99%)
    pallas_call x1, Pallas kernels, fused(): pl.pallas_call(layer_kernel, name='layer', out_shape=big + [jax.ShapeDtyp...  184 us

profile of v2, /device:TPU:1, one launch (start us, length us, event | category | flops | bytes accessed | tf_op | source)
XLA Modules:
  0.0 187.4 jit_solution(17712417449109865682)
XLA Ops:
  0.7 183.8 %layer.1 = (f32[2,64,768]{2,1,0:T(8,128)}, f32[2,64,768]{2,1,0:T(8,128)}, f32[24,2304]{1,0:T(8,128)}, f32[24,768]{1,0:T(8,128)}, f32[24,3072]{1,0:T(8,128)}, /*index=5*/f32[96,768]{1,0:T(8,128)}, f32[8,128]{1,0:T(8,128)}) custom-call(bf16[2,64,768]{2,1,0:T(8,128)(2,1)} %tokens.1, s32[2,16]{1,0:T(2,128)} %starts.1, bf16[24,2304]{1,0:T(8,128)(2,1)} %w_qkv.1, ...), custom_call_target="tpu_custom_call" | custom-call | tf_op jit(solution)/shard_map/layer/pallas_call | solution.py:1499
  184.5 2.8 %place.1 = (f32[2,64,768]{2,1,0:T(8,128)}, f32[2,64,768]{2,1,0:T(8,128)}, f32[24,2304]{1,0:T(8,128)}, f32[24,768]{1,0:T(8,128)}, f32[24,3072]{1,0:T(8,128)}, /*i...) custom-call(f32[2,64,768]{2,1,0:T(8,128)} %get-tuple-element.37.refs, ...), custom_call_target="tpu_custom_call" | custom-call | tf_op jit(solution)/shard_map/place/pallas_call | solution.py:1510

commit v3 on v2

--- a/solution.py
+++ b/solution.py
@@ -465,25 +465,30 @@
 TOK = 64
 SEQ = 2048
 HALF = DM // 2
-QKV_N = 3 * HALF
+GROUP = 3 * HD
 UP_N = FF // 2
 CHUNK = 256
-
-QKV, OUT, UP, DOWN = range(4)
+PAIRS = 6
+
+QKV, OUT, UP, DOWN, KV, Q = range(6)
 SHAPES = (
-    (4, 2, 4, 24, QKV_N),
+    (2, 2, 2, 4, 24, 3 * GROUP),
     (4, 4, 24, DM),
     (4, 2, 4, 24, UP_N),
     (4, 4, 96, DM),
+    (2, 2, 2, 4, 24, 2 * GROUP),
+    (2, 2, 2, 4, 24, GROUP),
 )
 
 
 def by_column(kind):
-    return kind in (QKV, UP)
+    return kind == UP
 
 
 def piece_shape(kind):
     shape = SHAPES[kind]
+    if kind in (QKV, KV, Q):
+        return shape[1:3] + shape[4:]
     return (2,) + shape[3:] if by_column(kind) else shape[2:]
 
 
@@ -495,10 +500,6 @@
 
 
 def both(left, right):
-    if left is None:
-        return right
-    if right is None:
-        return left
     return jnp.logical_and(left, right)
 
 
@@ -511,22 +512,25 @@
         y = lax.div(b, 4)
         self.b, self.z, self.c, self.x, self.y = b, z, c, x, y
         self.line = 4 * b + z
-        self.chip = 4 * lax.div(b, 2) + z
         self.sib = (b + 1 - 2 * c, z)
         self.dx = (4 * y + 2 * (1 - x) + c, z)
         self.dy = (4 * (1 - y) + 2 * x + c, z)
+        self.dx_other = (4 * y + 2 * (1 - x) + 1 - c, z)
         self.near = z + 1 - 2 * lax.rem(z, 2)
         self.far = lax.rem(z + 2, 4)
         self.cross = 3 - z
         self.swap = (4 * c + 2 * x + y, z)
         self.stays = y == c
         self.moves = y != c
-        q = 2 * y + x
-        self.q = q
-        turn = lax.rem(q - z + 4, 4)
-        self.active = turn < 3
-        self.pair = jnp.where(self.active, 4 * turn + z, 0)
-        self.part = lax.div(self.pair, 6)
+        self.group = 2 * c + x
+        self.seat = 4 * y + z
+        self.chip = 2 * self.seat + x
+        idle = jnp.logical_or(both(z == 0, y == 1), both(z == 3, y == 0))
+        self.active = jnp.logical_not(idle)
+        inner = jnp.where(z == 1, 4 * y, 1 + 4 * y)
+        outer = jnp.where(z == 0, 2, 3)
+        self.pair = jnp.where(jnp.logical_or(z == 1, z == 2), inner, outer)
+        self.part = lax.div(self.pair, 3)
 
     def cols(self, kind):
         x, y = self.x, self.y
@@ -535,9 +539,7 @@
         return (2 * x + y, 2 * (1 - x) + y, 2 * x + 1 - y, 2 * (1 - x) + 1 - y)
 
 
-def pair_place(pair):
-    z = pair % 4
-    return ((pair // 4 + z) % 4, z)
+SEATS = ((0, 1), (0, 2), (0, 0), (1, 3), (1, 1), (1, 2))
 
 
 def chunk(kind, ref, col, z):
@@ -546,7 +548,8 @@
 
 class Links:
     def __init__(self, sems, here):
-        self.sems, self.here, self.count, self.pending, self.waits = sems, here, 0, [], []
+        self.sems, self.here, self.count = sems, here, 0
+        self.waits = []
 
     def alloc(self, n=1):
         at = self.count
@@ -559,16 +562,17 @@
             device_id=dev, device_id_type=MESH,
         )
 
-    def send(self, src, dst, s, r, dev, cond=None, keep=True):
+    def send(self, src, dst, s, r, dev, cond=None):
         when(cond, lambda: self.make(src, dst, s, r, dev).start())
-        if keep:
-            self.pending.append((cond, src, dst, s, r, dev))
 
     def recv(self, dst, r, cond=None):
         when(cond, lambda: self.make(dst, dst, r, r, self.here.sib).wait_recv())
 
-    def sent(self, src, dst, s, r, dev, cond=None):
-        when(cond, lambda: self.make(src, dst, s, r, dev).wait_send())
+    def sent(self, src, s, cond=None):
+        when(cond, lambda: self.make(src, src, s, s, self.here.sib).wait_send())
+
+    def drain(self, like, s, cond=None):
+        self.waits.append(lambda: self.sent(like, s, cond))
 
     def local(self, src, dst, cond=None):
         sem = self.sems.at[self.alloc()]
@@ -579,8 +583,6 @@
         self.waits.append(self.local(src, dst))
 
     def finish(self):
-        for cond, src, dst, s, r, dev in self.pending:
-            self.sent(src, dst, s, r, dev, cond)
         for wait in self.waits:
             wait()
 
@@ -589,14 +591,17 @@
     def __init__(self, links, here, kind, ref):
         self.links, self.here, self.kind, self.ref = links, here, kind, ref
         self.s0, self.r0 = links.alloc(), links.alloc()
-        self.su, self.sd, self.rz = links.alloc(4), links.alloc(4), links.alloc(4)
-        self.sx, self.sy, self.rx, self.ry = (links.alloc(4) for _ in range(4))
-        self.s_far, self.r_far = links.alloc(4), links.alloc(4)
+        self.sz, self.rz = links.alloc(), links.alloc(4)
+        self.s_plane, self.s_relay = links.alloc(), links.alloc()
+        self.r_relay, self.r_rest = links.alloc(4), links.alloc()
         self.col, self.col_x, self.col_y, self.col_d = here.cols(kind)
+        links.drain(ref.at[0, :, pl.ds(0, 3)] if by_column(kind) else ref.at[0, pl.ds(0, 3)], self.sz)
+        links.drain(ref.at[pl.ds(0, 2)], self.s_plane)
+        links.drain(ref.at[0], self.s_relay)
 
     def first_wait(self):
-        here, kind = self.here, self.kind
-        if by_column(kind):
+        here = self.here
+        if by_column(self.kind):
             self.links.recv(self.ref.at[self.col, 1 - here.c, here.z], self.r0)
         else:
             self.links.recv(self.ref.at[self.col, here.z], self.r0, here.moves)
@@ -604,20 +609,22 @@
     def piece(self, col, z):
         return chunk(self.kind, self.ref, col, z)
 
-    def z_hop(self, z, to, base):
+    def z_hop(self, z, to):
         piece = self.piece(self.col, z)
-        self.links.send(piece, piece, base + z, self.rz + z, (self.here.b, to))
+        self.links.send(piece, piece, self.sz, self.rz + z, (self.here.b, to))
 
     def spread(self, z):
         piece = self.piece(self.col, z)
-        self.links.send(piece, piece, self.sx + z, self.rx + z, self.here.dx)
-        self.links.send(piece, piece, self.sy + z, self.ry + z, self.here.dy)
+        on_y = z < 1
+        to_x = jnp.where(on_y, self.r_relay + z, self.r_rest)
+        to_y = jnp.where(on_y, self.r_rest, self.r_relay + z)
+        self.links.send(piece, piece, self.s_plane, to_x, self.here.dx)
+        self.links.send(piece, piece, self.s_plane, to_y, self.here.dy)
 
     def own_z(self):
-        self.first_wait()
         here = self.here
-        self.z_hop(here.z, here.far, self.su)
-        self.z_hop(here.z, here.near, self.sd)
+        self.z_hop(here.z, here.far)
+        self.z_hop(here.z, here.near)
 
     def own_plane(self):
         self.spread(self.here.z)
@@ -626,97 +633,129 @@
         self.links.recv(self.piece(self.col, z), self.rz + z)
 
     def hop(self):
-        self.z_hop(self.here.far, self.here.near, self.sd)
+        self.z_hop(self.here.far, self.here.near)
 
     def relay(self, z):
         here = self.here
-        low = z < 2
-        piece = self.piece(jnp.where(low, self.col_x, self.col_y), z)
-        self.links.recv(piece, jnp.where(low, self.rx + z, self.ry + z))
-        dev = (jnp.where(low, here.dy[0], here.dx[0]), here.z)
-        self.links.send(piece, piece, self.s_far + z, self.r_far + z, dev)
+        on_y = z < 1
+        piece = self.piece(jnp.where(on_y, self.col_x, self.col_y), z)
+        self.links.recv(piece, self.r_relay + z)
+        dev = (jnp.where(on_y, here.dy[0], here.dx[0]), here.z)
+        self.links.send(piece, piece, self.s_relay, self.r_rest, dev)
 
     def done(self):
-        for z in range(4):
-            if z < 2:
-                self.links.recv(self.piece(self.col_y, z), self.ry + z)
-            else:
-                self.links.recv(self.piece(self.col_x, z), self.rx + z)
-            self.links.recv(self.piece(self.col_d, z), self.r_far + z)
+        self.links.recv(self.ref.at[pl.ds(0, 2)], self.r_rest)
+
+
+class PairGather:
+    def __init__(self, links, here, ref):
+        self.links, self.here, self.ref = links, here, ref
+        self.s0, self.r0 = links.alloc(), links.alloc()
+        self.sz, self.rz = links.alloc(), links.alloc(4)
+        self.sy, self.ry = links.alloc(), links.alloc()
+        links.drain(ref.at[0, 0, 0, pl.ds(0, 3)], self.s0)
+        links.drain(ref.at[0, :, :, pl.ds(0, 3)], self.sz)
+        links.drain(ref.at[0], self.sy)
+
+    def first_wait(self):
+        self.links.recv(self.ref.at[0, 0, 0, pl.ds(0, 3)], self.r0)
+
+    def piece(self, z):
+        return self.ref.at[self.here.y, :, :, z]
+
+    def z_hop(self, z, to):
+        self.links.send(self.piece(z), self.piece(z), self.sz, self.rz + z, (self.here.b, to))
+
+    def own_z(self):
+        here = self.here
+        self.z_hop(here.z, here.far)
+        self.z_hop(here.z, here.near)
+
+    def land(self, z):
+        self.links.recv(self.piece(z), self.rz + z)
+
+    def hop(self):
+        self.z_hop(self.here.far, self.here.near)
+
+    def spread(self, z):
+        self.links.send(self.piece(z), self.piece(z), self.sy, self.ry, self.here.dy)
+
+    def done(self):
+        self.links.recv(self.ref.at[0], self.ry)
+
+
+def add_blocks(dst, terms, blocks):
+    for at in blocks:
+        total = terms[0][at].astype(F32)
+        for term in terms[1:]:
+            total = total + term[at].astype(F32)
+        dst[at] = total.astype(dst.dtype)
 
 
 class Scatter:
     def __init__(self, links, here, kind, refs):
         self.links, self.here, self.kind = links, here, kind
         self.grad, self.far, self.cxy, self.zb, self.zr, self.fin, self.last = refs
-        self.s_far, self.r_far = links.alloc(4), links.alloc(4)
-        self.sxy, self.rxy = links.alloc(8), links.alloc(8)
-        self.sz, self.rz = links.alloc(4), links.alloc(4)
+        self.s_first, self.s_relay, self.sz = links.alloc(), links.alloc(), links.alloc()
+        self.r_far, self.r_plane, self.rz = links.alloc(4), links.alloc(4), links.alloc(3)
         self.s_end, self.r_end = links.alloc(), links.alloc()
         self.col, self.col_x, self.col_y, self.col_d = here.cols(kind)
+        links.drain(self.cxy, self.s_first)
+        links.drain(self.far, self.s_relay)
+        links.drain(self.zr.at[pl.ds(0, 3)], self.sz)
+        if by_column(kind):
+            links.drain(self.last, self.s_end)
+        else:
+            links.drain(self.last, self.s_end, here.moves)
 
     def piece(self, col, z):
         return chunk(self.kind, self.grad, col, z)
 
     def add(self, dst, terms):
-        blocks = [(h,) for h in range(2)] if by_column(self.kind) else [(slice(0, None),)]
-        for at in blocks:
-            total = terms[0][at].astype(F32)
-            for term in terms[1:]:
-                total = total + term[at].astype(F32)
-            dst[at] = total.astype(dst.dtype)
-
-    def side(self, z, first):
+        add_blocks(dst, terms, [(h,) for h in range(2)] if by_column(self.kind) else [(slice(0, None),)])
+
+    def side(self, z, to_x, sem):
         here = self.here
-        to_x = z < 2 if first else z >= 2
         col = jnp.where(to_x, self.col_x, self.col_y)
         dev = (jnp.where(to_x, here.dx[0], here.dy[0]), here.z)
         slot = jnp.where(to_x, z, 4 + z)
-        self.links.send(self.piece(col, z), self.cxy.at[slot], self.sxy + slot, self.rxy + slot, dev)
+        self.links.send(self.piece(col, z), self.cxy.at[slot], sem, self.r_plane + z, dev)
 
     def send(self, z):
         here = self.here
-        dev = (jnp.where(z < 2, here.dx[0], here.dy[0]), here.z)
-        self.links.send(self.piece(self.col_d, z), self.far.at[z], self.s_far + z, self.r_far + z, dev)
-        self.side(z, True)
+        to_x = z >= 2
+        dev = (jnp.where(to_x, here.dx[0], here.dy[0]), here.z)
+        self.links.send(self.piece(self.col_d, z), self.far.at[z], self.s_first, self.r_far + z, dev)
+        self.side(z, to_x, self.s_first)
 
     def relay(self, z):
+        to_y = z >= 2
         self.links.recv(self.far.at[z], self.r_far + z)
-        piece = self.piece(jnp.where(z < 2, self.col_y, self.col_x), z)
+        piece = self.piece(jnp.where(to_y, self.col_y, self.col_x), z)
         self.add(piece, (piece, self.far.at[z]))
-        self.side(z, False)
+        self.side(z, jnp.logical_not(to_y), self.s_relay)
 
     def plane(self, z):
-        self.links.recv(self.cxy.at[z], self.rxy + z)
-        self.links.recv(self.cxy.at[4 + z], self.rxy + 4 + z)
+        self.links.recv(self.cxy.at[pl.ds(0, 2)], self.r_plane + z)
         self.add(self.zb.at[z], (self.piece(self.col, z), self.cxy.at[z], self.cxy.at[4 + z]))
 
     def z_first(self):
         here = self.here
         for i, z in enumerate((here.near, here.cross)):
-            self.links.send(self.zb.at[z], self.zr.at[i], self.sz + i, self.rz + i, (here.b, here.near))
+            self.links.send(self.zb.at[z], self.zr.at[i], self.sz, self.rz + i, (here.b, here.near))
 
     def z_second(self):
         here = self.here
         self.links.recv(self.zr.at[1], self.rz + 1)
         piece = self.zb.at[here.far]
         self.add(piece, (piece, self.zr.at[1]))
-        self.links.send(piece, self.zr.at[2], self.sz + 2, self.rz + 2, (here.b, here.far))
-
-    def z_direct(self, z):
-        here = self.here
-        self.links.send(self.zb.at[z], self.zr.at[here.z], self.sz + z, self.rz + here.z, (here.b, z))
-
-    def z_last(self, direct=False):
+        self.links.send(piece, self.zr.at[2], self.sz, self.rz + 2, (here.b, here.far))
+
+    def z_last(self):
         links, here = self.links, self.here
-        own = self.zb.at[here.z]
-        if direct:
-            others = (here.near, here.cross, here.far)
-        else:
-            others = (0, 2)
-        for z in others:
-            links.recv(self.zr.at[z], self.rz + z)
-        self.add(self.fin, [own] + [self.zr.at[z] for z in others])
+        links.recv(self.zr.at[0], self.rz)
+        links.recv(self.zr.at[2], self.rz + 2)
+        self.add(self.fin, [self.zb.at[here.z], self.zr.at[0], self.zr.at[2]])
         if by_column(self.kind):
             links.send(self.fin.at[1 - here.c], self.last, self.s_end, self.r_end, here.sib)
         else:
@@ -725,15 +764,7 @@
     def finish(self, out):
         links, here, kind = self.links, self.here, self.kind
         c = here.c
-        if kind == QKV:
-            for j in range(3):
-                at = pl.multiple_of(DM * j + HALF * c, 128)
-                out[:, pl.ds(at, HALF)] = self.fin[c, :, HALF * j : HALF * (j + 1)]
-            links.recv(self.last, self.r_end)
-            for j in range(3):
-                at = pl.multiple_of(DM * j + HALF * (1 - c), 128)
-                out[:, pl.ds(at, HALF)] = self.last[:, HALF * j : HALF * (j + 1)]
-        elif kind == UP:
+        if by_column(kind):
             out[:, pl.ds(pl.multiple_of(UP_N * c, 128), UP_N)] = self.fin[c]
             links.recv(self.last, self.r_end)
             out[:, pl.ds(pl.multiple_of(UP_N * (1 - c), 128), UP_N)] = self.last[...]
@@ -748,6 +779,63 @@
 
             when(here.stays, keep)
             when(here.moves, take)
+
+
+class PairScatter:
+    def __init__(self, links, here, kind, refs):
+        self.links, self.here, self.kind = links, here, kind
+        self.grad, self.cy, self.zb, self.zr, self.fin, self.last = refs
+        self.sy, self.ry = links.alloc(), links.alloc(4)
+        self.sz, self.rz = links.alloc(), links.alloc(3)
+        self.s_end, self.r_end = links.alloc(), links.alloc()
+        links.drain(self.cy, self.sy)
+        links.drain(self.zr.at[pl.ds(0, 3)], self.sz)
+        links.drain(self.last.at[pl.ds(0, 3)], self.s_end)
+
+    def add(self, dst, terms):
+        add_blocks(dst, terms, [(i, j) for i in range(2) for j in range(2)])
+
+    def send(self, z):
+        here = self.here
+        self.links.send(self.grad.at[1 - here.y, :, :, z], self.cy.at[z], self.sy, self.ry + z, here.dy)
+
+    def plane(self, z):
+        self.links.recv(self.cy.at[z], self.ry + z)
+        self.add(self.zb.at[z], (self.grad.at[self.here.y, :, :, z], self.cy.at[z]))
+
+    def z_first(self):
+        here = self.here
+        for i, z in enumerate((here.near, here.cross)):
+            self.links.send(self.zb.at[z], self.zr.at[i], self.sz, self.rz + i, (here.b, here.near))
+
+    def z_second(self):
+        here = self.here
+        self.links.recv(self.zr.at[1], self.rz + 1)
+        piece = self.zb.at[here.far]
+        self.add(piece, (piece, self.zr.at[1]))
+        self.links.send(piece, self.zr.at[2], self.sz, self.rz + 2, (here.b, here.far))
+
+    def z_last(self):
+        links, here = self.links, self.here
+        links.recv(self.zr.at[0], self.rz)
+        links.recv(self.zr.at[2], self.rz + 2)
+        self.add(self.fin, [self.zb.at[here.z], self.zr.at[0], self.zr.at[2]])
+        x, c = here.x, here.c
+        slot = self.last.at[here.group]
+        links.send(self.fin.at[1 - x, c], slot, self.s_end, self.r_end, here.dx)
+        links.send(self.fin.at[1 - x, 1 - c], slot, self.s_end, self.r_end, here.dx_other)
+        links.send(self.fin.at[x, 1 - c], slot, self.s_end, self.r_end, here.sib)
+
+    def finish(self, out):
+        self.last[self.here.group] = self.fin[self.here.x, self.here.c]
+        self.links.recv(self.last.at[pl.ds(0, 3)], self.r_end)
+        for group in range(4):
+            if self.kind == Q:
+                out[:, GROUP * group : GROUP * (group + 1)] = self.last[group]
+            else:
+                for i in range(2):
+                    at = DM * (i + 1) + GROUP * group
+                    out[:, at : at + GROUP] = self.last[group, :, GROUP * i : GROUP * (i + 1)]
 
 
 def dot(a, b):
@@ -804,11 +892,13 @@
 
 
 SCRATCH = dict(
+    w_rows=((24, 3 * DM), BF16),
+    w_parts=((4, 24, 3 * GROUP), BF16),
     vecs=((8, 128), F32),
     cot=((2, TOK, DM), BF16),
     b_out=((2, TOK, DM), F32),
     b_tok=((2, TOK, DM), F32),
-    b_qkv=((24, 2 * QKV_N), F32),
+    b_qkv=((24, 3 * DM), F32),
     b_wout=((24, DM), F32),
     b_up=((24, FF), F32),
     b_down=((96, DM), F32),
@@ -816,7 +906,7 @@
     vec_all=((32, 8, 128), F32),
     vec_rows=((8, DM), F32),
     up_row=((1, UP_N), F32),
-    x_chip=((2, 2, TOK, DM), BF16),
+    x_pair=((2, 2, 2, TOK, DM), BF16),
     fl_chip=((2, 2, TOK, DM), BF16),
     gf_chip=((2, 2, TOK, DM), BF16),
     ga_chip=((2, 2, TOK, DM), BF16),
@@ -824,9 +914,12 @@
     back0=((2, TOK, DM), F32),
     back1=((2, TOK, DM), F32),
     back2=((2, TOK, DM), F32),
-    back3=((2, TOK, DM), F32),
-    send_q=((12, 192, 128), BF16),
-    qkv_t=((192, SEQ), BF16),
+    tok_part=((2, 2, 2, TOK, DM), F32),
+    tok_back=((2, 2, TOK, DM), F32),
+    tok_send=((2, TOK, DM), BF16),
+    tok_last=((2, TOK, DM), BF16),
+    send_q=((PAIRS, GROUP, 256), BF16),
+    qkv_t=((GROUP, SEQ), BF16),
     k_rows=((SEQ, HD), BF16),
     v_rows=((SEQ, HD), BF16),
     q_rows=((SEQ, HD), BF16),
@@ -845,8 +938,8 @@
     corr=((1, SEQ), F32),
     ds=((CHUNK, SEQ), BF16),
     dq_t=((HD, SEQ), F32),
-    d_send=((192, SEQ), BF16),
-    d_in=((12, 192, 128), BF16),
+    d_send=((GROUP, SEQ), BF16),
+    d_in=((PAIRS, GROUP, 256), BF16),
     mixed_t=((HALF, 2 * 128), BF16),
     first=((2 * TOK, DM), F32),
     normed1=((2 * TOK, DM), F32),
@@ -856,7 +949,8 @@
     gh=((4 * TOK, UP_N), BF16),
     gh2=((2 * TOK, DM), F32),
     gh1=((2 * TOK, DM), F32),
-    gp=((4 * TOK, QKV_N), BF16),
+    gp_kv=((8 * TOK, 2 * GROUP), BF16),
+    gp_q=((8 * TOK, GROUP), BF16),
     vec_grad=((8, DM), F32),
     up_grad=((1, UP_N), F32),
     vec_send=((32, 8, 128), F32),
@@ -864,23 +958,29 @@
 )
 
 
-def kind_scratch(kind):
-    shape = SHAPES[kind]
+def sum_scratch(kind):
     piece = piece_shape(kind)
-    last = piece[1:] if by_column(kind) else piece
-    low = [shape, shape, (4,) + piece, (8,) + piece, (4,) + piece, (4,) + piece]
-    return [(s, BF16) for s in low] + [(piece, F32), (last, F32)]
+    if kind in (KV, Q):
+        low = [SHAPES[kind]] + [(4,) + piece] * 3
+        last = (4,) + piece[2:]
+    else:
+        low = [SHAPES[kind], (4,) + piece, (8,) + piece, (4,) + piece, (4,) + piece]
+        last = piece[1:] if by_column(kind) else piece
+    return [(shape, BF16) for shape in low] + [(piece, F32), (last, F32)]
+
+
+GATHERED = (QKV, OUT, UP, DOWN)
+SUMMED = (OUT, UP, DOWN, KV, Q)
+N_SEM = 180
 
 
 def all_scratch():
     shapes = list(SCRATCH.values())
-    for kind in range(4):
-        shapes += kind_scratch(kind)
+    shapes += [(SHAPES[kind], BF16) for kind in GATHERED]
+    for kind in SUMMED:
+        shapes += sum_scratch(kind)
     shapes += [((24,), BF16)] * 8 + [((96,), BF16)]
     return [pltpu.VMEM(shape, dtype) for shape, dtype in shapes] + [pltpu.SemaphoreType.DMA((N_SEM,))]
-
-
-N_SEM = 414
 
 
 def layer_kernel(
@@ -890,37 +990,39 @@
     *scratch,
 ):
     vec_in = (v0, v1, v2, v3, v4, v5, v6, v7, v8)
-    named = len(SCRATCH)
     m = SimpleNamespace(**dict(zip(SCRATCH, scratch)))
-    kinds = [scratch[named + 8 * kind : named + 8 * (kind + 1)] for kind in range(4)]
-    vec_rows_in = scratch[-10:-1]
+    at = len(SCRATCH)
+    gathered = scratch[at : at + 4]
+    at += 4
+    summed = []
+    for kind in SUMMED:
+        n = len(sum_scratch(kind))
+        summed.append(scratch[at : at + n])
+        at += n
+    vec_rows_in = scratch[at : at + 9]
     sems = scratch[-1]
     here = Place()
     links = Links(sems, here)
-    b, z, c = here.b, here.z, here.c
-    line, chip = here.line, here.chip
-    gathers = [Gather(links, here, kind, kinds[kind][0]) for kind in range(4)]
-    scatters = [Scatter(links, here, kind, kinds[kind][1:]) for kind in range(4)]
+    b, z, c, x = here.b, here.z, here.c, here.x
+    line, chip, group = here.line, here.chip, here.group
+    g_qkv = PairGather(links, here, gathered[0])
+    g_out, g_up, g_down = [Gather(links, here, kind, ref) for kind, ref in zip(GATHERED[1:], gathered[1:])]
+    s_out, s_up, s_down = [Scatter(links, here, kind, refs) for kind, refs in zip(SUMMED[:3], summed[:3])]
+    s_kv, s_q = [PairScatter(links, here, kind, refs) for kind, refs in zip(SUMMED[3:], summed[3:])]
+    ahead = (g_out, g_up)
 
     def peer(d):
         other = lax.rem(line + d, 32)
         return (lax.div(other, 4), lax.rem(other, 4))
 
-    g_qkv, g_out, g_up, g_down = gathers
-    x_chip = m.x_chip
-
-    def third(j, which):
-        return w_qkv.at[:, pl.ds(pl.multiple_of(DM * j + HALF * which, 128), HALF)]
+    x_pair = m.x_pair
 
     def up_part(which):
         return w_up.at[:, pl.ds(pl.multiple_of(UP_N * which, 128), UP_N)]
 
-    def slot_part(j):
-        return g_qkv.ref.at[g_qkv.col, c, z, :, pl.ds(HALF * j, HALF)]
-
+    qkv_wait = links.local(w_qkv, m.w_rows)
     vec_waits = [links.local(src, dst) for src, dst in zip(vec_in, vec_rows_in)]
-    qkv_waits = [links.local(third(j, c), slot_part(j)) for j in range(3)]
-    x_wait = links.local(tokens, x_chip.at[:, c])
+    x_wait = links.local(tokens, x_pair.at[:, x, c])
     up_wait = links.local(up_part(c), g_up.ref.at[g_up.col, c, z])
     row_waits = [
         links.local(shard, gather.ref.at[gather.col, z], here.stays)
@@ -934,6 +1036,11 @@
     for j in range(8):
         m.vecs[j : j + 1, 0:24] = vec_rows_in[j][...].astype(F32).reshape(1, 24)
     m.vecs[0:1, 32:128] = vec_rows_in[8][...].astype(F32).reshape(1, 96)
+    qkv_wait()
+    for k in range(4):
+        for j in range(3):
+            block = m.w_rows[:, DM * j + GROUP * k : DM * j + GROUP * (k + 1)]
+            m.w_parts[k, :, GROUP * j : GROUP * (j + 1)] = block
 
     barrier = pltpu.get_barrier_semaphore()
 
@@ -944,15 +1051,23 @@
     lax.fori_loop(1, 32, greet, 0)
     pl.semaphore_wait(barrier, 31)
 
-    q_sem = links.alloc(3)
-    for j in range(3):
-        links.send(third(j, 1 - c), slot_part(j), q_sem + j, g_qkv.r0, here.sib)
-    x_sem = links.alloc(2)
-    links.send(tokens, x_chip.at[:, c], x_sem, x_sem + 1, here.sib)
-    links.send(up_part(1 - c), g_up.ref.at[g_up.col, c, z], g_up.s0, g_up.r0, here.sib)
+    slot = g_qkv.ref.at[here.y, x, c, z]
+    links.send(m.w_parts.at[2 * c + 1 - x], slot, g_qkv.s0, g_qkv.r0, here.dx)
+    links.send(m.w_parts.at[2 * (1 - c) + 1 - x], slot, g_qkv.s0, g_qkv.r0, here.dx_other)
+    links.send(m.w_parts.at[2 * (1 - c) + x], slot, g_qkv.s0, g_qkv.r0, here.sib)
+    x_sem = links.alloc(6)
+    own_x = x_pair.at[:, x, c]
+    links.send(tokens, own_x, x_sem, x_sem + 1, here.dx)
+    links.send(tokens, own_x, x_sem + 2, x_sem + 3, here.sib)
+    links.drain(own_x, x_sem)
+    links.drain(own_x, x_sem + 2)
+    up_slot = g_up.ref.at[g_up.col, c, z]
+    links.send(up_part(1 - c), up_slot, g_up.s0, g_up.r0, here.sib)
+    links.drain(up_slot, g_up.s0)
     for gather, shard in ((g_out, w_out), (g_down, w_down)):
-        slot = gather.ref.at[2 * here.x + c, z]
+        slot = gather.ref.at[2 * x + c, z]
         links.send(shard, slot, gather.s0, gather.r0, here.swap, here.moves)
+        links.drain(slot, gather.s0, here.moves)
     vec_sem = links.alloc(4)
     vec_all = m.vec_all
 
@@ -965,19 +1080,23 @@
 
     lax.fori_loop(1, 32, vec_start, 0)
     vec_all[line] = m.vecs[...]
-    for wait in (*qkv_waits, x_wait, up_wait, *row_waits, cot_wait):
+    g_qkv.ref[here.y, x, c, z] = m.w_parts[group]
+    for wait in (x_wait, up_wait, *row_waits, cot_wait):
         wait()
 
+    g_qkv.first_wait()
     g_qkv.own_z()
-    g_qkv.own_plane()
-    rest = (g_out, g_up, g_down)
+    g_qkv.spread(z)
+    for gather in ahead:
+        gather.first_wait()
+        gather.own_plane()
 
     def documents():
         def position(n):
-            q_part = lax.shift_left(lax.shift_right_logical(n, 9), 9)
-            core_part = lax.shift_left(jnp.bitwise_and(lax.shift_right_logical(n, 6), 1), 8)
-            z_part = lax.shift_left(jnp.bitwise_and(lax.shift_right_logical(n, 7), 3), 6)
-            return q_part + core_part + z_part + jnp.bitwise_and(n, 63)
+            z_part = lax.shift_left(jnp.bitwise_and(lax.shift_right_logical(n, 8), 3), 6)
+            xc_part = lax.shift_left(jnp.bitwise_and(lax.shift_right_logical(n, 6), 3), 8)
+            y_part = lax.shift_left(lax.shift_right_logical(n, 10), 10)
+            return y_part + xc_part + z_part + jnp.bitwise_and(n, 63)
 
         def doc_of(n):
             place = position(n)
@@ -989,22 +1108,25 @@
         m.query_doc[...] = doc_of(iota((1, SEQ), 1))
 
         def rows(i, carry):
-            at = pl.multiple_of(i * 256, 256)
-            m.key_doc[pl.ds(at, 256), :] = doc_of(iota((256, 128), 0) + i * 256)
+            start = pl.multiple_of(i * 256, 256)
+            m.key_doc[pl.ds(start, 256), :] = doc_of(iota((256, 128), 0) + i * 256)
             return carry
 
         lax.fori_loop(0, SEQ // 256, rows, 0)
 
     when(here.active, documents)
 
-    g_qkv.relay(z)
+    other_x = x_pair.at[:, 1 - x, c]
+    links.recv(other_x, x_sem + 1)
+    links.send(other_x, other_x, x_sem + 4, x_sem + 5, here.sib)
+    links.drain(other_x, x_sem + 4)
     g_qkv.land(here.far)
     g_qkv.hop()
     g_qkv.spread(here.far)
-    for gather in rest[:2]:
+    for gather in ahead:
         gather.own_z()
     many = vec_all.at[pl.ds(0, 31)]
-    links.make(many, many, vec_sem, vec_sem + 1, here.sib).wait_send()
+    links.sent(many, vec_sem)
     links.recv(many, vec_sem + 1)
     spread = dot(vec_all[...].reshape(256, 128).astype(BF16), select_24()).reshape(32, 8, DM)
     m.vec_rows[...] = jnp.sum(jnp.where(owner_24(32), spread, 0.0), axis=0)
@@ -1014,105 +1136,115 @@
     def vector(j):
         return m.vec_rows[j : j + 1, :]
 
-    def vector_half(j):
-        return m.vec_rows[j : j + 1, pl.ds(pl.multiple_of(HALF * c, 128), HALF)]
+    def vector_group(j):
+        total = jnp.zeros((1, GROUP), F32)
+        for k in range(4):
+            total = total + jnp.where(group == k, m.vec_rows[j : j + 1, GROUP * k : GROUP * (k + 1)], 0.0)
+        return total
 
     g_qkv.land(here.near)
     g_qkv.spread(here.near)
-    g_qkv.relay(here.far)
-    for gather in rest[:2]:
-        gather.own_plane()
+    for gather in ahead:
+        gather.relay(z)
     g_qkv.land(here.cross)
     g_qkv.spread(here.cross)
-    g_qkv.relay(here.near)
-    g_qkv.relay(here.cross)
-    for gather in rest[:2]:
+    for gather in ahead:
         gather.land(here.far)
         gather.hop()
-    links.recv(x_chip.at[:, 1 - c], x_sem + 1)
+        gather.spread(here.far)
+    links.recv(x_pair.at[:, x, 1 - c], x_sem + 3)
+    links.recv(x_pair.at[:, 1 - x, 1 - c], x_sem + 5)
     g_qkv.done()
 
-    def weight_qkv(j):
-        return g_qkv.ref[:, :, :, :, HALF * j : HALF * (j + 1)].reshape(DM, HALF)
+    def weight_qkv():
+        return g_qkv.ref[...].reshape(DM, 3 * GROUP)
 
     def x_rows():
-        return x_chip[...].reshape(4 * TOK, DM)
+        return x_pair[...].reshape(8 * TOK, DM)
 
     send_q = m.send_q
-    for j in range(3):
-        rows = dot(x_rows(), weight_qkv(j))
-        if j == 0:
-            rows = (rows + vector_half(0)).astype(BF16) * jnp.asarray(HD ** (-0.5), BF16)
-        elif j == 1:
-            rows = rows.astype(BF16)
-        else:
-            rows = (rows + vector_half(1)).astype(BF16)
+    bias = jnp.concatenate([vector_group(0), jnp.zeros((1, GROUP), F32), vector_group(1)], axis=1)
+    for part in range(MB):
+        rows = (dot(x_pair[part].reshape(4 * TOK, DM), weight_qkv()) + bias).astype(BF16)
         turned = rows.T
-        for part in range(MB):
-            piece = turned[:, 128 * part : 128 * (part + 1)].reshape(6, HD, 128)
-            send_q[6 * part : 6 * part + 6, HD * j : HD * (j + 1), :] = piece
+        for i in range(3):
+            for j in range(3):
+                block = turned[GROUP * j + HD * i : GROUP * j + HD * (i + 1), :]
+                if j == 0:
+                    block = block * jnp.asarray(HD ** (-0.5), BF16)
+                send_q[3 * part + i, HD * j : HD * (j + 1), :] = block
 
     chip_lanes = pl.ds(pl.multiple_of(chip * 128, 128), 128)
-
-    def to_pairs(src, dst_of, rows):
-        s, r, local = links.alloc(12), links.alloc(), links.alloc()
-        for pair in range(12):
-            q_to, z_to = pair_place(pair)
-            mine = jnp.logical_and(here.q == q_to, z == z_to)
-            links.send(src.at[pair], dst_of(chip_lanes), s + pair, r, (2 * q_to + c, z_to), jnp.logical_not(mine))
-
-        def own():
-            copy = pltpu.make_async_copy(src.at[here.pair], dst_of(chip_lanes), sems.at[local])
-            copy.start()
-            copy.wait()
-
-        when(here.active, own)
-        return lambda: links.recv(dst_of(pl.ds(0, 15 * 128)), r, here.active)
-
-    class ToChips:
-        def __init__(self, src_of, dst_of, own):
-            self.src_of, self.dst_of, self.own = src_of, dst_of, own
-            self.s, self.r = links.alloc(16), links.alloc()
+    seat_lanes = pl.ds(pl.multiple_of(here.seat * 256, 256), 256)
+    idle = jnp.logical_not(here.active)
+
+    def seat_dev(y_to, z_to, x_to):
+        return (4 * y_to + 2 * x_to + c, z_to)
+
+    qkv_t = m.qkv_t
+    q_sem = links.alloc(3)
+    for pair in range(PAIRS):
+        mine = both(here.active, here.pair == pair)
+        dev = seat_dev(*SEATS[pair], x)
+        links.send(send_q.at[pair], qkv_t.at[:, seat_lanes], q_sem, q_sem + 1, dev, jnp.logical_not(mine))
+    links.drain(send_q.at[pl.ds(0, PAIRS - 1)], q_sem, here.active)
+    links.drain(send_q, q_sem, idle)
+
+    def own_q():
+        qkv_t[:, seat_lanes] = send_q[here.pair]
+
+    when(here.active, own_q)
+
+    class ToSeats:
+        def __init__(self, src_of, dst_of, slot, slots, seats, own):
+            self.src_of, self.dst_of, self.slot, self.slots = src_of, dst_of, slot, slots
+            self.seats, self.own = seats, own
+            self.s, self.r = links.alloc(), links.alloc()
+            self.width = SEQ // seats
 
         def start(self, other):
-            src, dst = self.src_of(pl.ds(pl.multiple_of(128 * other, 128), 128)), self.dst_of(here.pair)
-            dev = (2 * lax.div(other, 4) + c, lax.rem(other, 4))
-            links.send(src, dst, self.s + other, self.r, dev, chip != other, keep=False)
+            start = pl.multiple_of(self.width * other, self.width)
+            src, dst = self.src_of(pl.ds(start, self.width)), self.dst_of(self.slot)
+            if self.seats == 16:
+                place, x_to, mine = lax.div(other, 2), lax.rem(other, 2), chip
+            else:
+                place, x_to, mine = other, x, here.seat
+            dev = seat_dev(lax.div(place, 4), lax.rem(place, 4), x_to)
+            links.send(src, dst, self.s, self.r, dev, mine != other)
 
         def finish(self):
-            for other in range(16):
-                src, dst = self.src_of(pl.ds(128 * other, 128)), self.dst_of(here.pair)
-                links.pending.append((both(here.active, chip != other), src, dst, self.s + other, self.r, here.sib))
+            links.drain(self.src_of(pl.ds(0, SEQ - self.width)), self.s, here.active)
             when(here.active, self.own)
 
         def wait(self):
-            links.recv(self.dst_of(pl.ds(0, 11)), self.r, here.active)
-            links.recv(self.dst_of(pl.ds(0, 12)), self.r, jnp.logical_not(here.active))
-
-    qkv_t = m.qkv_t
-    wait_q = to_pairs(send_q, lambda lanes: qkv_t.at[:, lanes], 192)
-    for gather in rest[:2]:
-        gather.spread(here.far)
-    for gather in rest[:2]:
-        gather.relay(z)
-    for gather in rest[:2]:
+            links.recv(self.dst_of(pl.ds(0, self.slots - 1)), self.r, here.active)
+            links.recv(self.dst_of(pl.ds(0, self.slots)), self.r, idle)
+
+    g_down.first_wait()
+    g_down.own_plane()
+    g_down.own_z()
+    for gather in ahead:
         gather.land(here.near)
         gather.spread(here.near)
-    for gather in rest[:2]:
+    for gather in ahead:
         gather.relay(here.far)
-    wait_q()
-    g_down.own_z()
-    for gather in rest[:2]:
+    for gather in ahead:
         gather.land(here.cross)
         gather.spread(here.cross)
-    g_down.own_plane()
+    links.recv(qkv_t.at[:, pl.ds(0, SEQ - 256)], q_sem + 1, here.active)
+    for gather in ahead:
+        gather.relay(here.near)
+    g_down.relay(z)
+
+    weights = m.weights
+    mix_slot = 6 * here.part + 3 * x + here.pair - 3 * here.part
 
     def own_mix():
-        m.mix_in[here.pair] = m.att_send[:, chip_lanes]
-
-    mix = ToChips(lambda lanes: m.att_send.at[:, lanes], lambda pair: m.mix_in.at[pair], own_mix)
-
-    weights = m.weights
+        m.mix_in[mix_slot] = m.att_send[:, chip_lanes]
+
+    mix = ToSeats(
+        lambda lanes: m.att_send.at[:, lanes], lambda slot: m.mix_in.at[slot], mix_slot, 12, 16, own_mix
+    )
 
     def turn_keys():
         m.k_rows[...] = qkv_t[HD : 2 * HD, :].T
@@ -1149,50 +1281,50 @@
         mix.start(2 * i)
         mix.start(2 * i + 1)
 
-    def attend_some(first, last):
+    def some(body, first, last):
         def run():
             def one(i, carry):
-                attend(i)
+                body(i)
                 return carry
 
             lax.fori_loop(first, last, one, 0)
 
         when(here.active, run)
 
-    attend_some(0, 2)
-    for gather in rest[:2]:
-        gather.relay(here.near)
+    some(attend, 0, 2)
+    for gather in ahead:
+        gather.relay(here.cross)
     g_down.land(here.far)
     g_down.hop()
     g_down.spread(here.far)
-    attend_some(2, 5)
-    for gather in rest[:2]:
-        gather.relay(here.cross)
+    some(attend, 2, 5)
     g_down.land(here.near)
     g_down.spread(here.near)
-    g_down.relay(z)
-    attend_some(5, 8)
-
+    some(attend, 5, 7)
+    g_down.relay(here.far)
+    some(attend, 7, 8)
     g_down.land(here.cross)
     g_down.spread(here.cross)
-    g_down.relay(here.far)
     mix.finish()
     mix.wait()
     g_out.done()
+    g_down.relay(here.near)
+
     def share(buf, values):
-        at = links.alloc(2)
+        sem = links.alloc(2)
         buf[:, c] = values.reshape(MB, TOK, DM)
-        links.send(buf.at[:, c], buf.at[:, c], at, at + 1, here.sib)
-        links.recv(buf.at[:, 1 - c], at + 1)
+        links.send(buf.at[:, c], buf.at[:, c], sem, sem + 1, here.sib)
+        links.drain(buf.at[:, c], sem)
+        links.recv(buf.at[:, 1 - c], sem + 1)
 
     def combine(values, back):
-        at = links.alloc(2)
+        sem = links.alloc(2)
         partial = m.partial
         partial[...] = values.reshape(MB, 2, TOK, DM)
-        links.send(partial.at[:, 1 - c], back, at, at + 1, here.sib, keep=False)
-        links.recv(back, at + 1)
+        links.send(partial.at[:, 1 - c], back, sem, sem + 1, here.sib)
+        links.recv(back, sem + 1)
         total = partial[:, c].reshape(2 * TOK, DM) + back[...].reshape(2 * TOK, DM)
-        links.sent(partial.at[:, 1 - c], back, at, at + 1, here.sib)
+        links.sent(partial.at[:, 1 - c], sem)
         return total
 
     def norm_rows(values, gain, shift):
@@ -1221,15 +1353,13 @@
         return g_out.ref[...].reshape(HALF, DM)
 
     attn = combine(dot(mixed, weight_out()), m.back0) + vector(2)
-    first, normed_one, inverse_one = norm_rows(
-        x_chip[:, c].reshape(2 * TOK, DM).astype(F32) + attn, vector(3), vector(4)
-    )
+    own_tokens = x_pair[:, x, c].reshape(2 * TOK, DM).astype(F32)
+    first, normed_one, inverse_one = norm_rows(own_tokens + attn, vector(3), vector(4))
     m.first[...] = first
     m.normed1[...] = normed_one
     m.inv1[...] = inverse_one
     share(m.fl_chip, first.astype(BF16))
 
-    g_down.relay(here.near)
     g_up.done()
     def fl_rows():
         return m.fl_chip[...].reshape(4 * TOK, DM)
@@ -1258,6 +1388,7 @@
     m.b_out[...] = result.reshape(MB, TOK, DM)
     links.put(m.b_out, o_out)
 
+    targets = (here.near, here.cross, here.far, z)
     vec_grad = m.vec_grad
     grad_result = m.cot[...].reshape(2 * TOK, DM).astype(F32)
     vec_grad[6:7, :] = row_sum(grad_result * normed_two)
@@ -1271,20 +1402,18 @@
     def gf_rows():
         return m.gf_chip[...].reshape(4 * TOK, DM)
 
-    s_qkv, s_out, s_up, s_down = scatters
-    targets = (here.near, here.cross, here.far, z)
     for j in range(4):
         lanes = slice(HALF * j, HALF * (j + 1))
         s_down.grad[j] = dot_tn(m.active[:, lanes], gf_rows()).astype(BF16).reshape(4, 96, DM)
     for t in targets:
         s_down.send(t)
+    grad_first = None
     for j in range(4):
         lanes = slice(HALF * j, HALF * (j + 1))
         grad_active = dot_nt(gf_rows(), weight_down(j))
         grad_hidden = (grad_active * m.slope[:, lanes]).astype(BF16)
         m.gh[:, lanes] = grad_hidden
         m.up_grad[:, lanes] = row_sum(grad_hidden.astype(F32))
-    grad_first = None
     for j in range(4):
         lanes = slice(HALF * j, HALF * (j + 1))
         term = dot_nt(m.gh[:, lanes], weight_up(j))
@@ -1306,34 +1435,50 @@
     for part in range(MB):
         m.g_send[6 * part : 6 * part + 6] = turned[:, 128 * part : 128 * (part + 1)].reshape(6, HD, 128)
     g_t = m.g_t
-    wait_g = to_pairs(m.g_send, lambda lanes: g_t.at[:, lanes], HD)
+    g_sem = links.alloc(2)
+    for slot in range(12):
+        part, head = slot // 6, slot % 6
+        pair, x_to = 3 * part + head % 3, head // 3
+        mine = both(here.active, both(here.pair == pair, x == x_to))
+        dev = seat_dev(*SEATS[pair], x_to)
+        links.send(m.g_send.at[slot], g_t.at[:, chip_lanes], g_sem, g_sem + 1, dev, jnp.logical_not(mine))
+    links.drain(m.g_send.at[pl.ds(0, 11)], g_sem, here.active)
+    links.drain(m.g_send, g_sem, idle)
+
+    def own_g():
+        g_t[:, chip_lanes] = m.g_send[mix_slot]
+
+    when(here.active, own_g)
     for j in range(4):
         lanes = slice(HALF * j, HALF * (j + 1))
         s_up.grad[:, :, :, :, lanes] = (
             dot_tn(fl_rows(), m.gh[:, lanes]).astype(BF16).reshape(4, 2, 4, 24, HALF)
         )
+    s_out.grad[...] = dot(mixed_t[...], ga_rows()).astype(BF16).reshape(SHAPES[OUT])
+    for t in targets:
+        s_down.relay(t)
     for t in targets:
         s_up.send(t)
-    s_out.grad[...] = dot(mixed_t[...], ga_rows()).astype(BF16).reshape(SHAPES[OUT])
     for t in targets:
         s_out.send(t)
-    for t in targets:
-        s_down.relay(t)
-    wait_g()
-
-    d_in = m.d_in
+    links.recv(g_t.at[:, pl.ds(0, SEQ - 128)], g_sem + 1, here.active)
+
+    d_send, d_in = m.d_send, m.d_in
 
     def own_kv():
-        d_in[here.pair, HD : 3 * HD, :] = d_send[HD : 3 * HD, chip_lanes]
-
-    def own_q():
-        d_in[here.pair, 0:HD, :] = d_send[0:HD, chip_lanes]
-
-    grad_kv = ToChips(
-        lambda lanes: d_send.at[pl.ds(HD, 2 * HD), lanes], lambda pair: d_in.at[pair, pl.ds(HD, 2 * HD)], own_kv
+        d_in[here.pair, HD : 3 * HD, :] = d_send[HD : 3 * HD, seat_lanes]
+
+    def own_dq():
+        d_in[here.pair, 0:HD, :] = d_send[0:HD, seat_lanes]
+
+    grad_kv = ToSeats(
+        lambda lanes: d_send.at[pl.ds(HD, 2 * HD), lanes], lambda slot: d_in.at[slot, pl.ds(HD, 2 * HD)],
+        here.pair, PAIRS, 8, own_kv,
     )
-    grad_q = ToChips(lambda lanes: d_send.at[pl.ds(0, HD), lanes], lambda pair: d_in.at[pair, pl.ds(0, HD)], own_q)
-    d_send = m.d_send
+    grad_q = ToSeats(
+        lambda lanes: d_send.at[pl.ds(0, HD), lanes], lambda slot: d_in.at[slot, pl.ds(0, HD)],
+        here.pair, PAIRS, 8, own_dq,
+    )
 
     def turn_grads():
         grad = g_t[...].astype(F32)
@@ -1347,67 +1492,76 @@
     when(here.active, turn_grads)
 
     def back(k):
-        at = pl.ds(pl.multiple_of(k * CHUNK, CHUNK), CHUNK)
-        value = m.v_rows[at, :]
+        keys = pl.ds(pl.multiple_of(k * CHUNK, CHUNK), CHUNK)
+        value = m.v_rows[keys, :]
         for i in range(4):
             lanes = slice(512 * i, 512 * (i + 1))
             grad_weights = dot(value, m.gn_t[:, lanes])
-            grown = weights[at, lanes].astype(F32)
+            grown = weights[keys, lanes].astype(F32)
             m.ds[:, lanes] = (grown * (grad_weights - m.corr[:, lanes])).astype(BF16)
         ds = m.ds
-        d_send[HD : 2 * HD, at] = dot(ds[...], m.q_rows[...]).T.astype(BF16)
-        d_send[2 * HD : 3 * HD, at] = dot(weights[at, :], m.g_rows[...]).T.astype(BF16)
-        grad_kv.start(2 * k)
-        grad_kv.start(2 * k + 1)
-        m.dq_t[...] += dot(qkv_t[HD : 2 * HD, at], ds[...])
-
-    def back_some(first, last):
-        def run():
-            def one(i, carry):
-                back(i)
-                return carry
-
-            lax.fori_loop(first, last, one, 0)
-
-        when(here.active, run)
-
-    back_some(0, 4)
-    back_some(4, 8)
+        d_send[HD : 2 * HD, keys] = dot(ds[...], m.q_rows[...]).T.astype(BF16)
+        d_send[2 * HD : 3 * HD, keys] = dot(weights[keys, :], m.g_rows[...]).T.astype(BF16)
+        grad_kv.start(k)
+        m.dq_t[...] += dot(qkv_t[HD : 2 * HD, keys], ds[...])
+
+    some(back, 0, 8)
 
     def last_query():
         d_send[0:HD, :] = (m.dq_t[...] * (HD ** (-0.5))).astype(BF16)
-        for other in range(16):
+        for other in range(8):
             grad_q.start(other)
 
     when(here.active, last_query)
     grad_kv.finish()
     grad_q.finish()
     for t in targets:
+        s_down.plane(t)
+        if t is here.cross:
+            s_down.z_first()
+    for t in targets:
         s_up.relay(t)
     for t in targets:
         s_out.relay(t)
+    grad_kv.wait()
+    s_down.z_second()
+    gp_kv, gp_q = m.gp_kv, m.gp_q
+    for part in range(MB):
+        heads = slice(3 * part, 3 * part + 3)
+        rows = [d_in[heads, HD * j : HD * (j + 1), :].reshape(GROUP, 256) for j in (1, 2)]
+        gp_kv[256 * part : 256 * (part + 1), :] = jnp.concatenate(rows, axis=0).T
+    s_kv.grad[...] = dot_tn(x_rows(), gp_kv[...]).astype(BF16).reshape(SHAPES[KV])
     for t in targets:
-        s_down.plane(t)
+        s_kv.send(t)
+    for t in targets:
+        s_up.plane(t)
         if t is here.cross:
-            s_down.z_first()
-    grad_kv.wait()
+            s_up.z_first()
     grad_q.wait()
-    s_down.z_second()
-    gp = m.gp
     for part in range(MB):
-        for j in range(3):
-            piece = d_in[6 * part : 6 * part + 6, HD * j : HD * (j + 1), :].reshape(HALF, 128)
-            gp[128 * part : 128 * (part + 1), HALF * j : HALF * (j + 1)] = piece.T
-    own_half = pl.ds(pl.multiple_of(HALF * c, 128), HALF)
-    for j in range(3):
-        lanes = slice(HALF * j, HALF * (j + 1))
-        s_qkv.grad[:, :, :, :, lanes] = (
-            dot_tn(x_rows(), gp[:, lanes]).astype(BF16).reshape(4, 2, 4, 24, HALF)
-        )
+        gp_q[256 * part : 256 * (part + 1), :] = d_in[3 * part : 3 * part + 3, 0:HD, :].reshape(GROUP, 256).T
+    s_q.grad[...] = dot_tn(x_rows(), gp_q[...]).astype(BF16).reshape(SHAPES[Q])
     for t in targets:
-        s_qkv.send(t)
-    vec_grad[0:1, own_half] = row_sum(gp[:, 0:HALF].astype(F32))
-    vec_grad[1:2, own_half] = row_sum(gp[:, 2 * HALF : 3 * HALF].astype(F32))
+        s_q.send(t)
+    all_weights = weight_qkv()
+    t_sem = links.alloc(4)
+    for part in range(MB):
+        rows = slice(256 * part, 256 * (part + 1))
+        terms = dot_nt(gp_q[rows, :], all_weights[:, 0:GROUP]) + dot_nt(gp_kv[rows, :], all_weights[:, GROUP:])
+        m.tok_part[part] = terms.reshape(2, 2, TOK, DM)
+    links.send(m.tok_part.at[:, :, 1 - c], m.tok_back, t_sem, t_sem + 1, here.sib)
+    links.drain(m.tok_back, t_sem)
+    sum_q = row_sum(gp_q[...].astype(F32))
+    sum_v = row_sum(gp_kv[:, GROUP:].astype(F32))
+    for k in range(4):
+        lanes = slice(GROUP * k, GROUP * (k + 1))
+        vec_grad[0:1, lanes] = jnp.where(group == k, sum_q, 0.0)
+        vec_grad[1:2, lanes] = jnp.where(group == k, sum_v, 0.0)
+    links.recv(m.tok_back, t_sem + 1)
+    for part in range(MB):
+        m.tok_send[part] = (m.tok_part[part, 1 - x, c] + m.tok_back[part, 1 - x]).astype(BF16)
+    links.send(m.tok_send, m.tok_last, t_sem + 2, t_sem + 3, here.dx)
+    links.drain(m.tok_send, t_sem + 2)
 
     vec_send, vec_recv = m.vec_send, m.vec_recv
     spread = jnp.where(owner_24(32), vec_grad[...][None], 0.0).reshape(256, DM)
@@ -1416,54 +1570,55 @@
     own_lines = pl.ds(16 * c, 16)
     vec_send[own_lines, 0, :] = vec_send[own_lines, 0, :] + exact_nt(spread, select_96())
 
-    def grad_copy(d):
+    def grad_start(d, carry):
         other = lax.rem(line + d, 32)
-        return links.make(vec_send.at[other], vec_recv.at[line], vec_sem + 2, vec_sem + 3, peer(d))
-
-    def grad_start(d, carry):
-        grad_copy(d).start()
+        links.make(vec_send.at[other], vec_recv.at[line], vec_sem + 2, vec_sem + 3, peer(d)).start()
         return carry
 
     lax.fori_loop(1, 32, grad_start, 0)
     vec_recv[line] = vec_send[line]
 
-    grad_tokens = None
-    for j in range(3):
-        term = dot_nt(gp[:, HALF * j : HALF * (j + 1)], weight_qkv(j))
-        grad_tokens = term if grad_tokens is None else grad_tokens + term
-    m.b_tok[...] = (m.gh1[...] + combine(grad_tokens, m.back3)).reshape(MB, TOK, DM)
+    for t in targets:
+        s_out.plane(t)
+        if t is here.cross:
+            s_out.z_first()
+    for t in targets:
+        s_kv.plane(t)
+        if t is here.cross:
+            s_kv.z_first()
+    s_up.z_second()
+    for t in targets:
+        s_q.plane(t)
+        if t is here.cross:
+            s_q.z_first()
+    s_kv.z_second()
+    s_q.z_second()
+    s_out.z_second()
+    links.recv(m.tok_last, t_sem + 3)
+    for part in range(MB):
+        rows = slice(TOK * part, TOK * (part + 1))
+        own = m.tok_part[part, x, c] + m.tok_back[part, x]
+        m.b_tok[part] = m.gh1[rows, :] + (own + m.tok_last[part].astype(F32))
     links.put(m.b_tok, o_tok)
-
-    for scatter in (s_up, s_out):
-        for t in targets:
-            scatter.plane(t)
-            if t is here.cross:
-                scatter.z_first()
-    for t in targets:
-        s_qkv.relay(t)
-    s_up.z_second()
-    s_out.z_second()
-    for t in targets:
-        s_qkv.plane(t)
-        if t is not z:
-            s_qkv.z_direct(t)
-    for scatter in (s_down, s_up, s_out):
-        scatter.z_last()
-    for scatter, out, to in ((s_down, m.b_down, o_down), (s_up, m.b_up, o_up), (s_out, m.b_wout, o_wout)):
-        scatter.finish(out)
-        links.put(out, to)
-
     many_send, many_recv = vec_send.at[pl.ds(0, 31)], vec_recv.at[pl.ds(0, 31)]
-    links.make(many_send, many_send, vec_sem + 2, vec_sem + 3, here.sib).wait_send()
+    links.sent(many_send, vec_sem + 2)
     links.recv(many_recv, vec_sem + 3)
     m.b_vec[...] = jnp.sum(vec_recv[...], axis=0)
     links.put(m.b_vec, o_vec)
-
-    s_qkv.z_last(direct=True)
-    s_qkv.finish(m.b_qkv)
+    s_down.z_last()
+    s_down.finish(m.b_down)
+    links.put(m.b_down, o_down)
+    s_kv.z_last()
+    s_q.z_last()
+    for scatter, out, to in ((s_up, m.b_up, o_up), (s_out, m.b_wout, o_wout)):
+        scatter.z_last()
+    s_kv.finish(m.b_qkv)
+    s_q.finish(m.b_qkv)
     links.put(m.b_qkv, o_qkv)
+    for scatter, out, to in ((s_up, m.b_up, o_up), (s_out, m.b_wout, o_wout)):
+        scatter.finish(out)
+        links.put(out, to)
     links.finish()
-    assert links.count == N_SEM, links.count
 
 
 def place_kernel(*refs):

time: 188 us -> 173 us (0.920)
  Pallas kernels: 187 us -> 172 us
    pallas_call x1, Pallas kernels: 184 us -> 169 us  [fused(): pl.pallas_call(layer_kernel, name='layer', out_shape=big + [jax.ShapeDtyp...]
where the time goes in v3:
time: 173 us
  Pallas kernels  172 us (99%)
    pallas_call x1, Pallas kernels, fused(): pl.pallas_call(layer_kernel, name='layer', out_shape=big + [jax.ShapeDtyp...  169 us

profile of v3, /device:TPU:1, one launch (start us, length us, event | category | flops | bytes accessed | tf_op | source)
XLA Modules:
  0.0 172.6 jit_solution(3293499144815480771)
XLA Ops:
  0.7 169.0 %layer.1 = (f32[2,64,768]{2,1,0:T(8,128)}, f32[2,64,768]{2,1,0:T(8,128)}, f32[24,2304]{1,0:T(8,128)}, f32[24,768]{1,0:T(8,128)}, f32[24,3072]{1,0:T(8,128)}, /*index=5*/f32[96,768]{1,0:T(8,128)}, f32[8,128]{1,0:T(8,128)}) custom-call(bf16[2,64,768]{2,1,0:T(8,128)(2,1)} %tokens.1, s32[2,16]{1,0:T(2,128)} %starts.1, bf16[24,2304]{1,0:T(8,128)(2,1)} %w_qkv.1, ...), custom_call_target="tpu_custom_call" | custom-call | tf_op jit(solution)/shard_map/layer/pallas_call | solution.py:1654
  169.7 2.8 %place.1 = (f32[2,64,768]{2,1,0:T(8,128)}, f32[2,64,768]{2,1,0:T(8,128)}, f32[24,2304]{1,0:T(8,128)}, f32[24,768]{1,0:T(8,128)}, f32[24,3072]{1,0:T(8,128)}, /*i...) custom-call(f32[2,64,768]{2,1,0:T(8,128)} %get-tuple-element.37.refs, ...), custom_call_target="tpu_custom_call" | custom-call | tf_op jit(solution)/shard_map/place/pallas_call | solution.py:1665

commit v4 on v3

--- a/solution.py
+++ b/solution.py
@@ -695,6 +695,7 @@
 class Scatter:
     def __init__(self, links, here, kind, refs):
         self.links, self.here, self.kind = links, here, kind
+        self.tilt = 2
         self.grad, self.far, self.cxy, self.zb, self.zr, self.fin, self.last = refs
         self.s_first, self.s_relay, self.sz = links.alloc(), links.alloc(), links.alloc()
         self.r_far, self.r_plane, self.rz = links.alloc(4), links.alloc(4), links.alloc(3)
@@ -721,15 +722,19 @@
         slot = jnp.where(to_x, z, 4 + z)
         self.links.send(self.piece(col, z), self.cxy.at[slot], sem, self.r_plane + z, dev)
 
-    def send(self, z):
+    def send_far(self, order):
         here = self.here
-        to_x = z >= 2
-        dev = (jnp.where(to_x, here.dx[0], here.dy[0]), here.z)
-        self.links.send(self.piece(self.col_d, z), self.far.at[z], self.s_first, self.r_far + z, dev)
-        self.side(z, to_x, self.s_first)
+        for z in order:
+            to_x = z >= self.tilt
+            dev = (jnp.where(to_x, here.dx[0], here.dy[0]), here.z)
+            self.links.send(self.piece(self.col_d, z), self.far.at[z], self.s_first, self.r_far + z, dev)
+
+    def send_sides(self, order):
+        for z in order:
+            self.side(z, z >= self.tilt, self.s_first)
 
     def relay(self, z):
-        to_y = z >= 2
+        to_y = z >= self.tilt
         self.links.recv(self.far.at[z], self.r_far + z)
         piece = self.piece(jnp.where(to_y, self.col_y, self.col_x), z)
         self.add(piece, (piece, self.far.at[z]))
@@ -739,10 +744,10 @@
         self.links.recv(self.cxy.at[pl.ds(0, 2)], self.r_plane + z)
         self.add(self.zb.at[z], (self.piece(self.col, z), self.cxy.at[z], self.cxy.at[4 + z]))
 
-    def z_first(self):
+    def z_first(self, i):
         here = self.here
-        for i, z in enumerate((here.near, here.cross)):
-            self.links.send(self.zb.at[z], self.zr.at[i], self.sz, self.rz + i, (here.b, here.near))
+        z = here.cross if i else here.near
+        self.links.send(self.zb.at[z], self.zr.at[i], self.sz, self.rz + i, (here.b, here.near))
 
     def z_second(self):
         here = self.here
@@ -779,6 +784,61 @@
 
             when(here.stays, keep)
             when(here.moves, take)
+
+
+class ColumnScatter(Scatter):
+    def __init__(self, links, here, kind, refs):
+        self.links, self.here, self.kind = links, here, kind
+        self.grad, self.far, self.cxy, self.zb, self.zr, self.fin, self.last = refs
+        self.s_first, self.s_relay, self.sz = links.alloc(), links.alloc(), links.alloc()
+        self.r_far, self.r_plane, self.rz = links.alloc(4), links.alloc(4), links.alloc(3)
+        self.s_far, self.s_column = links.alloc(), links.alloc()
+        self.s_end, self.r_end = links.alloc(), links.alloc()
+        self.col, self.col_x, self.col_y, self.col_d = here.cols(kind)
+        links.drain(self.cxy.at[pl.ds(0, 7)], self.s_first)
+        links.drain(self.far.at[0], self.s_relay)
+        links.drain(self.far.at[0], self.s_far)
+        links.drain(self.far.at[pl.ds(0, 3)], self.s_column)
+        links.drain(self.zr.at[pl.ds(0, 3)], self.sz)
+        links.drain(self.last, self.s_end, None if by_column(kind) else here.moves)
+
+    def to_side(self, z, to_x, sem):
+        here = self.here
+        col, slot, dev = (self.col_x, z, here.dx) if to_x else (self.col_y, 4 + z, here.dy)
+        self.links.send(self.piece(col, z), self.cxy.at[slot], sem, self.r_plane + z, dev)
+
+    def send_sides(self, order):
+        for z in order:
+            self.to_side(z, True, self.s_first)
+            if z is not self.here.z:
+                self.to_side(z, False, self.s_first)
+
+    def column_first(self):
+        here = self.here
+        for i, z in enumerate((here.near, here.cross)):
+            self.links.send(self.piece(self.col_d, z), self.far.at[i], self.s_column, self.r_far + i, (here.b, here.near))
+
+    def column_second(self):
+        here = self.here
+        self.links.recv(self.far.at[1], self.r_far + 1)
+        piece = self.piece(self.col_d, here.far)
+        self.add(piece, (piece, self.far.at[1]))
+        self.links.send(piece, self.far.at[2], self.s_column, self.r_far + 2, (here.b, here.far))
+
+    def column_last(self):
+        here = self.here
+        self.links.recv(self.far.at[0], self.r_far)
+        self.links.recv(self.far.at[2], self.r_far + 2)
+        piece = self.piece(self.col_d, here.z)
+        self.add(piece, (piece, self.far.at[0], self.far.at[2]))
+        self.links.send(piece, self.far.at[3], self.s_far, self.r_far + 3, here.dx)
+
+    def relay_own(self):
+        here = self.here
+        self.links.recv(self.far.at[3], self.r_far + 3)
+        piece = self.piece(self.col_y, here.z)
+        self.add(piece, (piece, self.far.at[3]))
+        self.to_side(here.z, False, self.s_relay)
 
 
 class PairScatter:
@@ -803,10 +863,10 @@
         self.links.recv(self.cy.at[z], self.ry + z)
         self.add(self.zb.at[z], (self.grad.at[self.here.y, :, :, z], self.cy.at[z]))
 
-    def z_first(self):
+    def z_first(self, i):
         here = self.here
-        for i, z in enumerate((here.near, here.cross)):
-            self.links.send(self.zb.at[z], self.zr.at[i], self.sz, self.rz + i, (here.b, here.near))
+        z = here.cross if i else here.near
+        self.links.send(self.zb.at[z], self.zr.at[i], self.sz, self.rz + i, (here.b, here.near))
 
     def z_second(self):
         here = self.here
@@ -971,7 +1031,7 @@
 
 GATHERED = (QKV, OUT, UP, DOWN)
 SUMMED = (OUT, UP, DOWN, KV, Q)
-N_SEM = 180
+N_SEM = 181
 
 
 def all_scratch():
@@ -1007,7 +1067,10 @@
     line, chip, group = here.line, here.chip, here.group
     g_qkv = PairGather(links, here, gathered[0])
     g_out, g_up, g_down = [Gather(links, here, kind, ref) for kind, ref in zip(GATHERED[1:], gathered[1:])]
-    s_out, s_up, s_down = [Scatter(links, here, kind, refs) for kind, refs in zip(SUMMED[:3], summed[:3])]
+    s_out, s_up, s_down = [
+        make(links, here, kind, refs)
+        for make, kind, refs in zip((Scatter, Scatter, ColumnScatter), SUMMED[:3], summed[:3])
+    ]
     s_kv, s_q = [PairScatter(links, here, kind, refs) for kind, refs in zip(SUMMED[3:], summed[3:])]
     ahead = (g_out, g_up)
 
@@ -1162,7 +1225,15 @@
     def x_rows():
         return x_pair[...].reshape(8 * TOK, DM)
 
-    send_q = m.send_q
+    chip_lanes = pl.ds(pl.multiple_of(chip * 128, 128), 128)
+    seat_lanes = pl.ds(pl.multiple_of(here.seat * 256, 256), 256)
+    idle = jnp.logical_not(here.active)
+
+    def seat_dev(y_to, z_to, x_to):
+        return (4 * y_to + 2 * x_to + c, z_to)
+
+    send_q, qkv_t = m.send_q, m.qkv_t
+    q_sem = links.alloc(2)
     bias = jnp.concatenate([vector_group(0), jnp.zeros((1, GROUP), F32), vector_group(1)], axis=1)
     for part in range(MB):
         rows = (dot(x_pair[part].reshape(4 * TOK, DM), weight_qkv()) + bias).astype(BF16)
@@ -1173,20 +1244,11 @@
                 if j == 0:
                     block = block * jnp.asarray(HD ** (-0.5), BF16)
                 send_q[3 * part + i, HD * j : HD * (j + 1), :] = block
-
-    chip_lanes = pl.ds(pl.multiple_of(chip * 128, 128), 128)
-    seat_lanes = pl.ds(pl.multiple_of(here.seat * 256, 256), 256)
-    idle = jnp.logical_not(here.active)
-
-    def seat_dev(y_to, z_to, x_to):
-        return (4 * y_to + 2 * x_to + c, z_to)
-
-    qkv_t = m.qkv_t
-    q_sem = links.alloc(3)
-    for pair in range(PAIRS):
-        mine = both(here.active, here.pair == pair)
-        dev = seat_dev(*SEATS[pair], x)
-        links.send(send_q.at[pair], qkv_t.at[:, seat_lanes], q_sem, q_sem + 1, dev, jnp.logical_not(mine))
+            pair = 3 * part + i
+            other = jnp.logical_not(both(here.active, here.pair == pair))
+            dev = seat_dev(*SEATS[pair], x)
+            links.send(send_q.at[pair], qkv_t.at[:, seat_lanes], q_sem, q_sem + 1, dev, other)
+
     links.drain(send_q.at[pl.ds(0, PAIRS - 1)], q_sem, here.active)
     links.drain(send_q, q_sem, idle)
 
@@ -1291,24 +1353,24 @@
 
         when(here.active, run)
 
-    some(attend, 0, 2)
+    some(attend, 0, 4)
     for gather in ahead:
         gather.relay(here.cross)
     g_down.land(here.far)
     g_down.hop()
     g_down.spread(here.far)
-    some(attend, 2, 5)
     g_down.land(here.near)
     g_down.spread(here.near)
-    some(attend, 5, 7)
-    g_down.relay(here.far)
-    some(attend, 7, 8)
+    some(attend, 4, 7)
     g_down.land(here.cross)
     g_down.spread(here.cross)
+    some(attend, 7, 8)
+    g_down.relay(here.far)
+    g_down.relay(here.near)
     mix.finish()
     mix.wait()
     g_out.done()
-    g_down.relay(here.near)
+    g_down.relay(here.cross)
 
     def share(buf, values):
         sem = links.alloc(2)
@@ -1376,7 +1438,6 @@
         cdf = 0.5 * (1.0 + lax.erf(hidden * (0.5**0.5)))
         m.slope[:, lanes] = cdf + hidden * (jnp.exp(-0.5 * hidden * hidden) * 0.3989422804014327)
         m.active[:, lanes] = (hidden * cdf).astype(BF16)
-    g_down.relay(here.cross)
     g_down.done()
     ffn = None
     for j in range(4):
@@ -1405,8 +1466,8 @@
     for j in range(4):
         lanes = slice(HALF * j, HALF * (j + 1))
         s_down.grad[j] = dot_tn(m.active[:, lanes], gf_rows()).astype(BF16).reshape(4, 96, DM)
-    for t in targets:
-        s_down.send(t)
+    s_down.send_sides(targets)
+    s_down.column_first()
     grad_first = None
     for j in range(4):
         lanes = slice(HALF * j, HALF * (j + 1))
@@ -1455,12 +1516,19 @@
             dot_tn(fl_rows(), m.gh[:, lanes]).astype(BF16).reshape(4, 2, 4, 24, HALF)
         )
     s_out.grad[...] = dot(mixed_t[...], ga_rows()).astype(BF16).reshape(SHAPES[OUT])
-    for t in targets:
-        s_down.relay(t)
-    for t in targets:
-        s_up.send(t)
-    for t in targets:
-        s_out.send(t)
+    s_up.send_far(targets)
+    s_out.send_far(targets)
+    s_up.send_sides(targets)
+    s_out.send_sides(targets)
+
+    def planes(scatter, order=targets):
+        for i, t in enumerate(order):
+            scatter.plane(t)
+            if i < 2:
+                scatter.z_first(i)
+
+    s_down.column_second()
+    planes(s_down, targets[:3])
     links.recv(g_t.at[:, pl.ds(0, SEQ - 128)], g_sem + 1, here.active)
 
     d_send, d_in = m.d_send, m.d_in
@@ -1505,7 +1573,13 @@
         grad_kv.start(k)
         m.dq_t[...] += dot(qkv_t[HD : 2 * HD, keys], ds[...])
 
-    some(back, 0, 8)
+    some(back, 0, 4)
+    s_down.column_last()
+    for t in targets:
+        s_up.relay(t)
+    for t in targets:
+        s_out.relay(t)
+    some(back, 4, 8)
 
     def last_query():
         d_send[0:HD, :] = (m.dq_t[...] * (HD ** (-0.5))).astype(BF16)
@@ -1515,16 +1589,10 @@
     when(here.active, last_query)
     grad_kv.finish()
     grad_q.finish()
-    for t in targets:
-        s_down.plane(t)
-        if t is here.cross:
-            s_down.z_first()
-    for t in targets:
-        s_up.relay(t)
-    for t in targets:
-        s_out.relay(t)
+    s_down.relay_own()
+    s_down.z_second()
+    planes(s_up, targets[:2])
     grad_kv.wait()
-    s_down.z_second()
     gp_kv, gp_q = m.gp_kv, m.gp_q
     for part in range(MB):
         heads = slice(3 * part, 3 * part + 3)
@@ -1533,16 +1601,18 @@
     s_kv.grad[...] = dot_tn(x_rows(), gp_kv[...]).astype(BF16).reshape(SHAPES[KV])
     for t in targets:
         s_kv.send(t)
-    for t in targets:
+    for t in targets[2:]:
         s_up.plane(t)
-        if t is here.cross:
-            s_up.z_first()
+    planes(s_out)
+    s_down.plane(z)
     grad_q.wait()
     for part in range(MB):
         gp_q[256 * part : 256 * (part + 1), :] = d_in[3 * part : 3 * part + 3, 0:HD, :].reshape(GROUP, 256).T
     s_q.grad[...] = dot_tn(x_rows(), gp_q[...]).astype(BF16).reshape(SHAPES[Q])
     for t in targets:
         s_q.send(t)
+    planes(s_kv)
+    s_out.z_second()
     all_weights = weight_qkv()
     t_sem = links.alloc(4)
     for part in range(MB):
@@ -1551,6 +1621,7 @@
         m.tok_part[part] = terms.reshape(2, 2, TOK, DM)
     links.send(m.tok_part.at[:, :, 1 - c], m.tok_back, t_sem, t_sem + 1, here.sib)
     links.drain(m.tok_back, t_sem)
+    s_up.z_second()
     sum_q = row_sum(gp_q[...].astype(F32))
     sum_v = row_sum(gp_kv[:, GROUP:].astype(F32))
     for k in range(4):
@@ -1563,6 +1634,8 @@
     links.send(m.tok_send, m.tok_last, t_sem + 2, t_sem + 3, here.dx)
     links.drain(m.tok_send, t_sem + 2)
 
+    planes(s_q)
+    s_kv.z_second()
     vec_send, vec_recv = m.vec_send, m.vec_recv
     spread = jnp.where(owner_24(32), vec_grad[...][None], 0.0).reshape(256, DM)
     vec_send[...] = exact_nt(spread, select_24()).reshape(32, 8, 128)
@@ -1578,22 +1651,12 @@
     lax.fori_loop(1, 32, grad_start, 0)
     vec_recv[line] = vec_send[line]
 
-    for t in targets:
-        s_out.plane(t)
-        if t is here.cross:
-            s_out.z_first()
-    for t in targets:
-        s_kv.plane(t)
-        if t is here.cross:
-            s_kv.z_first()
-    s_up.z_second()
-    for t in targets:
-        s_q.plane(t)
-        if t is here.cross:
-            s_q.z_first()
-    s_kv.z_second()
     s_q.z_second()
-    s_out.z_second()
+    s_kv.z_last()
+    s_down.z_last()
+    s_out.z_last()
+    s_up.z_last()
+    s_q.z_last()
     links.recv(m.tok_last, t_sem + 3)
     for part in range(MB):
         rows = slice(TOK * part, TOK * (part + 1))
@@ -1605,19 +1668,15 @@
     links.recv(many_recv, vec_sem + 3)
     m.b_vec[...] = jnp.sum(vec_recv[...], axis=0)
     links.put(m.b_vec, o_vec)
-    s_down.z_last()
     s_down.finish(m.b_down)
     links.put(m.b_down, o_down)
-    s_kv.z_last()
-    s_q.z_last()
-    for scatter, out, to in ((s_up, m.b_up, o_up), (s_out, m.b_wout, o_wout)):
-        scatter.z_last()
+    s_out.finish(m.b_wout)
+    links.put(m.b_wout, o_wout)
+    s_up.finish(m.b_up)
+    links.put(m.b_up, o_up)
     s_kv.finish(m.b_qkv)
     s_q.finish(m.b_qkv)
     links.put(m.b_qkv, o_qkv)
-    for scatter, out, to in ((s_up, m.b_up, o_up), (s_out, m.b_wout, o_wout)):
-        scatter.finish(out)
-        links.put(out, to)
     links.finish()
 
 

time: 173 us -> 165 us (0.954)
  Pallas kernels: 172 us -> 163 us
    pallas_call x1, Pallas kernels: 169 us -> 161 us  [fused(): pl.pallas_call(layer_kernel, name='layer', out_shape=big + [jax.ShapeDtyp...]
where the time goes in v4:
time: 165 us; the launch traced here: 164 us
  Pallas kernels  163 us (99%)
    pallas_call x1, Pallas kernels, fused(): pl.pallas_call(layer_kernel, name='layer', out_shape=big + [jax.ShapeDtyp...  161 us

profile of v4, /device:TPU:1, one launch (start us, length us, event | category | flops | bytes accessed | tf_op | source)
XLA Modules:
  0.0 164.2 jit_solution(14079295741446738913)
XLA Ops:
  0.7 160.6 %layer.1 = (f32[2,64,768]{2,1,0:T(8,128)}, f32[2,64,768]{2,1,0:T(8,128)}, f32[24,2304]{1,0:T(8,128)}, f32[24,768]{1,0:T(8,128)}, f32[24,3072]{1,0:T(8,128)}, /*index=5*/f32[96,768]{1,0:T(8,128)}, f32[8,128]{1,0:T(8,128)}) custom-call(bf16[2,64,768]{2,1,0:T(8,128)(2,1)} %tokens.1, s32[2,16]{1,0:T(2,128)} %starts.1, bf16[24,2304]{1,0:T(8,128)(2,1)} %w_qkv.1, ...), custom_call_target="tpu_custom_call" | custom-call | tf_op jit(solution)/shard_map/layer/pallas_call | solution.py:1713
  161.2 2.8 %place.1 = (f32[2,64,768]{2,1,0:T(8,128)}, f32[2,64,768]{2,1,0:T(8,128)}, f32[24,2304]{1,0:T(8,128)}, f32[24,768]{1,0:T(8,128)}, f32[24,3072]{1,0:T(8,128)}, /*i...) custom-call(f32[2,64,768]{2,1,0:T(8,128)} %get-tuple-element.37.refs, ...), custom_call_target="tpu_custom_call" | custom-call | tf_op jit(solution)/shard_map/place/pallas_call | solution.py:1724

commit v5 on v4

--- a/solution.py
+++ b/solution.py
@@ -971,9 +971,10 @@
     gf_chip=((2, 2, TOK, DM), BF16),
     ga_chip=((2, 2, TOK, DM), BF16),
     partial=((2, 2, TOK, DM), F32),
-    back0=((2, TOK, DM), F32),
-    back1=((2, TOK, DM), F32),
-    back2=((2, TOK, DM), F32),
+    partial_low=((2, TOK, DM), BF16),
+    back0=((2, TOK, DM), BF16),
+    back1=((2, TOK, DM), BF16),
+    back2=((2, TOK, DM), BF16),
     tok_part=((2, 2, 2, TOK, DM), F32),
     tok_back=((2, 2, TOK, DM), F32),
     tok_send=((2, TOK, DM), BF16),
@@ -1381,12 +1382,13 @@
 
     def combine(values, back):
         sem = links.alloc(2)
-        partial = m.partial
+        partial, other = m.partial, m.partial_low
         partial[...] = values.reshape(MB, 2, TOK, DM)
-        links.send(partial.at[:, 1 - c], back, sem, sem + 1, here.sib)
+        other[...] = partial[:, 1 - c].astype(BF16)
+        links.send(other, back, sem, sem + 1, here.sib)
         links.recv(back, sem + 1)
-        total = partial[:, c].reshape(2 * TOK, DM) + back[...].reshape(2 * TOK, DM)
-        links.sent(partial.at[:, 1 - c], sem)
+        total = partial[:, c].reshape(2 * TOK, DM) + back[...].reshape(2 * TOK, DM).astype(F32)
+        links.sent(other, sem)
         return total
 
     def norm_rows(values, gain, shift):
@@ -1605,6 +1607,7 @@
         s_up.plane(t)
     planes(s_out)
     s_down.plane(z)
+    s_up.z_second()
     grad_q.wait()
     for part in range(MB):
         gp_q[256 * part : 256 * (part + 1), :] = d_in[3 * part : 3 * part + 3, 0:HD, :].reshape(GROUP, 256).T
@@ -1621,7 +1624,6 @@
         m.tok_part[part] = terms.reshape(2, 2, TOK, DM)
     links.send(m.tok_part.at[:, :, 1 - c], m.tok_back, t_sem, t_sem + 1, here.sib)
     links.drain(m.tok_back, t_sem)
-    s_up.z_second()
     sum_q = row_sum(gp_q[...].astype(F32))
     sum_v = row_sum(gp_kv[:, GROUP:].astype(F32))
     for k in range(4):
@@ -1636,6 +1638,7 @@
 
     planes(s_q)
     s_kv.z_second()
+    s_q.z_second()
     vec_send, vec_recv = m.vec_send, m.vec_recv
     spread = jnp.where(owner_24(32), vec_grad[...][None], 0.0).reshape(256, DM)
     vec_send[...] = exact_nt(spread, select_24()).reshape(32, 8, 128)
@@ -1651,7 +1654,6 @@
     lax.fori_loop(1, 32, grad_start, 0)
     vec_recv[line] = vec_send[line]
 
-    s_q.z_second()
     s_kv.z_last()
     s_down.z_last()
     s_out.z_last()

time: 165 us -> 161 us (0.976)
  Pallas kernels: 163 us -> 159 us
    pallas_call x1, Pallas kernels: 161 us -> 157 us  [fused(): pl.pallas_call(layer_kernel, name='layer', out_shape=big + [jax.ShapeDtyp...]
where the time goes in v5:
time: 161 us; the launch traced here: 160 us
  Pallas kernels  159 us (99%)
    pallas_call x1, Pallas kernels, fused(): pl.pallas_call(layer_kernel, name='layer', out_shape=big + [jax.ShapeDtyp...  157 us

profile of v5, /device:TPU:1, one launch (start us, length us, event | category | flops | bytes accessed | tf_op | source)
XLA Modules:
  0.0 160.2 jit_solution(6215300508238185922)
XLA Ops:
  0.7 156.5 %layer.1 = (f32[2,64,768]{2,1,0:T(8,128)}, f32[2,64,768]{2,1,0:T(8,128)}, f32[24,2304]{1,0:T(8,128)}, f32[24,768]{1,0:T(8,128)}, f32[24,3072]{1,0:T(8,128)}, /*index=5*/f32[96,768]{1,0:T(8,128)}, f32[8,128]{1,0:T(8,128)}) custom-call(bf16[2,64,768]{2,1,0:T(8,128)(2,1)} %tokens.1, s32[2,16]{1,0:T(2,128)} %starts.1, bf16[24,2304]{1,0:T(8,128)(2,1)} %w_qkv.1, ...), custom_call_target="tpu_custom_call" | custom-call | tf_op jit(solution)/shard_map/layer/pallas_call | solution.py:1715
  157.2 2.8 %place.1 = (f32[2,64,768]{2,1,0:T(8,128)}, f32[2,64,768]{2,1,0:T(8,128)}, f32[24,2304]{1,0:T(8,128)}, f32[24,768]{1,0:T(8,128)}, f32[24,3072]{1,0:T(8,128)}, /*i...) custom-call(f32[2,64,768]{2,1,0:T(8,128)} %get-tuple-element.37.refs, ...), custom_call_target="tpu_custom_call" | custom-call | tf_op jit(solution)/shard_map/place/pallas_call | solution.py:1726

commit v6 on v5

--- a/solution.py
+++ b/solution.py
@@ -1285,7 +1285,6 @@
 
     g_down.first_wait()
     g_down.own_plane()
-    g_down.own_z()
     for gather in ahead:
         gather.land(here.near)
         gather.spread(here.near)
@@ -1295,6 +1294,7 @@
         gather.land(here.cross)
         gather.spread(here.cross)
     links.recv(qkv_t.at[:, pl.ds(0, SEQ - 256)], q_sem + 1, here.active)
+    g_down.own_z()
     for gather in ahead:
         gather.relay(here.near)
     g_down.relay(z)
@@ -1316,7 +1316,8 @@
 
     when(here.active, turn_keys)
 
-    def attend(i):
+    def attend(step):
+        i = 4 * lax.rem(step, 2) + lax.div(step, 2)
         lanes = pl.ds(pl.multiple_of(i * CHUNK, CHUNK), CHUNK)
         query = qkv_t[0:HD, lanes]
         doc = m.query_doc[:, lanes]

time: 161 us -> 160 us (level)
  no operation moved by 1% of the time
where the time goes in v6:
time: 160 us
  Pallas kernels  159 us (99%)
    pallas_call x1, Pallas kernels, fused(): pl.pallas_call(layer_kernel, name='layer', out_shape=big + [jax.ShapeDtyp...  156 us

profile of v6, /device:TPU:1, one launch (start us, length us, event | category | flops | bytes accessed | tf_op | source)
XLA Modules:
  0.0 159.8 jit_solution(10271610931314324315)
XLA Ops:
  0.7 156.2 %layer.1 = (f32[2,64,768]{2,1,0:T(8,128)}, f32[2,64,768]{2,1,0:T(8,128)}, f32[24,2304]{1,0:T(8,128)}, f32[24,768]{1,0:T(8,128)}, f32[24,3072]{1,0:T(8,128)}, /*index=5*/f32[96,768]{1,0:T(8,128)}, f32[8,128]{1,0:T(8,128)}) custom-call(bf16[2,64,768]{2,1,0:T(8,128)(2,1)} %tokens.1, s32[2,16]{1,0:T(2,128)} %starts.1, bf16[24,2304]{1,0:T(8,128)(2,1)} %w_qkv.1, ...), custom_call_target="tpu_custom_call" | custom-call | tf_op jit(solution)/shard_map/layer/pallas_call | solution.py:1716
  156.9 2.8 %place.1 = (f32[2,64,768]{2,1,0:T(8,128)}, f32[2,64,768]{2,1,0:T(8,128)}, f32[24,2304]{1,0:T(8,128)}, f32[24,768]{1,0:T(8,128)}, f32[24,3072]{1,0:T(8,128)}, /*i...) custom-call(f32[2,64,768]{2,1,0:T(8,128)} %get-tuple-element.37.refs, ...), custom_call_target="tpu_custom_call" | custom-call | tf_op jit(solution)/shard_map/place/pallas_call | solution.py:1727

commit v7 on v6

--- a/solution.py
+++ b/solution.py
@@ -1531,8 +1531,8 @@
                 scatter.z_first(i)
 
     s_down.column_second()
+    links.recv(g_t.at[:, pl.ds(0, SEQ - 128)], g_sem + 1, here.active)
     planes(s_down, targets[:3])
-    links.recv(g_t.at[:, pl.ds(0, SEQ - 128)], g_sem + 1, here.active)
 
     d_send, d_in = m.d_send, m.d_in
 

time: 160 us -> 160 us (level)
  no operation moved by 1% of the time
where the time goes in v7:
time: 160 us
  Pallas kernels  159 us (99%)
    pallas_call x1, Pallas kernels, fused(): pl.pallas_call(layer_kernel, name='layer', out_shape=big + [jax.ShapeDtyp...  156 us

profile of v7, /device:TPU:1, one launch (start us, length us, event | category | flops | bytes accessed | tf_op | source)
XLA Modules:
  0.0 159.9 jit_solution(8662776735846021431)
XLA Ops:
  0.7 156.3 %layer.1 = (f32[2,64,768]{2,1,0:T(8,128)}, f32[2,64,768]{2,1,0:T(8,128)}, f32[24,2304]{1,0:T(8,128)}, f32[24,768]{1,0:T(8,128)}, f32[24,3072]{1,0:T(8,128)}, /*index=5*/f32[96,768]{1,0:T(8,128)}, f32[8,128]{1,0:T(8,128)}) custom-call(bf16[2,64,768]{2,1,0:T(8,128)(2,1)} %tokens.1, s32[2,16]{1,0:T(2,128)} %starts.1, bf16[24,2304]{1,0:T(8,128)(2,1)} %w_qkv.1, ...), custom_call_target="tpu_custom_call" | custom-call | tf_op jit(solution)/shard_map/layer/pallas_call | solution.py:1716
  156.9 2.8 %place.1 = (f32[2,64,768]{2,1,0:T(8,128)}, f32[2,64,768]{2,1,0:T(8,128)}, f32[24,2304]{1,0:T(8,128)}, f32[24,768]{1,0:T(8,128)}, f32[24,3072]{1,0:T(8,128)}, /*i...) custom-call(f32[2,64,768]{2,1,0:T(8,128)} %get-tuple-element.37.refs, ...), custom_call_target="tpu_custom_call" | custom-call | tf_op jit(solution)/shard_map/place/pallas_call | solution.py:1727
